TPU v7x, 32 devices: a whole 2x2x4 slice. The times are simulated.
32 devices in a mesh: groups: 2 (over y), edge: 4 (over z), trip: 2 (over x), sub: 2 (over core).
Axes of the slice: x: 2, y: 2, z: 4, core: 2. Of those that a mesh axis runs over, the one named last changes fastest.
Arguments:
- edge_feat: float32 [128, 128, 512], P(('groups', 'edge'), ('trip', 'sub')), parts along dimension 0, may hold values from -6 to 6
- edge_counts: int32 [128], P(('groups', 'edge')), parts along dimension 0, may hold values from 64 to 128
- reverse: int32 [128], P('groups'), parts along dimension 0, may hold values from 0 to 63, as said below
- patterns: int32 [8, 4, 64, 2], P(('groups', 'edge'), ('trip', 'sub')), parts along dimension 0, may hold values from 0 to 15
- trip_count: int32 [8, 4], P(('groups', 'edge'), ('trip', 'sub')), parts along dimension 0, may hold values from 16 to 64, as said below
- coef: float32 [8, 4, 64, 128, 128], P(('groups', 'edge'), ('trip', 'sub')), parts along dimension 0, may hold values from -0.1875 to 0.1875
- down_weight: float32 [3, 512, 256], replicated, may hold values from -0.25 to 0.25
- up_weight: float32 [3, 256, 512], replicated, may hold values from -0.375 to 0.375
- dense_weight: float32 [3, 512, 512], replicated, may hold values from -0.25 to 0.25
Outputs:
- edge_out: float32 [128, 128, 512], P(('groups', 'edge'), ('trip', 'sub')), parts along dimension 0
There are 2 independent parts, one for each index of `groups`. A program takes and returns all parts, laid end to end along the dimension named above; an argument that names none is the same for every part. Nothing has to cross between parts.
Inputs may be any that keep to these rules, and one draw needn't show every extreme that they name: reverse is an involution without fixed points; reverse[c] lies on another index of edge than c; from one index of edge at most 8 clusters have their reverse on one other index, and that many in every draw. `trip_count`: some device has all 64 slots live in every draw.
All inputs are finite; a program needn't handle non-finite values.
Results may differ from a plain program's by a relative error of at most 0.0003.
Values sent between devices are 32-bit elements; how exact they have to be, the bound alone decides.
No kernel may reach another device: no remote copies, remote signals or barrier semaphores. Data moves between devices by JAX's collectives and lax.ppermute only.
A program may use at most 128 MiB of HBM per device.

v0:
```python
import functools

import jax
import jax.numpy as jnp
from jax import lax
from jax.experimental import pallas as pl
from jax.experimental.pallas import tpu as pltpu
from jax.sharding import PartitionSpec as P

INV_THREE = 1.0 / 3.0**0.5
INV_TWO = 1.0 / 2.0**0.5
F32 = jnp.float32
BF16 = jnp.bfloat16
SMEM = pl.BlockSpec(memory_space=pltpu.SMEM)
VMEM = pl.BlockSpec(memory_space=pltpu.VMEM)


def split(v):
    high = v.astype(BF16)
    return high, (v - high.astype(F32)).astype(BF16)


def dot(a, b):
    return jnp.dot(a, b, preferred_element_type=F32)


def dot3(a, high, low):
    a_high, a_low = split(a)
    return dot(a_high, high) + (dot(a_low, high) + dot(a_high, low))


def params(mib):
    return pltpu.CompilerParams(vmem_limit_bytes=mib << 20)


def call(kernel, outs, ins, mib, scratch=(), flops=0, moved=0):
    return pl.pallas_call(
        kernel,
        out_shape=outs,
        in_specs=ins,
        out_specs=jax.tree.map(lambda _: VMEM, outs),
        scratch_shapes=list(scratch),
        compiler_params=params(mib),
        cost_estimate=pl.CostEstimate(flops=flops, bytes_accessed=moved, transcendentals=0),
    )


def cells_kernel(sizes, ids, pats, live, mine, theirs, rem_hi, rem_lo, loc_hi, loc_lo, acc):
    trips, chunks, rc, clusters = sizes
    x = ids[0]
    slots = mine.shape[0]
    zero = jnp.zeros(acc.shape[1:], F32)

    def clear(q, c):
        acc[q] = zero
        return c

    lax.fori_loop(0, clusters, clear, 0)
    for half, ref in enumerate((mine, theirs)):

        def add(p, c, half=half, ref=ref):
            t, q = pats[half, 2 * p], pats[half, 2 * p + 1]
            for d in range(trips):
                td = lax.rem(x + d, trips)
                for r in range(chunks):
                    g = d * chunks + r
                    acc[q, g, t] += ref[p, td, r * rc : (r + 1) * rc, :]
            return c

        lax.fori_loop(0, jnp.minimum(live[half], slots), add, 0)
    block = clusters * rc
    width = acc.shape[-1]

    def finish(q, c):
        lanes = pl.ds(pl.multiple_of(q * width, width), width)
        for d in range(trips):
            for r in range(chunks):
                high, low = split(acc[q, d * chunks + r].reshape(block, width))
                if d:
                    rem_hi[r, (d - 1) * block : d * block, lanes] = high
                    rem_lo[r, (d - 1) * block : d * block, lanes] = low
                else:
                    loc_hi[r * block : (r + 1) * block, lanes] = high
                    loc_lo[r * block : (r + 1) * block, lanes] = low
        return c

    lax.fori_loop(0, clusters, finish, 0)


def gather_kernel(sizes, places, ids, c_hi, c_lo, *refs):
    trips, subs, chunks, rc, clusters, rows, width = sizes
    pieces, (out, x_hi, x_lo) = refs[: len(places)], refs[len(places) :]
    x, s = ids[0], ids[1]
    share = chunks * rc
    for (d, other, r), ref in zip(places, pieces):
        core = 1 - s if other else s
        at = (lax.rem(x + trips - d, trips) * subs + core) * share + r * rc
        for q in range(clusters):
            high, low = split(ref[q])
            spot = pl.ds(pl.multiple_of(q * rows + at, rc), rc)
            x_hi[spot, :] = high
            x_lo[spot, :] = low
    out[...] = dot(c_hi[...], x_hi[...]) + (dot(c_lo[...], x_hi[...]) + dot(c_hi[...], x_lo[...]))


def terms_kernel(c_hi, c_lo, x_hi, x_lo, out):
    out[...] = dot(c_hi[...], x_hi[...]) + (dot(c_lo[...], x_hi[...]) + dot(c_hi[...], x_lo[...]))


def pack_kernel(sizes, arrivals, send_src, *refs):
    clusters, rc, cap = sizes
    local, refs = refs[0], refs[1:]
    got, agg, packs = refs[:arrivals], refs[arrivals], refs[arrivals + 1 :]
    total = local[...]
    for ref in got:
        total = total + ref[...]
    agg[...] = total
    for k, pack in enumerate(packs):
        for j in range(cap):
            pack[j] = agg[send_src[(k + 1) * cap + j]]


def rows_kernel(sizes, last, recv_pos, counts, ids, *refs):
    clusters, rc, cap, steps, first_row = sizes
    feat, agg, refs = refs[0], refs[1], refs[2:]
    got, refs = refs[:steps], refs[steps:]
    up_hi, up_lo, dense_hi, dense_lo, refs = *refs[:4], refs[4:]
    if last:
        (out, held, both), down = refs, None
    else:
        down, (out, low_out, held, both) = refs[:2], refs[2:]
    for k, ref in enumerate(got):
        held[k * cap : (k + 1) * cap] = ref[...]
    for c in range(clusters):
        both[c] = agg[c] + held[recv_pos[c] - cap]
    block = clusters * rc
    lifted = dot3(both[...].reshape(block, -1), up_hi[...], up_lo[...])
    merged = (feat[...].reshape(block, -1) + lifted) * INV_THREE
    v = dot3(merged, dense_hi[...], dense_lo[...])
    result = (merged + v / (1.0 + jnp.exp(-v))) * INV_TWO
    out[...] = result.reshape(out.shape)
    if not last:
        lower(result, down, counts, ids, first_row, low_out)


def lower(feat, down, counts, ids, first_row, out):
    clusters, rc, width = out.shape
    low = dot3(feat, down[0][...], down[1][...])
    ids_at = ids[2] + first_row + lax.broadcasted_iota(jnp.int32, (rc, width), 0)
    for c in range(clusters):
        out[c] = jnp.where(ids_at < counts[c], low[c * rc : (c + 1) * rc, :], 0.0)


def down_kernel(first_row, counts, ids, feat, down_hi, down_lo, out):
    lower(feat[...].reshape(out.shape[0] * out.shape[1], -1), (down_hi, down_lo), counts, ids, first_row, out)


def local(
    edge_feat,
    edge_counts,
    reverse,
    patterns,
    trip_count,
    coef,
    down_weight,
    up_weight,
    dense_weight,
):
    clusters, share, feat_width = edge_feat.shape
    layers, _, width = down_weight.shape
    edges, trips, subs = (lax.axis_size(a) for a in ("edge", "trip", "sub"))
    e, x, s = (lax.axis_index(a) for a in ("edge", "trip", "sub"))
    rows = trips * subs * share
    cap = 2 * ((clusters // 2 + edges // 2 - 1) // (edges // 2))
    rc = 16
    chunks = share // rc
    block = clusters * rc
    depth = clusters * rows
    slots = patterns.shape[2]
    ids = jnp.stack([x, s, (x * subs + s) * share]).astype(jnp.int32)
    swap = [(0, 1), (1, 0)]

    here = jnp.arange(clusters, dtype=jnp.int32)
    mine = lax.dynamic_slice_in_dim(reverse, e * clusters, clusters)
    to = mine // clusters
    earlier = (to[:, None] == to[None, :]) & (here[None, :] < here[:, None])
    send_pos = (to ^ e) * cap + jnp.sum(earlier.astype(jnp.int32), axis=1)
    places = jnp.arange(edges * cap, dtype=jnp.int32)
    send_src = jnp.sum(jnp.where(places[:, None] == send_pos[None, :], here[None, :], 0), axis=1)
    everyone = jnp.arange(reverse.shape[0], dtype=jnp.int32)
    before = (
        (everyone[None, :] // clusters == to[:, None])
        & (everyone[None, :] < mine[:, None])
        & ((reverse // clusters)[None, :] == e)
    )
    recv_pos = (to ^ e) * cap + jnp.sum(before.astype(jnp.int32), axis=1)

    def parts(w):
        high = lax.reduce_precision(w, 8, 7)
        return high.astype(BF16), (w - high).astype(BF16)

    down_hi, down_lo = parts(down_weight)
    up_hi, up_lo = parts(up_weight)
    dense_hi, dense_lo = parts(dense_weight)

    feats = [edge_feat[:, r * rc : (r + 1) * rc, :] for r in range(chunks)]
    small = jax.ShapeDtypeStruct((clusters, rc, width), F32)
    big = jax.ShapeDtypeStruct((clusters, rc, feat_width), F32)
    lows = [
        call(
            functools.partial(down_kernel, r * rc),
            small,
            [SMEM, SMEM, VMEM, VMEM, VMEM],
            16,
            flops=6 * block * feat_width * width,
        )(edge_counts, ids, feats[r], down_hi[0], down_lo[0])
        for r in range(chunks)
    ]

    halves = coef[0, 0].reshape(slots, trips, subs, share, rows)
    keep = lax.dynamic_index_in_dim(halves, s, 2, keepdims=False)
    give = lax.dynamic_index_in_dim(halves, 1 - s, 2, keepdims=False)
    note = jnp.concatenate([patterns[0, 0].reshape(-1), trip_count[0, 0][None]])
    note2 = lax.ppermute(note, "sub", swap)
    give = lax.ppermute(give, "sub", swap)
    pats = jnp.stack([note[:-1], note2[:-1]])
    live = jnp.stack([note[-1], note2[-1]])
    remote = (trips - 1) * block
    rem_hi, rem_lo, loc_hi, loc_lo = call(
        functools.partial(cells_kernel, (trips, chunks, rc, clusters)),
        [jax.ShapeDtypeStruct((chunks, remote, depth), BF16)] * 2
        + [jax.ShapeDtypeStruct((chunks * block, depth), BF16)] * 2,
        [SMEM, SMEM, SMEM, VMEM, VMEM],
        40,
        scratch=[pltpu.VMEM((clusters, trips * chunks, clusters, rc, rows), F32)],
        moved=12 << 20,
    )(ids, pats, live, keep, give)

    for layer in range(layers):
        pieces, spots = [], []
        for r in range(chunks):
            pieces += [lows[r], lax.ppermute(lows[r], "sub", swap)]
            spots += [(0, 0, r), (0, 1, r)]
            for d in range(1, trips):
                far = lax.ppermute(lows[r], "trip", [(i, (i + d) % trips) for i in range(trips)])
                pieces += [far, lax.ppermute(far, "sub", swap)]
                spots += [(d, 0, r), (d, 1, r)]
        sizes = (trips, subs, chunks, rc, clusters, rows, width)
        flops = 6 * remote * depth * width
        out, x_hi, x_lo = call(
            functools.partial(gather_kernel, sizes, spots),
            [jax.ShapeDtypeStruct((remote, width), F32)] + [jax.ShapeDtypeStruct((depth, width), BF16)] * 2,
            [SMEM, VMEM, VMEM] + [VMEM] * len(pieces),
            32,
            flops=flops,
        )(ids, rem_hi[0], rem_lo[0], *pieces)
        outs = [out]
        for r in range(1, chunks):
            outs.append(
                call(terms_kernel, jax.ShapeDtypeStruct((remote, width), F32), [VMEM] * 4, 32, flops=flops)(
                    rem_hi[r], rem_lo[r], x_hi, x_lo
                )
            )
        own = call(
            terms_kernel,
            jax.ShapeDtypeStruct((chunks * block, width), F32),
            [VMEM] * 4,
            32,
            flops=6 * chunks * block * depth * width,
        )(loc_hi, loc_lo, x_hi, x_lo).reshape(chunks, clusters, rc, width)
        next_feats, next_lows = [], []
        for r in range(chunks):
            sent = outs[r].reshape(trips - 1, clusters, rc, width)
            got = [
                lax.ppermute(sent[d - 1], "trip", [(i, (i + d) % trips) for i in range(trips)])
                for d in range(1, trips)
            ]
            agg, *packs = call(
                functools.partial(pack_kernel, (clusters, rc, cap), trips - 1),
                [small] + [jax.ShapeDtypeStruct((cap, rc, width), F32)] * (edges - 1),
                [SMEM] + [VMEM] * trips,
                16,
                moved=4 << 20,
            )(send_src, own[r], *got)
            back = [
                lax.ppermute(packs[k - 1], "edge", [(i, i ^ k) for i in range(edges)]) for k in range(1, edges)
            ]
            last = layer == layers - 1
            result = call(
                functools.partial(rows_kernel, (clusters, rc, cap, edges - 1, r * rc), last),
                [big] if last else [big, small],
                [SMEM] * 3 + [VMEM] * (2 + edges - 1 + 4 + (0 if last else 2)),
                32,
                scratch=[
                    pltpu.VMEM(((edges - 1) * cap, rc, width), F32),
                    pltpu.VMEM((clusters, rc, width), F32),
                ],
                flops=6 * block * feat_width * (2 * width + feat_width),
            )(
                recv_pos,
                edge_counts,
                ids,
                feats[r],
                agg,
                *back,
                up_hi[layer],
                up_lo[layer],
                dense_hi[layer],
                dense_lo[layer],
                *(() if last else (down_hi[layer + 1], down_lo[layer + 1])),
            )
            next_feats.append(result[0])
            next_lows += result[1:]
        feats, lows = next_feats, next_lows
    return jnp.concatenate(feats, axis=1)


def solution(mesh):
    placed = (
        P(("groups", "edge"), ("trip", "sub"), None),
        P(("groups", "edge")),
        P("groups"),
        P(("groups", "edge"), ("trip", "sub"), None, None),
        P(("groups", "edge"), ("trip", "sub")),
        P(("groups", "edge"), ("trip", "sub"), None, None, None),
        P(),
        P(),
        P(),
    )
    return jax.shard_map(
        local,
        mesh=mesh,
        in_specs=placed,
        out_specs=P(("groups", "edge"), ("trip", "sub"), None),
        check_vma=False,
    )
```

profile of v0, /device:TPU:0, one launch (start us, length us, event | category | flops | bytes accessed | tf_op | source)
XLA Modules:
  0.0 185.3 jit_solution(15452012525525301381)
XLA Ops:
  5.1 2.5 %collective-permute-start.3 = (f32[16,16,256]{2,1,0:T(8,128)}, f32[16,16,256]{2,1,0:T(8,128)}, u32[]{:S(2)}, u32[]{:S(2)}) collective-permute-start(f32[16,16,256]{2,1,0:T(8,128)} %shard_map.92.refs_0_), channel_id=1, source_target_pairs={{0,2},{2,0},{1,3},{3,1},{4,6},{6,4},{5,7},{7,5},{8,10},{10,8},{9,1... | collective-permute-start | bytes 786440 | tf_op jit(solution)/shard_map/ppermute | solution.py:245
  8.8 4.2 %dynamic-slice_bitcast_fusion = (f32[64,2,32,128]{3,2,1,0:T(8,128)}, f32[64,2,32,128]{3,2,1,0:T(8,128)S(1)}) fusion(f32[64,2,2,32,128]{4,3,2,1,0:T(8,128)} %bitcast.89, s32[]{:T(128)S(6)} %select_n.40, s32[]{:T(128)S(6)} %select_n.39), kind=kLoop, calls=%fused_computation.7 | loop fusion | bytes 8388616 | tf_op jit(solution)/shard_map/jit(dynamic_index_in_dim)/squeeze | solution.py:222
  15.7 2.4 %fusion = (bf16[3,512,512]{2,1,0:T(8,128)(2,1)S(1)}, bf16[3,512,512]{2,1,0:T(8,128)(2,1)S(1)}) fusion(f32[3,512,512]{2,1,0:T(8,128)} %param.17), kind=kLoop, calls=%fused_computation.2 | loop fusion | flops 3145728 | bytes 6291456 | tf_op jit(solution)/shard_map/convert_element_type | solution.py:200
  21.4 7.1 %collective-permute-done.6.refs_6_ = f32[16,16,256]{2,1,0:T(8,128)S(1)} collective-permute-done((f32[16,16,256]{2,1,0:T(8,128)}, f32[16,16,256]{2,1,0:T(8,128)S(1)}, u32[]{:S(2)}, u32[]{:S(2)}) %collective-permute-start.6) | collective-permute-done | bytes 262176 | tf_op jit(solution)/shard_map/ppermute | solution.py:245
  28.5 5.8 %shard_map.91 = (bf16[2,256,2048]{2,1,0:T(8,128)(2,1)S(1)}, bf16[2,256,2048]{2,1,0:T(8,128)(2,1)S(1)}, bf16[512,2048]{1,0:T(8,128)(2,1)S(1)}, bf16[512,2048]{1,0:T(8,128)(2,1)S(1)}) custom-call(s32[3]{0:T(128)S(1)} %pad_add_fusion.2.ids, s32[2,128]{1,0:T(2,128)S(1)} %pad_add_fusion.1.pats, s32[2]{0:T(128)S(1)} %pad_add_fusion.3.live, ...), custom_call_target="tpu_custom_call" | custom-call | bytes 12582912 | tf_op jit(solution)/shard_map/pallas_call | solution.py:229
  34.6 2.6 %shard_map.94 = (f32[256,256]{1,0:T(8,128)S(1)}, bf16[2048,256]{1,0:T(8,128)(2,1)S(1)}, bf16[2048,256]{1,0:T(8,128)(2,1)S(1)}) custom-call(s32[3]{0:T(128)S(1)} %pad_add_fusion.2.ids, bf16[256,2048]{1,0:T(8,128)(2,1)S(1)} %get-tuple-element.137.c_hi, bf16[256,2048]{1,0:T(8,128)(2,1)S(1)} %get-tuple-element.102.c_lo, f32[16,16,256]{2,1,0:T(8,128)} %shard_map.92.refs_0_, ...), custom_call_target="tpu_custom_call" | custom-call | flops 805306368 | tf_op jit(solution)/shard_map/pallas_call | solution.py:250
  42.2 10.5 %collective-permute-done.8.refs_1_ = f32[16,16,256]{2,1,0:T(8,128)S(1)} collective-permute-done((f32[16,16,256]{2,1,0:T(8,128)S(1)}, f32[16,16,256]{2,1,0:T(8,128)S(1)}, u32[]{:S(2)}, u32[]{:S(2)}) %collective-permute-start.8) | collective-permute-done | bytes 262176 | tf_op jit(solution)/shard_map/ppermute | solution.py:275
  56.4 2.6 %collective-permute-start.17 = (f32[8,16,256]{2,1,0:T(8,128)S(1)}, f32[8,16,256]{2,1,0:T(8,128)S(1)}, u32[]{:S(2)}, u32[]{:S(2)}) collective-permute-start(f32[8,16,256]{2,1,0:T(8,128)S(1)} %get-tuple-element.65), channel_id=1, source_target_pairs={{0,8},{4,12},{8,0},{12,4},{1,9},{5,13},{9,1},{13,5},{2,10},{6,14},... | collective-permute-start | bytes 393224 | tf_op jit(solution)/shard_map/ppermute | solution.py:286
  61.7 2.6 %collective-permute-start.11 = (f32[8,16,256]{2,1,0:T(8,128)S(1)}, f32[8,16,256]{2,1,0:T(8,128)S(1)}, u32[]{:S(2)}, u32[]{:S(2)}) collective-permute-start(f32[8,16,256]{2,1,0:T(8,128)S(1)} %get-tuple-element.60), channel_id=1, source_target_pairs={{0,12},{4,8},{8,4},{12,0},{1,13},{5,9},{9,5},{13,1},{2,14},{6,10},... | collective-permute-start | bytes 393224 | tf_op jit(solution)/shard_map/ppermute | solution.py:286
  64.4 15.9 %collective-permute-done.10.refs_3_ = f32[8,16,256]{2,1,0:T(8,128)S(1)} collective-permute-done((f32[8,16,256]{2,1,0:T(8,128)S(1)}, f32[8,16,256]{2,1,0:T(8,128)S(1)}, u32[]{:S(2)}, u32[]{:S(2)}) %collective-permute-start.10) | collective-permute-done | bytes 131104 | tf_op jit(solution)/shard_map/ppermute | solution.py:286
  80.3 2.1 %shard_map.97 = (f32[16,16,512]{2,1,0:T(8,128)S(1)}, f32[16,16,256]{2,1,0:T(8,128)S(1)}) custom-call(s32[16]{0:T(128)S(1)} %get-tuple-element.136.recv_pos, s32[16]{0:T(128)S(1)} %copy-done.11, s32[3]{0:T(128)S(1)} %pad_add_fusion.2.ids, f32[16,16,512]{2,1,0:T(8,128)S(1)} %copy-done.7, f32[16,16,256]{2,1,0:T(8,128)S(1)} %get-tuple-element.57.refs_1_, ...), custom_call_target="tpu_custom_call" | custom-call | flops 805306368 | tf_op jit(solution)/shard_map/pallas_call | solution.py:289
  87.2 4.1 %collective-permute-done.13.refs_2_ = f32[16,16,256]{2,1,0:T(8,128)S(1)} collective-permute-done((f32[16,16,256]{2,1,0:T(8,128)S(1)}, f32[16,16,256]{2,1,0:T(8,128)S(1)}, u32[]{:S(2)}, u32[]{:S(2)}) %collective-permute-start.13) | collective-permute-done | bytes 262176 | tf_op jit(solution)/shard_map/ppermute | solution.py:245
  91.3 2.8 %collective-permute-done.20.refs_6_ = f32[16,16,256]{2,1,0:T(8,128)S(1)} collective-permute-done((f32[16,16,256]{2,1,0:T(8,128)S(1)}, f32[16,16,256]{2,1,0:T(8,128)S(1)}, u32[]{:S(2)}, u32[]{:S(2)}) %collective-permute-start.20) | collective-permute-done | bytes 262176 | tf_op jit(solution)/shard_map/ppermute | solution.py:245
  102.6 4.1 %collective-permute-done.22.refs_1_ = f32[16,16,256]{2,1,0:T(8,128)S(1)} collective-permute-done((f32[16,16,256]{2,1,0:T(8,128)S(1)}, f32[16,16,256]{2,1,0:T(8,128)S(1)}, u32[]{:S(2)}, u32[]{:S(2)}) %collective-permute-start.22) | collective-permute-done | bytes 262176 | tf_op jit(solution)/shard_map/ppermute | solution.py:275
  107.3 3.4 %collective-permute-start.23 = (f32[8,16,256]{2,1,0:T(8,128)S(1)}, f32[8,16,256]{2,1,0:T(8,128)S(1)}, u32[]{:S(2)}, u32[]{:S(2)}) collective-permute-start(f32[8,16,256]{2,1,0:T(8,128)S(1)} %get-tuple-element.72), channel_id=1, source_target_pairs={{0,4},{4,0},{8,12},{12,8},{1,5},{5,1},{9,13},{13,9},{2,6},{6,2},{1... | collective-permute-start | bytes 393224 | tf_op jit(solution)/shard_map/ppermute | solution.py:286
  118.2 5.5 %collective-permute-done.24.refs_3_ = f32[8,16,256]{2,1,0:T(8,128)S(1)} collective-permute-done((f32[8,16,256]{2,1,0:T(8,128)S(1)}, f32[8,16,256]{2,1,0:T(8,128)S(1)}, u32[]{:S(2)}, u32[]{:S(2)}) %collective-permute-start.24) | collective-permute-done | bytes 131104 | tf_op jit(solution)/shard_map/ppermute | solution.py:286
  123.8 2.3 %shard_map.104 = (f32[16,16,512]{2,1,0:T(8,128)S(1)}, f32[16,16,256]{2,1,0:T(8,128)S(1)}) custom-call(s32[16]{0:T(128)S(1)} %get-tuple-element.136.recv_pos, s32[16]{0:T(128)S(1)} %copy-done.11, s32[3]{0:T(128)S(1)} %pad_add_fusion.2.ids, f32[16,16,512]{2,1,0:T(8,128)S(1)} %get-tuple-element.61.refs_0_, f32[16,16,256]{2,1,0:T(8,128)S(1)} %get-tuple-element.71.refs_1_, ...), custom_call_target="tpu_custom_call" | custom-call | flops 805306368 | tf_op jit(solution)/shard_map/pallas_call | solution.py:289
  126.7 6.9 %collective-permute-done.31.refs_3_ = f32[8,16,256]{2,1,0:T(8,128)S(1)} collective-permute-done((f32[8,16,256]{2,1,0:T(8,128)S(1)}, f32[8,16,256]{2,1,0:T(8,128)S(1)}, u32[]{:S(2)}, u32[]{:S(2)}) %collective-permute-start.31) | collective-permute-done | bytes 131104 | tf_op jit(solution)/shard_map/ppermute | solution.py:286
  133.6 2.1 %shard_map.107 = (f32[16,16,512]{2,1,0:T(8,128)S(1)}, f32[16,16,256]{2,1,0:T(8,128)S(1)}) custom-call(s32[16]{0:T(128)S(1)} %get-tuple-element.136.recv_pos, s32[16]{0:T(128)S(1)} %copy-done.11, s32[3]{0:T(128)S(1)} %pad_add_fusion.2.ids, f32[16,16,512]{2,1,0:T(8,128)S(1)} %get-tuple-element.77.refs_0_, f32[16,16,256]{2,1,0:T(8,128)S(1)} %get-tuple-element.78.refs_1_, ...), custom_call_target="tpu_custom_call" | custom-call | flops 805306368 | tf_op jit(solution)/shard_map/pallas_call | solution.py:289
  136.7 5.4 %collective-permute-done.34.refs_6_ = f32[16,16,256]{2,1,0:T(8,128)S(1)} collective-permute-done((f32[16,16,256]{2,1,0:T(8,128)S(1)}, f32[16,16,256]{2,1,0:T(8,128)S(1)}, u32[]{:S(2)}, u32[]{:S(2)}) %collective-permute-start.34) | collective-permute-done | bytes 262176 | tf_op jit(solution)/shard_map/ppermute | solution.py:245
  150.6 5.2 %collective-permute-done.40.refs_1_ = f32[16,16,256]{2,1,0:T(8,128)S(1)} collective-permute-done((f32[16,16,256]{2,1,0:T(8,128)S(1)}, f32[16,16,256]{2,1,0:T(8,128)S(1)}, u32[]{:S(2)}, u32[]{:S(2)}) %collective-permute-start.40) | collective-permute-done | bytes 262176 | tf_op jit(solution)/shard_map/ppermute | solution.py:275
  156.3 3.7 %collective-permute-start.41 = (f32[8,16,256]{2,1,0:T(8,128)S(1)}, f32[8,16,256]{2,1,0:T(8,128)S(1)}, u32[]{:S(2)}, u32[]{:S(2)}) collective-permute-start(f32[8,16,256]{2,1,0:T(8,128)S(1)} %get-tuple-element.92), channel_id=1, source_target_pairs={{0,4},{4,0},{8,12},{12,8},{1,5},{5,1},{9,13},{13,9},{2,6},{6,2},{1... | collective-permute-start | bytes 393224 | tf_op jit(solution)/shard_map/ppermute | solution.py:286
  167.5 5.5 %collective-permute-done.42.refs_3_ = f32[8,16,256]{2,1,0:T(8,128)S(1)} collective-permute-done((f32[8,16,256]{2,1,0:T(8,128)S(1)}, f32[8,16,256]{2,1,0:T(8,128)S(1)}, u32[]{:S(2)}, u32[]{:S(2)}) %collective-permute-start.42) | collective-permute-done | bytes 131104 | tf_op jit(solution)/shard_map/ppermute | solution.py:286
  174.6 8.0 %collective-permute-done.38.refs_3_ = f32[8,16,256]{2,1,0:T(8,128)S(1)} collective-permute-done((f32[8,16,256]{2,1,0:T(8,128)S(1)}, f32[8,16,256]{2,1,0:T(8,128)S(1)}, u32[]{:S(2)}, u32[]{:S(2)}) %collective-permute-start.38) | collective-permute-done | bytes 131104 | tf_op jit(solution)/shard_map/ppermute | solution.py:286
  (149 shorter events, 66.9 us)
Async XLA Ops:
  4.7 29.9 %collective-permute-start.2 = (f32[16,16,256]{2,1,0:T(8,128)}, f32[16,16,256]{2,1,0:T(8,128)}, u32[]{:S(2)}, u32[]{:S(2)}) collective-permute-start(f32[16,16,256]{2,1,0:T(8,128)} %shard_map.92.refs_0_), channel_id=1, source_target_pairs={{0,1},{1,0},{2,3},{3,2},{4,5},{5,4},{6,7},{7,6},{8,9},{9,8},{10,11... | collective-permute-start | bytes 786440 | tf_op jit(solution)/shard_map/ppermute | solution.py:242
  5.1 16.1 %collective-permute-start.3 = (f32[16,16,256]{2,1,0:T(8,128)}, f32[16,16,256]{2,1,0:T(8,128)}, u32[]{:S(2)}, u32[]{:S(2)}) collective-permute-start(f32[16,16,256]{2,1,0:T(8,128)} %shard_map.92.refs_0_), channel_id=1, source_target_pairs={{0,2},{2,0},{1,3},{3,1},{4,6},{6,4},{5,7},{7,5},{8,10},{10,8},{9,1... | collective-permute-start | bytes 786440 | tf_op jit(solution)/shard_map/ppermute | solution.py:245
  13.1 15.4 %collective-permute-start.1 = (f32[64,2,32,128]{3,2,1,0:T(8,128)}, f32[64,2,32,128]{3,2,1,0:T(8,128)}, u32[]{:S(2)}, u32[]{:S(2)}) collective-permute-start(f32[64,2,32,128]{3,2,1,0:T(8,128)} %get-tuple-element.97), channel_id=1, source_target_pairs={{0,1},{1,0},{2,3},{3,2},{4,5},{5,4},{6,7},{7,6},{8,9},{9,8},{10,11... | collective-permute-start | bytes 6291464 | tf_op jit(solution)/shard_map/ppermute | solution.py:225
  15.0 19.6 %collective-permute-start.5 = (f32[16,16,256]{2,1,0:T(8,128)}, f32[16,16,256]{2,1,0:T(8,128)}, u32[]{:S(2)}, u32[]{:S(2)}) collective-permute-start(f32[16,16,256]{2,1,0:T(8,128)} %shard_map.93.refs_4_), channel_id=1, source_target_pairs={{0,1},{1,0},{2,3},{3,2},{4,5},{5,4},{6,7},{7,6},{8,9},{9,8},{10,11... | collective-permute-start | bytes 786440 | tf_op jit(solution)/shard_map/ppermute | solution.py:242
  21.3 13.3 %collective-permute-start.4 = (f32[16,16,256]{2,1,0:T(8,128)}, f32[16,16,256]{2,1,0:T(8,128)S(1)}, u32[]{:S(2)}, u32[]{:S(2)}) collective-permute-start(f32[16,16,256]{2,1,0:T(8,128)} %collective-permute-done.3.refs_2_), channel_id=1, source_target_pairs={{0,1},{1,0},{2,3},{3,2},{4,5},{5,4},{6,7},{7,6},{8,9},{9,8},{10,11... | collective-permute-start | bytes 786440 | tf_op jit(solution)/shard_map/ppermute | solution.py:246
  38.2 16.5 %collective-permute-start.15 = (f32[16,16,256]{2,1,0:T(8,128)S(1)}, f32[16,16,256]{2,1,0:T(8,128)S(1)}, u32[]{:S(2)}, u32[]{:S(2)}) collective-permute-start(f32[16,16,256]{2,1,0:T(8,128)S(1)} %bitcast.83), channel_id=1, source_target_pairs={{0,2},{2,0},{1,3},{3,1},{4,6},{6,4},{5,7},{7,5},{8,10},{10,8},{9,1... | collective-permute-start | bytes 786440 | tf_op jit(solution)/shard_map/ppermute | solution.py:275
  39.1 13.6 %collective-permute-start.8 = (f32[16,16,256]{2,1,0:T(8,128)S(1)}, f32[16,16,256]{2,1,0:T(8,128)S(1)}, u32[]{:S(2)}, u32[]{:S(2)}) collective-permute-start(f32[16,16,256]{2,1,0:T(8,128)S(1)} %bitcast.87), channel_id=1, source_target_pairs={{0,2},{2,0},{1,3},{3,1},{4,6},{6,4},{5,7},{7,5},{8,10},{10,8},{9,1... | collective-permute-start | bytes 786440 | tf_op jit(solution)/shard_map/ppermute | solution.py:275
  55.3 28.1 %collective-permute-start.16 = (f32[8,16,256]{2,1,0:T(8,128)S(1)}, f32[8,16,256]{2,1,0:T(8,128)S(1)}, u32[]{:S(2)}, u32[]{:S(2)}) collective-permute-start(f32[8,16,256]{2,1,0:T(8,128)S(1)} %get-tuple-element.64), channel_id=1, source_target_pairs={{0,4},{4,0},{8,12},{12,8},{1,5},{5,1},{9,13},{13,9},{2,6},{6,2},{1... | collective-permute-start | bytes 393224 | tf_op jit(solution)/shard_map/ppermute | solution.py:286
  56.4 27.0 %collective-permute-start.17 = (f32[8,16,256]{2,1,0:T(8,128)S(1)}, f32[8,16,256]{2,1,0:T(8,128)S(1)}, u32[]{:S(2)}, u32[]{:S(2)}) collective-permute-start(f32[8,16,256]{2,1,0:T(8,128)S(1)} %get-tuple-element.65), channel_id=1, source_target_pairs={{0,8},{4,12},{8,0},{12,4},{1,9},{5,13},{9,1},{13,5},{2,10},{6,14},... | collective-permute-start | bytes 393224 | tf_op jit(solution)/shard_map/ppermute | solution.py:286
  58.9 24.5 %collective-permute-start.18 = (f32[8,16,256]{2,1,0:T(8,128)S(1)}, f32[8,16,256]{2,1,0:T(8,128)S(1)}, u32[]{:S(2)}, u32[]{:S(2)}) collective-permute-start(f32[8,16,256]{2,1,0:T(8,128)S(1)} %get-tuple-element.66), channel_id=1, source_target_pairs={{0,12},{4,8},{8,4},{12,0},{1,13},{5,9},{9,5},{13,1},{2,14},{6,10},... | collective-permute-start | bytes 393224 | tf_op jit(solution)/shard_map/ppermute | solution.py:286
  59.8 20.5 %collective-permute-start.10 = (f32[8,16,256]{2,1,0:T(8,128)S(1)}, f32[8,16,256]{2,1,0:T(8,128)S(1)}, u32[]{:S(2)}, u32[]{:S(2)}) collective-permute-start(f32[8,16,256]{2,1,0:T(8,128)S(1)} %get-tuple-element.59), channel_id=1, source_target_pairs={{0,8},{4,12},{8,0},{12,4},{1,9},{5,13},{9,1},{13,5},{2,10},{6,14},... | collective-permute-start | bytes 393224 | tf_op jit(solution)/shard_map/ppermute | solution.py:286
  61.7 18.6 %collective-permute-start.11 = (f32[8,16,256]{2,1,0:T(8,128)S(1)}, f32[8,16,256]{2,1,0:T(8,128)S(1)}, u32[]{:S(2)}, u32[]{:S(2)}) collective-permute-start(f32[8,16,256]{2,1,0:T(8,128)S(1)} %get-tuple-element.60), channel_id=1, source_target_pairs={{0,12},{4,8},{8,4},{12,0},{1,13},{5,9},{9,5},{13,1},{2,14},{6,10},... | collective-permute-start | bytes 393224 | tf_op jit(solution)/shard_map/ppermute | solution.py:286
  101.6 11.6 %collective-permute-start.29 = (f32[16,16,256]{2,1,0:T(8,128)S(1)}, f32[16,16,256]{2,1,0:T(8,128)S(1)}, u32[]{:S(2)}, u32[]{:S(2)}) collective-permute-start(f32[16,16,256]{2,1,0:T(8,128)S(1)} %bitcast.84), channel_id=1, source_target_pairs={{0,2},{2,0},{1,3},{3,1},{4,6},{6,4},{5,7},{7,5},{8,10},{10,8},{9,1... | collective-permute-start | bytes 786440 | tf_op jit(solution)/shard_map/ppermute | solution.py:275
  110.7 13.0 %collective-permute-start.24 = (f32[8,16,256]{2,1,0:T(8,128)S(1)}, f32[8,16,256]{2,1,0:T(8,128)S(1)}, u32[]{:S(2)}, u32[]{:S(2)}) collective-permute-start(f32[8,16,256]{2,1,0:T(8,128)S(1)} %get-tuple-element.73), channel_id=1, source_target_pairs={{0,8},{4,12},{8,0},{12,4},{1,9},{5,13},{9,1},{13,5},{2,10},{6,14},... | collective-permute-start | bytes 393224 | tf_op jit(solution)/shard_map/ppermute | solution.py:286
  111.6 12.1 %collective-permute-start.25 = (f32[8,16,256]{2,1,0:T(8,128)S(1)}, f32[8,16,256]{2,1,0:T(8,128)S(1)}, u32[]{:S(2)}, u32[]{:S(2)}) collective-permute-start(f32[8,16,256]{2,1,0:T(8,128)S(1)} %get-tuple-element.74), channel_id=1, source_target_pairs={{0,12},{4,8},{8,4},{12,0},{1,13},{5,9},{9,5},{13,1},{2,14},{6,10},... | collective-permute-start | bytes 393224 | tf_op jit(solution)/shard_map/ppermute | solution.py:286
  113.8 12.9 %collective-permute-start.30 = (f32[8,16,256]{2,1,0:T(8,128)S(1)}, f32[8,16,256]{2,1,0:T(8,128)S(1)}, u32[]{:S(2)}, u32[]{:S(2)}) collective-permute-start(f32[8,16,256]{2,1,0:T(8,128)S(1)} %get-tuple-element.79), channel_id=1, source_target_pairs={{0,4},{4,0},{8,12},{12,8},{1,5},{5,1},{9,13},{13,9},{2,6},{6,2},{1... | collective-permute-start | bytes 393224 | tf_op jit(solution)/shard_map/ppermute | solution.py:286
  115.6 18.0 %collective-permute-start.31 = (f32[8,16,256]{2,1,0:T(8,128)S(1)}, f32[8,16,256]{2,1,0:T(8,128)S(1)}, u32[]{:S(2)}, u32[]{:S(2)}) collective-permute-start(f32[8,16,256]{2,1,0:T(8,128)S(1)} %get-tuple-element.80), channel_id=1, source_target_pairs={{0,8},{4,12},{8,0},{12,4},{1,9},{5,13},{9,1},{13,5},{2,10},{6,14},... | collective-permute-start | bytes 393224 | tf_op jit(solution)/shard_map/ppermute | solution.py:286
  116.7 16.9 %collective-permute-start.32 = (f32[8,16,256]{2,1,0:T(8,128)S(1)}, f32[8,16,256]{2,1,0:T(8,128)S(1)}, u32[]{:S(2)}, u32[]{:S(2)}) collective-permute-start(f32[8,16,256]{2,1,0:T(8,128)S(1)} %get-tuple-element.81), channel_id=1, source_target_pairs={{0,12},{4,8},{8,4},{12,0},{1,13},{5,9},{9,5},{13,1},{2,14},{6,10},... | collective-permute-start | bytes 393224 | tf_op jit(solution)/shard_map/ppermute | solution.py:286
  148.9 13.6 %collective-permute-start.36 = (f32[16,16,256]{2,1,0:T(8,128)S(1)}, f32[16,16,256]{2,1,0:T(8,128)S(1)}, u32[]{:S(2)}, u32[]{:S(2)}) collective-permute-start(f32[16,16,256]{2,1,0:T(8,128)S(1)} %bitcast.86), channel_id=1, source_target_pairs={{0,2},{2,0},{1,3},{3,1},{4,6},{6,4},{5,7},{7,5},{8,10},{10,8},{9,1... | collective-permute-start | bytes 786440 | tf_op jit(solution)/shard_map/ppermute | solution.py:275
  160.0 13.0 %collective-permute-start.42 = (f32[8,16,256]{2,1,0:T(8,128)S(1)}, f32[8,16,256]{2,1,0:T(8,128)S(1)}, u32[]{:S(2)}, u32[]{:S(2)}) collective-permute-start(f32[8,16,256]{2,1,0:T(8,128)S(1)} %get-tuple-element.93), channel_id=1, source_target_pairs={{0,8},{4,12},{8,0},{12,4},{1,9},{5,13},{9,1},{13,5},{2,10},{6,14},... | collective-permute-start | bytes 393224 | tf_op jit(solution)/shard_map/ppermute | solution.py:286
  160.5 12.5 %collective-permute-start.43 = (f32[8,16,256]{2,1,0:T(8,128)S(1)}, f32[8,16,256]{2,1,0:T(8,128)S(1)}, u32[]{:S(2)}, u32[]{:S(2)}) collective-permute-start(f32[8,16,256]{2,1,0:T(8,128)S(1)} %get-tuple-element.94), channel_id=1, source_target_pairs={{0,12},{4,8},{8,4},{12,0},{1,13},{5,9},{9,5},{13,1},{2,14},{6,10},... | collective-permute-start | bytes 393224 | tf_op jit(solution)/shard_map/ppermute | solution.py:286
  163.1 11.5 %collective-permute-start.37 = (f32[8,16,256]{2,1,0:T(8,128)S(1)}, f32[8,16,256]{2,1,0:T(8,128)S(1)}, u32[]{:S(2)}, u32[]{:S(2)}) collective-permute-start(f32[8,16,256]{2,1,0:T(8,128)S(1)} %get-tuple-element.87), channel_id=1, source_target_pairs={{0,4},{4,0},{8,12},{12,8},{1,5},{5,1},{9,13},{13,9},{2,6},{6,2},{1... | collective-permute-start | bytes 393224 | tf_op jit(solution)/shard_map/ppermute | solution.py:286
  164.8 17.8 %collective-permute-start.38 = (f32[8,16,256]{2,1,0:T(8,128)S(1)}, f32[8,16,256]{2,1,0:T(8,128)S(1)}, u32[]{:S(2)}, u32[]{:S(2)}) collective-permute-start(f32[8,16,256]{2,1,0:T(8,128)S(1)} %get-tuple-element.88), channel_id=1, source_target_pairs={{0,8},{4,12},{8,0},{12,4},{1,9},{5,13},{9,1},{13,5},{2,10},{6,14},... | collective-permute-start | bytes 393224 | tf_op jit(solution)/shard_map/ppermute | solution.py:286
  165.6 17.0 %collective-permute-start.39 = (f32[8,16,256]{2,1,0:T(8,128)S(1)}, f32[8,16,256]{2,1,0:T(8,128)S(1)}, u32[]{:S(2)}, u32[]{:S(2)}) collective-permute-start(f32[8,16,256]{2,1,0:T(8,128)S(1)} %get-tuple-element.89), channel_id=1, source_target_pairs={{0,12},{4,8},{8,4},{12,0},{1,13},{5,9},{9,5},{13,1},{2,14},{6,10},... | collective-permute-start | bytes 393224 | tf_op jit(solution)/shard_map/ppermute | solution.py:286
  (36 other events, 398.2 us)
where the time goes:
time: 186 us; the launch traced here: 185 us
  waiting for transfers between devices  84 us (45%)
  starting transfers between devices  45.8 us (25%)
  Pallas kernels  39.2 us (21%)
  local copies, waits for them, and re-layouts  9.7 us (5%)
  other arithmetic  5.36 us (3%)
    ppermute x18, waiting for transfers between devices, local(): lax.ppermute(packs[k - 1], 'edge', [(i, i ^ k) for i in range(edges)])  41.9 us
    ppermute x18, starting transfers between devices, local(): lax.ppermute(packs[k - 1], 'edge', [(i, i ^ k) for i in range(edges)])  30.9 us
    ppermute x6, waiting for transfers between devices, local(): lax.ppermute(sent[d - 1], 'trip', [(i, (i + d) % trips) for i in range(tr...  19.8 us
    ppermute x6, waiting for transfers between devices, local(): lax.ppermute(lows[r], 'trip', [(i, (i + d) % trips) for i in range(trips)])  19.3 us
    pallas_call x6, Pallas kernels, local(): call(functools.partial(rows_kernel, (clusters, rc, cap, edges - 1, r * rc...  11.8 us
    ppermute x6, starting transfers between devices, local(): lax.ppermute(sent[d - 1], 'trip', [(i, (i + d) % trips) for i in range(tr...  6.4 us
    pallas_call x3, Pallas kernels, local(): call(functools.partial(gather_kernel, sizes, spots), [jax.ShapeDtypeStruc...  6.29 us
    ppermute x6, starting transfers between devices, local(): lax.ppermute(lows[r], 'trip', [(i, (i + d) % trips) for i in range(trips)])  6.1 us
  transfers between devices with their start and end apart: 44, of which 14 were waited for; matrix products, arithmetic and copies ran while one was open for 6% of the time, Pallas kernels for 15%

commit v1 on v0

v1 whole, which is shorter than its diff:
```python
import functools

import jax
import jax.numpy as jnp
from jax import lax
from jax.experimental import pallas as pl
from jax.experimental.pallas import tpu as pltpu
from jax.sharding import PartitionSpec as P

INV_THREE = 1.0 / 3.0**0.5
INV_TWO = 1.0 / 2.0**0.5
F32 = jnp.float32
BF16 = jnp.bfloat16
SMEM = pl.BlockSpec(memory_space=pltpu.SMEM)
VMEM = pl.BlockSpec(memory_space=pltpu.VMEM)
ANY = pl.BlockSpec(memory_space=pl.ANY)


def split(v):
    high = v.astype(BF16)
    return high, (v - high.astype(F32)).astype(BF16)


def dot(a, b):
    return jnp.dot(a, b, preferred_element_type=F32)


def dot3(a, high, low):
    a_high, a_low = split(a)
    return dot(a_high, high) + (dot(a_low, high) + dot(a_high, low))


def call(kernel, outs, ins, mib, out_specs=None, scratch=(), flops=0, moved=0, alias=None, grid=()):
    return pl.pallas_call(
        kernel,
        grid=grid,
        out_shape=outs,
        in_specs=ins,
        out_specs=jax.tree.map(lambda _: VMEM, outs) if out_specs is None else out_specs,
        scratch_shapes=list(scratch),
        input_output_aliases=alias or {},
        compiler_params=pltpu.CompilerParams(vmem_limit_bytes=mib << 20),
        cost_estimate=pl.CostEstimate(flops=flops, bytes_accessed=moved, transcendentals=0),
    )


def rows_of(clusters, start, size, width):
    return pl.BlockSpec((clusters, size, width), lambda i: (0, start // size, 0))


def add_cells(acc, d, pats, live, half, load, slots):
    def add(p, c):
        t, q = pats[half, 2 * p], pats[half, 2 * p + 1]
        acc[q, d, t] += load(p)
        return c

    lax.fori_loop(0, jnp.minimum(live[half], slots), add, 0)


def clear(acc):
    zero = jnp.zeros(acc.shape[1:], F32)

    def one(q, c):
        acc[q] = zero
        return c

    lax.fori_loop(0, acc.shape[0], one, 0)


def cells_kernel(sizes, ids, pats, live, mine, theirs, *refs):
    trips, subs, share, chunks, clusters = sizes
    outs, (buf, acc, sems) = refs[:-3], refs[-3:]
    n = len(chunks)
    rem_hi, rem_lo, loc_hi, loc_lo = (outs[i * n : (i + 1) * n] for i in range(4))
    x, s = ids[0], ids[1]
    slots, _, width = mine.shape
    copies = {}
    for half, ref in enumerate((mine, theirs)):
        for d in range(trips):
            start = pl.multiple_of((lax.rem(x + d, trips) * subs + s) * share, share)
            copies[half, d] = pltpu.make_async_copy(
                ref.at[:, pl.ds(start, share), :], buf.at[half, d], sems.at[half, d]
            )
            copies[half, d].start()
    clear(acc)
    for half in range(2):
        for d in range(trips):
            copies[half, d].wait()
            add_cells(acc, d, pats, live, half, lambda p, half=half, d=d: buf[half, d, p], slots)

    def finish(q, c):
        lanes = pl.ds(pl.multiple_of(q * width, width), width)
        for r, (off, rc) in enumerate(chunks):
            block = clusters * rc
            for d in range(trips):
                high, low = split(acc[q, d, :, off : off + rc, :].reshape(block, width))
                if d:
                    rem_hi[r][(d - 1) * block : d * block, lanes] = high
                    rem_lo[r][(d - 1) * block : d * block, lanes] = low
                else:
                    loc_hi[r][:, lanes] = high
                    loc_lo[r][:, lanes] = low
        return c

    lax.fori_loop(0, clusters, finish, 0)


def early_kernel(sizes, ids, pats, live, mine, theirs, *refs):
    subs, share, off, rc, clusters = sizes
    far, (out_hi, out_lo, buf, acc, sems) = refs[:-5], refs[-5:]
    slots, _, width = mine.shape
    start = pl.multiple_of((ids[0] * subs + ids[1]) * share + off, rc)
    copies = []
    for half, ref in enumerate((mine, theirs)):
        copies.append(pltpu.make_async_copy(ref.at[:, pl.ds(start, rc), :], buf.at[half], sems.at[half]))
        copies[-1].start()
    clear(acc)
    for i, ref in enumerate(far):
        add_cells(acc, 0, pats, live, 2 + i, lambda p, ref=ref: ref[p], slots)
    for half in range(2):
        copies[half].wait()
        add_cells(acc, 0, pats, live, half, lambda p, half=half: buf[half, p], slots)

    def finish(q, c):
        lanes = pl.ds(pl.multiple_of(q * width, width), width)
        high, low = split(acc[q, 0].reshape(clusters * rc, width))
        out_hi[:, lanes] = high
        out_lo[:, lanes] = low
        return c

    lax.fori_loop(0, clusters, finish, 0)


def terms(c_hi, c_lo, x_hi, x_lo):
    return dot(c_hi[...], x_hi[...]) + (dot(c_lo[...], x_hi[...]) + dot(c_hi[...], x_lo[...]))


def terms_kernel(c_hi, c_lo, x_hi, x_lo, out):
    out[...] = terms(c_hi, c_lo, x_hi, x_lo)


def pack(agg, send_src, cap, packs):
    for k, ref in enumerate(packs):
        for j in range(cap):
            ref[j] = agg[send_src[(k + 1) * cap + j]]


def gather_kernel(sizes, places, whole, ids, send_src, c_hi, c_lo, *refs):
    trips, subs, share, n, clusters, rows, cap = sizes
    count = len(places) * n
    pieces, (x_hi, x_lo, *outs) = refs[:count], refs[count:]
    x, s = ids[0], ids[1]
    for i, (d, other) in enumerate(places):
        at = (lax.rem(x + trips - d, trips) * subs + (1 - s if other else s)) * share
        group = pieces[i * n : (i + 1) * n]
        for q in range(clusters):
            high, low = split(jnp.concatenate([ref[q] for ref in group], axis=0))
            spot = pl.ds(pl.multiple_of(q * rows + at, share), share)
            x_hi[spot, :] = high
            x_lo[spot, :] = low
    out = terms(c_hi, c_lo, x_hi, x_lo)
    if whole:
        agg, *packs = outs
        agg[...] = out.reshape(agg.shape)
        pack(agg, send_src, cap, packs)
    else:
        outs[0][...] = out


def pack_kernel(cap, arrivals, send_src, local, *refs):
    got, agg, packs = refs[:arrivals], refs[arrivals], refs[arrivals + 1 :]
    total = local[...]
    for ref in got:
        total = total + ref[...]
    agg[...] = total
    pack(agg, send_src, cap, packs)


def rows_kernel(sizes, last, alias, recv_pos, counts, ids, *refs):
    clusters, rc, cap, steps, first_row = sizes
    feat, agg, refs = refs[0], refs[1], refs[2:]
    got, refs = refs[:steps], refs[steps:]
    up_hi, up_lo, dense_hi, dense_lo, refs = *refs[:4], refs[4:]
    if last:
        out, held, both = refs[1:] if alias else refs
    else:
        down, (out, low_out, held, both) = refs[:2], refs[2:]
    for k, ref in enumerate(got):
        held[k * cap : (k + 1) * cap] = ref[...]
    for c in range(clusters):
        both[c] = agg[c] + held[recv_pos[c] - cap]
    block = clusters * rc
    lifted = dot3(both[...].reshape(block, -1), up_hi[...], up_lo[...])
    merged = (feat[...].reshape(block, -1) + lifted) * INV_THREE
    v = dot3(merged, dense_hi[...], dense_lo[...])
    result = (merged + v / (1.0 + jnp.exp(-v))) * INV_TWO
    out[...] = result.reshape(out.shape)
    if not last:
        lower(result, down[0][...], down[1][...], counts, ids, first_row, low_out)


def lower(feat, down_hi, down_lo, counts, ids, first_row, out):
    clusters, rc, width = out.shape
    low = dot3(feat, down_hi, down_lo)
    row = ids[2] + first_row + lax.broadcasted_iota(jnp.int32, (rc, width), 0)
    for c in range(clusters):
        out[c] = jnp.where(row < counts[c], low[c * rc : (c + 1) * rc, :], 0.0)


def down_kernel(first_row, counts, ids, feat, down, out):
    high, low = split(down[...])
    block = out.shape[0] * out.shape[1]
    lower(feat[...].reshape(block, -1), high, low, counts, ids, first_row, out)


def local(
    edge_feat,
    edge_counts,
    reverse,
    patterns,
    trip_count,
    coef,
    down_weight,
    up_weight,
    dense_weight,
):
    clusters, share, feat_width = edge_feat.shape
    layers, _, width = down_weight.shape
    edges, trips, subs = (lax.axis_size(a) for a in ("edge", "trip", "sub"))
    e, x, s = (lax.axis_index(a) for a in ("edge", "trip", "sub"))
    rows = trips * subs * share
    cap = 2 * ((clusters // 2 + edges // 2 - 1) // (edges // 2))
    half_share = share // 2
    chunks = [(0, half_share)] + [(half_share + i, 8) for i in range(0, half_share, 8)]
    n = len(chunks)
    depth = clusters * rows
    slots = patterns.shape[2]
    swap = [(0, 1), (1, 0)]

    def turn(d):
        return [(i, (i + d) % trips) for i in range(trips)]

    ids = jnp.stack([x, s, (x * subs + s) * share]).astype(jnp.int32)
    coef = coef.reshape(coef.shape[2:])
    coef2 = lax.ppermute(coef, "sub", swap)

    def small(rc):
        return jax.ShapeDtypeStruct((clusters, rc, width), F32)

    def big(rc):
        return jax.ShapeDtypeStruct((clusters, rc, feat_width), F32)

    lows = [
        call(
            functools.partial(down_kernel, off),
            small(rc),
            [
                SMEM,
                SMEM,
                rows_of(clusters, off, rc, feat_width),
                pl.BlockSpec((None, feat_width, width), lambda i: (0, 0, 0)),
            ],
            16,
            flops=6 * clusters * rc * feat_width * width,
            grid=(1,),
            out_specs=pl.BlockSpec((clusters, rc, width), lambda i: (0, 0, 0)),
        )(edge_counts, ids, edge_feat, down_weight)
        for off, rc in chunks
    ]
    (down_weight, up_weight, dense_weight, reverse, patterns, trip_count, *lows) = lax.optimization_barrier(
        (down_weight, up_weight, dense_weight, reverse, patterns, trip_count, *lows)
    )

    note = jnp.concatenate([patterns.reshape(-1), trip_count.reshape(-1)])
    note = jnp.stack([note, lax.ppermute(note, "sub", swap)])
    notes = jnp.concatenate([note] + [lax.ppermute(note, "trip", turn(d)) for d in range(1, trips)])
    pats, live = notes[:, :-1], notes[:, -1]

    here = jnp.arange(clusters, dtype=jnp.int32)
    mine = lax.dynamic_slice_in_dim(reverse, e * clusters, clusters)
    to = mine // clusters
    earlier = (to[:, None] == to[None, :]) & (here[None, :] < here[:, None])
    send_pos = (to ^ e) * cap + jnp.sum(earlier.astype(jnp.int32), axis=1)
    places = jnp.arange(edges * cap, dtype=jnp.int32)
    send_src = jnp.sum(jnp.where(places[:, None] == send_pos[None, :], here[None, :], 0), axis=1)
    everyone = jnp.arange(reverse.shape[0], dtype=jnp.int32)
    before = (
        (everyone[None, :] // clusters == to[:, None])
        & (everyone[None, :] < mine[:, None])
        & ((reverse // clusters)[None, :] == e)
    )
    recv_pos = (to ^ e) * cap + jnp.sum(before.astype(jnp.int32), axis=1)

    def parts(w):
        high = lax.reduce_precision(w, 8, 7)
        return high.astype(BF16), (w - high).astype(BF16)

    down = [parts(down_weight[i]) for i in range(1, layers)]
    up = [parts(up_weight[i]) for i in range(layers)]
    dense = [parts(dense_weight[i]) for i in range(layers)]

    cells = call(
        functools.partial(cells_kernel, (trips, subs, share, chunks, clusters)),
        [jax.ShapeDtypeStruct(((trips - 1) * clusters * rc, depth), BF16) for _, rc in chunks] * 2
        + [jax.ShapeDtypeStruct((clusters * rc, depth), BF16) for _, rc in chunks] * 2,
        [SMEM, SMEM, SMEM, ANY, ANY],
        40,
        scratch=[
            pltpu.VMEM((2, trips, slots, share, rows), F32),
            pltpu.VMEM((clusters, trips, clusters, share, rows), F32),
            pltpu.SemaphoreType.DMA((2, trips)),
        ],
        moved=12 << 20,
    )(ids, pats[:2], live[:2], coef, coef2)
    rem_hi, rem_lo, loc_hi, loc_lo = (cells[i * n : (i + 1) * n] for i in range(4))

    feats, first = None, None
    for layer in range(layers):
        last = layer == layers - 1
        places = [(d, other) for d in range(trips) for other in range(2)]
        pieces = {}
        for r in range(n):
            for d in range(trips):
                far = lax.ppermute(lows[r], "trip", turn(d)) if d else lows[r]
                pieces[d, 0, r] = far
                pieces[d, 1, r] = lax.ppermute(far, "sub", swap)
        inputs = [pieces[d, other, r] for d, other in places for r in range(n)]
        whole = layer > 0
        order = list(range(n)) if whole else [1, 0, *range(2, n)]
        lead = order[0]
        lead_rc = chunks[lead][1]
        c_hi, c_lo = first if whole else (rem_hi[lead], rem_lo[lead])
        if whole:
            outs = [small(lead_rc)] + [jax.ShapeDtypeStruct((cap, lead_rc, width), F32)] * (edges - 1)
        else:
            outs = [jax.ShapeDtypeStruct(((trips - 1) * clusters * lead_rc, width), F32)]
        x_hi, x_lo, *outs = call(
            functools.partial(gather_kernel, (trips, subs, share, n, clusters, rows, cap), places, whole),
            [jax.ShapeDtypeStruct((depth, width), BF16)] * 2 + outs,
            [SMEM, SMEM, VMEM, VMEM] + [VMEM] * len(inputs),
            32,
            flops=6 * c_hi.shape[0] * depth * width,
        )(ids, send_src, c_hi, c_lo, *inputs)

        def product(high, low, x_hi=x_hi, x_lo=x_lo):
            return call(
                terms_kernel,
                jax.ShapeDtypeStruct((high.shape[0], width), F32),
                [VMEM] * 4,
                32,
                flops=6 * high.shape[0] * depth * width,
            )(high, low, x_hi, x_lo)

        summed = order[1:] if whole else order
        sent = {r: outs[0] if r == lead and not whole else product(rem_hi[r], rem_lo[r]) for r in summed}
        got = {}
        for r in summed:
            block = clusters * chunks[r][1]
            got[r] = [
                lax.ppermute(
                    sent[r][(d - 1) * block : d * block].reshape(clusters, -1, width), "trip", turn(d)
                )
                for d in range(1, trips)
            ]
        if layer == 0:
            off, rc = chunks[0]
            base, got[summed[-1]] = lax.optimization_barrier((ids, got[summed[-1]]))
            far = []
            for d in range(1, trips):
                for other in range(2):
                    core = 1 - base[1] if other else base[1]
                    start = (lax.rem(base[0] + d, trips) * subs + core) * share + off
                    part = lax.dynamic_slice_in_dim(coef, start, rc, 1)
                    perm = [
                        (i * subs + j, (i + d) % trips * subs + (j ^ other)) for i in range(trips) for j in range(subs)
                    ]
                    far.append(lax.ppermute(part, ("trip", "sub"), perm))
            first = call(
                functools.partial(early_kernel, (subs, share, off, rc, clusters)),
                [jax.ShapeDtypeStruct((clusters * rc, depth), BF16)] * 2,
                [SMEM, SMEM, SMEM, ANY, ANY] + [VMEM] * len(far),
                40,
                scratch=[
                    pltpu.VMEM((2, slots, rc, rows), F32),
                    pltpu.VMEM((clusters, 1, clusters, rc, rows), F32),
                    pltpu.SemaphoreType.DMA((2,)),
                ],
                moved=6 << 20,
            )(ids, pats, live, coef, coef2, *far)
        next_feats, next_lows = [None] * n, [None] * n
        result = None
        for r in order:
            off, rc = chunks[r]
            block = clusters * rc
            if r in summed:
                own = product(loc_hi[r], loc_lo[r]).reshape(clusters, rc, width)
                agg, *packs = call(
                    functools.partial(pack_kernel, cap, trips - 1),
                    [small(rc)] + [jax.ShapeDtypeStruct((cap, rc, width), F32)] * (edges - 1),
                    [SMEM] + [VMEM] * trips,
                    16,
                    moved=4 << 20,
                )(send_src, own, *got[r])
            else:
                agg, *packs = outs
            back = [None] * (edges - 1)
            for k in range(edges - 1, 0, -1):
                back[k - 1] = lax.ppermute(packs[k - 1], "edge", [(i, i ^ k) for i in range(edges)])
            alias = last and result is not None
            feat, feat_spec = (
                (edge_feat, rows_of(clusters, off, rc, feat_width))
                if layer == 0
                else (feats[r], pl.BlockSpec((clusters, rc, feat_width), lambda i: (0, 0, 0)))
            )
            extra = ([result] if alias else []) if last else list(down[layer])
            before_extra = 3 + 2 + (edges - 1) + 4
            result = call(
                functools.partial(rows_kernel, (clusters, rc, cap, edges - 1, off), last, alias),
                big(share) if last else [big(rc), small(rc)],
                [SMEM] * 3
                + [feat_spec]
                + [VMEM] * (1 + edges - 1 + 4)
                + ([ANY] * len(extra) if last else [VMEM] * len(extra)),
                32,
                grid=(1,),
                out_specs=rows_of(clusters, off, rc, feat_width) if last else [VMEM, VMEM],
                scratch=[
                    pltpu.VMEM(((edges - 1) * cap, rc, width), F32),
                    pltpu.VMEM((clusters, rc, width), F32),
                ],
                flops=6 * block * feat_width * (2 * width + feat_width),
                alias={before_extra: 0} if alias else None,
            )(recv_pos, edge_counts, ids, feat, agg, *back, *up[layer], *dense[layer], *extra)
            if not last:
                next_feats[r], next_lows[r] = result
        feats, lows = next_feats, next_lows
    return result


def solution(mesh):
    placed = (
        P(("groups", "edge"), ("trip", "sub"), None),
        P(("groups", "edge")),
        P("groups"),
        P(("groups", "edge"), ("trip", "sub"), None, None),
        P(("groups", "edge"), ("trip", "sub")),
        P(("groups", "edge"), ("trip", "sub"), None, None, None),
        P(),
        P(),
        P(),
    )
    return jax.shard_map(
        local,
        mesh=mesh,
        in_specs=placed,
        out_specs=P(("groups", "edge"), ("trip", "sub"), None),
        check_vma=False,
    )
```

time: 186 us -> 187 us (level)
  waiting for transfers between devices: 84 us -> 34.9 us
  starting transfers between devices: 45.8 us -> 78.2 us
  Pallas kernels: 39.2 us -> 49.6 us
  local copies, waits for them, and re-layouts: 9.7 us -> 13.4 us
  between operations: 1.17 us -> 3.68 us
    ppermute x26 -> x39, waiting for transfers between devices: 42.2 us -> 15.7 us  [the longest x9 12 us: local(): far = lax.ppermute(lows[r], 'trip', turn(d)) if d else lows[r]]
    ppermute x18 -> x27, waiting for transfers between devices: 41.9 us -> 19.2 us  [local(): lax.ppermute(packs[k - 1], 'edge', [(i, i ^ k) for i in range(edges)])]
    ppermute x18 -> x27, starting transfers between devices: 30.9 us -> 52.4 us  [local(): lax.ppermute(packs[k - 1], 'edge', [(i, i ^ k) for i in range(edges)])]
    ppermute x26 -> x39, starting transfers between devices: 14.9 us -> 25.8 us  [the longest x9 12.5 us: local(): far = lax.ppermute(lows[r], 'trip', turn(d)) if d else lows[r]]
    unnamed x33 -> x126, local copies, waits for them, and re-layouts: 0.49 us -> 10.9 us
    pallas_call x24 -> x37, Pallas kernels: 39.2 us -> 49.6 us  [the longest x9 16.5 us: local(): call(functools.partial(rows_kernel, (clusters, rc, cap, edges - 1, off),...]
    squeeze x5 -> x0, local copies, waits for them, and re-layouts: 6.9 us -> none  [the longest x1 4.22 us: local(): give = lax.dynamic_index_in_dim(halves, 1 - s, 2, keepdims=False)]
  transfers between devices with their start and end apart: 44 -> 66, of which waited for: 14 -> 14; matrix products, arithmetic and copies ran while one was open for 6% -> 5% of each run, Pallas kernels for 15% -> 23%
where the time goes in v1:
time: 187 us
  starting transfers between devices  78.2 us (42%)
  Pallas kernels  49.6 us (27%)
  waiting for transfers between devices  34.9 us (19%)
  local copies, waits for them, and re-layouts  13.4 us (7%)
  other arithmetic  7.1 us (4%)
  between operations  3.68 us (2%)
    ppermute x27, starting transfers between devices, local(): lax.ppermute(packs[k - 1], 'edge', [(i, i ^ k) for i in range(edges)])  52.4 us
    ppermute x27, waiting for transfers between devices, local(): lax.ppermute(packs[k - 1], 'edge', [(i, i ^ k) for i in range(edges)])  19.2 us
    pallas_call x9, Pallas kernels, local(): call(functools.partial(rows_kernel, (clusters, rc, cap, edges - 1, off),...  16.5 us
    ppermute x9, starting transfers between devices, local(): far = lax.ppermute(lows[r], 'trip', turn(d)) if d else lows[r]  12.5 us
    ppermute x9, waiting for transfers between devices, local(): far = lax.ppermute(lows[r], 'trip', turn(d)) if d else lows[r]  12 us
    unnamed x126, local copies, waits for them, and re-layouts  10.9 us
    pallas_call x13, Pallas kernels, product(): call(terms_kernel, jax.ShapeDtypeStruct((high.shape[0], width), F32), [VM...  9.09 us
    ppermute x7, starting transfers between devices, local(): lax.ppermute(sent[r][(d - 1) * block:d * block].reshape(clusters, -1, wid...  7.51 us
  transfers between devices with their start and end apart: 66, of which 14 were waited for; matrix products, arithmetic and copies ran while one was open for 5% of the time, Pallas kernels for 23%

profile of v1, /device:TPU:0, one launch (start us, length us, event | category | flops | bytes accessed | tf_op | source)
XLA Modules:
  0.0 187.0 jit_solution(11441338200503402635)
XLA Ops:
  6.5 2.6 %collective-permute-start.6 = (f32[16,8,256]{2,1,0:T(8,128)S(1)}, f32[16,8,256]{2,1,0:T(8,128)S(1)}, u32[]{:S(2)}, u32[]{:S(2)}) collective-permute-start(f32[16,8,256]{2,1,0:T(8,128)S(1)} %shard_map.92.refs_1_), channel_id=1, source_target_pairs={{0,2},{2,0},{1,3},{3,1},{4,6},{6,4},{5,7},{7,5},{8,10},{10,8},{9,1... | collective-permute-start | bytes 393224 | tf_op jit(solution)/shard_map/ppermute | solution.py:324
  16.9 4.9 %collective-permute-done.7.refs_8_ = f32[16,8,256]{2,1,0:T(8,128)S(1)} collective-permute-done((f32[16,8,256]{2,1,0:T(8,128)S(1)}, f32[16,8,256]{2,1,0:T(8,128)S(1)}, u32[]{:S(2)}, u32[]{:S(2)}) %collective-permute-start.7) | collective-permute-done | bytes 131104 | tf_op jit(solution)/shard_map/ppermute | solution.py:324
  25.9 6.5 %shard_map.94 = (bf16[256,2048]{1,0:T(8,128)(2,1)S(1)}, bf16[128,2048]{1,0:T(8,128)(2,1)S(1)}, bf16[128,2048]{1,0:T(8,128)(2,1)S(1)}, bf16[256,2048]{1,0:T(8,128...) custom-call(s32[3]{0:T(128)S(1)} %pad_add_fusion.3.ids, ...), custom_call_target="tpu_custom_call" | custom-call | bytes 12582912 | tf_op jit(solution)/shard_map/pallas_call | solution.py:302
  36.2 2.1 %shard_map.95 = (bf16[2048,256]{1,0:T(8,128)(2,1)S(1)}, bf16[2048,256]{1,0:T(8,128)(2,1)S(1)}, f32[128,256]{1,0:T(8,128)}) custom-call(s32[3]{0:T(128)S(1)} %pad_add_fusion.3.ids, s32[32]{0:T(128)S(1)} %select_reduce_fusion.send_src, bf16[128,2048]{1,0:T(8,128)(2,1)S(1)} %get-tuple-element.90.c_hi, bf16[128,2048]{1,0:T(8,128)(2,1)S(1)} %get-tuple-element.91.c_lo, ...), custom_call_target="tpu_custom_call" | custom-call | flops 402653184 | tf_op jit(solution)/shard_map/pallas_call | solution.py:337
  45.5 2.2 %collective-permute-done.11.refs_0_ = f32[16,8,256]{2,1,0:T(8,128)S(1)} collective-permute-done((f32[16,8,256]{2,1,0:T(8,128)S(1)}, f32[16,8,256]{2,1,0:T(8,128)S(1)}, u32[]{:S(2)}, u32[]{:S(2)}) %collective-permute-start.11) | collective-permute-done | bytes 131104 | tf_op jit(solution)/shard_map/ppermute | solution.py:360
  61.3 2.4 %collective-permute-start.20 = (f32[8,16,256]{2,1,0:T(8,128)S(1)}, f32[8,16,256]{2,1,0:T(8,128)S(1)}, u32[]{:S(2)}, u32[]{:S(2)}) collective-permute-start(f32[8,16,256]{2,1,0:T(8,128)S(1)} %get-tuple-element.117), channel_id=1, source_target_pairs={{0,8},{4,12},{8,0},{12,4},{1,9},{5,13},{9,1},{13,5},{2,10},{6,14},... | collective-permute-start | bytes 393224 | tf_op jit(solution)/shard_map/ppermute | solution.py:408
  66.5 3.0 %collective-permute-done.19.refs_2_ = f32[8,16,256]{2,1,0:T(8,128)S(1)} collective-permute-done((f32[8,16,256]{2,1,0:T(8,128)S(1)}, f32[8,16,256]{2,1,0:T(8,128)S(1)}, u32[]{:S(2)}, u32[]{:S(2)}) %collective-permute-start.19) | collective-permute-done | bytes 131104 | tf_op jit(solution)/shard_map/ppermute | solution.py:408
  69.9 9.4 %collective-permute-start.25 = (f32[8,8,256]{2,1,0:T(8,128)S(1)}, f32[8,8,256]{2,1,0:T(8,128)S(1)}, u32[]{:S(2)}, u32[]{:S(2)}) collective-permute-start(f32[8,8,256]{2,1,0:T(8,128)S(1)} %copy-done.52), channel_id=1, source_target_pairs={{0,12},{4,8},{8,4},{12,0},{1,13},{5,9},{9,5},{13,1},{2,14},{6,10},... | collective-permute-start | bytes 196616 | tf_op jit(solution)/shard_map/ppermute | solution.py:408
  79.3 2.1 %shard_map.104 = (f32[16,16,512]{2,1,0:T(8,128)S(1)}, f32[16,16,256]{2,1,0:T(8,128)S(1)}) custom-call(s32[16]{0:T(128)S(1)} %get-tuple-element.188.recv_pos, s32[16]{0:T(128)S(1)} %copy-done.48, s32[3]{0:T(128)S(1)} %pad_add_fusion.3.ids, f32[16,32,512]{2,1,0:T(8,128)S(1)} %copy-done.1, f32[16,16,256]{2,1,0:T(8,128)S(1)} %get-tuple-element.115.refs_1_, ...), custom_call_target="tpu_custom_call" | custom-call | flops 805306368 | tf_op jit(solution)/shard_map/pallas_call | solution.py:417
  87.1 3.3 %collective-permute-start.14 = (f32[8,8,256]{2,1,0:T(8,128)S(1)}, f32[8,8,256]{2,1,0:T(8,128)S(1)}, u32[]{:S(2)}, u32[]{:S(2)}) collective-permute-start(f32[8,8,256]{2,1,0:T(8,128)S(1)} %get-tuple-element.103), channel_id=1, source_target_pairs={{0,12},{4,8},{8,4},{12,0},{1,13},{5,9},{9,5},{13,1},{2,14},{6,10},... | collective-permute-start | bytes 196616 | tf_op jit(solution)/shard_map/ppermute | solution.py:408
  90.3 2.9 %collective-permute-done.14.refs_4_ = f32[8,8,256]{2,1,0:T(8,128)S(1)} collective-permute-done((f32[8,8,256]{2,1,0:T(8,128)S(1)}, f32[8,8,256]{2,1,0:T(8,128)S(1)}, u32[]{:S(2)}, u32[]{:S(2)}) %collective-permute-start.14) | collective-permute-done | bytes 65568 | tf_op jit(solution)/shard_map/ppermute | solution.py:408
  96.6 4.2 %collective-permute-done.31.refs_8_ = f32[16,8,256]{2,1,0:T(8,128)S(1)} collective-permute-done((f32[16,8,256]{2,1,0:T(8,128)S(1)}, f32[16,8,256]{2,1,0:T(8,128)S(1)}, u32[]{:S(2)}, u32[]{:S(2)}) %collective-permute-start.31) | collective-permute-done | bytes 131104 | tf_op jit(solution)/shard_map/ppermute | solution.py:324
  102.2 3.6 %shard_map.100 = (bf16[256,2048]{1,0:T(8,128)(2,1)S(1)}, bf16[256,2048]{1,0:T(8,128)(2,1)S(1)}) custom-call(s32[3]{0:T(128)S(1)} %pad_add_fusion.3.ids, s32[4,128]{1,0:T(4,128)S(1)} %slice.70.pats, s32[4]{0:T(128)S(1)} %slice_reduce_fusion.live, f32[64,128,128]{2,1,0:T(8,128)S(1)} %bitcast.56, f32[64,128,128]{2,1,0:T(8,128)} %collective-permute-done.1.theirs, ...), custom_call_target="tpu_custom_call" | custom-call | bytes 6291456 | tf_op jit(solution)/shard_map/pallas_call | solution.py:378
  108.2 3.6 %collective-permute-start.40 = (f32[8,16,256]{2,1,0:T(8,128)S(1)}, f32[8,16,256]{2,1,0:T(8,128)S(1)}, u32[]{:S(2)}, u32[]{:S(2)}) collective-permute-start(f32[8,16,256]{2,1,0:T(8,128)S(1)} %get-tuple-element.139), channel_id=1, source_target_pairs={{0,8},{4,12},{8,0},{12,4},{1,9},{5,13},{9,1},{13,5},{2,10},{6,14},... | collective-permute-start | bytes 393224 | tf_op jit(solution)/shard_map/ppermute | solution.py:408
  116.2 5.5 %collective-permute-done.40.refs_3_ = f32[8,16,256]{2,1,0:T(8,128)S(1)} collective-permute-done((f32[8,16,256]{2,1,0:T(8,128)S(1)}, f32[8,16,256]{2,1,0:T(8,128)S(1)}, u32[]{:S(2)}, u32[]{:S(2)}) %collective-permute-start.40) | collective-permute-done | bytes 131104 | tf_op jit(solution)/shard_map/ppermute | solution.py:408
  121.7 2.1 %shard_map.113 = (f32[16,16,512]{2,1,0:T(8,128)S(1)}, f32[16,16,256]{2,1,0:T(8,128)S(1)}) custom-call(s32[16]{0:T(128)S(1)} %get-tuple-element.188.recv_pos, s32[16]{0:T(128)S(1)} %copy-done.48, s32[3]{0:T(128)S(1)} %pad_add_fusion.3.ids, f32[16,16,512]{2,1,0:T(8,128)S(1)} %get-tuple-element.136.refs_0_, f32[16,16,256]{2,1,0:T(8,128)S(1)} %get-tuple-element.137.refs_1_, ...), custom_call_target="tpu_custom_call" | custom-call | flops 805306368 | tf_op jit(solution)/shard_map/pallas_call | solution.py:417
  127.7 3.0 %collective-permute-start.43 = (f32[8,8,256]{2,1,0:T(8,128)S(1)}, f32[8,8,256]{2,1,0:T(8,128)S(1)}, u32[]{:S(2)}, u32[]{:S(2)}) collective-permute-start(f32[8,8,256]{2,1,0:T(8,128)S(1)} %get-tuple-element.144), channel_id=1, source_target_pairs={{0,4},{4,0},{8,12},{12,8},{1,5},{5,1},{9,13},{13,9},{2,6},{6,2},{1... | collective-permute-start | bytes 196616 | tf_op jit(solution)/shard_map/ppermute | solution.py:408
  134.5 3.6 %collective-permute-start.36 = (f32[8,8,256]{2,1,0:T(8,128)S(1)}, f32[8,8,256]{2,1,0:T(8,128)S(1)}, u32[]{:S(2)}, u32[]{:S(2)}) collective-permute-start(f32[8,8,256]{2,1,0:T(8,128)S(1)} %get-tuple-element.132), channel_id=1, source_target_pairs={{0,4},{4,0},{8,12},{12,8},{1,5},{5,1},{9,13},{13,9},{2,6},{6,2},{1... | collective-permute-start | bytes 196616 | tf_op jit(solution)/shard_map/ppermute | solution.py:408
  149.0 2.9 %collective-permute-done.51.refs_8_ = f32[16,8,256]{2,1,0:T(8,128)S(1)} collective-permute-done((f32[16,8,256]{2,1,0:T(8,128)S(1)}, f32[16,8,256]{2,1,0:T(8,128)S(1)}, u32[]{:S(2)}, u32[]{:S(2)}) %collective-permute-start.51) | collective-permute-done | bytes 131104 | tf_op jit(solution)/shard_map/ppermute | solution.py:324
  159.5 2.4 %collective-permute-start.64 = (f32[8,16,256]{2,1,0:T(8,128)S(1)}, f32[8,16,256]{2,1,0:T(8,128)S(1)}, u32[]{:S(2)}, u32[]{:S(2)}) collective-permute-start(f32[8,16,256]{2,1,0:T(8,128)S(1)} %get-tuple-element.163), channel_id=1, source_target_pairs={{0,8},{4,12},{8,0},{12,4},{1,9},{5,13},{9,1},{13,5},{2,10},{6,14},... | collective-permute-start | bytes 393224 | tf_op jit(solution)/shard_map/ppermute | solution.py:408
  164.8 3.3 %collective-permute-start.61 = (f32[8,8,256]{2,1,0:T(8,128)S(1)}, f32[8,8,256]{2,1,0:T(8,128)S(1)}, u32[]{:S(2)}, u32[]{:S(2)}) collective-permute-start(f32[8,8,256]{2,1,0:T(8,128)S(1)} %get-tuple-element.158), channel_id=1, source_target_pairs={{0,8},{4,12},{8,0},{12,4},{1,9},{5,13},{9,1},{13,5},{2,10},{6,14},... | collective-permute-start | bytes 196616 | tf_op jit(solution)/shard_map/ppermute | solution.py:408
  169.8 4.0 %collective-permute-done.64.refs_3_ = f32[8,16,256]{2,1,0:T(8,128)S(1)} collective-permute-done((f32[8,16,256]{2,1,0:T(8,128)S(1)}, f32[8,16,256]{2,1,0:T(8,128)S(1)}, u32[]{:S(2)}, u32[]{:S(2)}) %collective-permute-start.64) | collective-permute-done | bytes 131104 | tf_op jit(solution)/shard_map/ppermute | solution.py:408
  173.8 5.2 %collective-permute-start.57 = (f32[8,8,256]{2,1,0:T(8,128)S(1)}, f32[8,8,256]{2,1,0:T(8,128)S(1)}, u32[]{:S(2)}, u32[]{:S(2)}) collective-permute-start(f32[8,8,256]{2,1,0:T(8,128)S(1)} %get-tuple-element.153), channel_id=1, source_target_pairs={{0,8},{4,12},{8,0},{12,4},{1,9},{5,13},{9,1},{13,5},{2,10},{6,14},... | collective-permute-start | bytes 196616 | tf_op jit(solution)/shard_map/ppermute | solution.py:408
  180.6 2.3 %shard_map.125.refs_9_ = f32[16,32,512]{2,1,0:T(8,128)} custom-call(s32[16]{0:T(128)S(1)} %get-tuple-element.188.recv_pos, s32[16]{0:T(128)S(1)} %copy-done.48, s32[3]{0:T(128)S(1)} %pad_add_fusion.3.ids, f32[16,16,512]{2,1,0:T(8,128)S(1)} %get-tuple-element.160.refs_0_, f32[16,16,256]{2,1,0:T(8,128)S(1)} %get-tuple-element.161.refs_1_, ...), custom_call_target="tpu_custom_call" | custom-call | flops 805306368 | tf_op jit(solution)/shard_map/pallas_call | solution.py:417
  (293 shorter events, 96.5 us)
Async XLA Ops:
  0.0 23.0 %collective-permute-start.1 = (f32[64,128,128]{2,1,0:T(8,128)}, f32[64,128,128]{2,1,0:T(8,128)}, u32[]{:S(2)}, u32[]{:S(2)}) collective-permute-start(f32[64,128,128]{2,1,0:T(8,128)} %bitcast.54), channel_id=1, source_target_pairs={{0,1},{1,0},{2,3},{3,2},{4,5},{5,4},{6,7},{7,6},{8,9},{9,8},{10,11... | collective-permute-start | bytes 12582920 | tf_op jit(solution)/shard_map/ppermute | solution.py:245
  6.5 15.9 %collective-permute-start.6 = (f32[16,8,256]{2,1,0:T(8,128)S(1)}, f32[16,8,256]{2,1,0:T(8,128)S(1)}, u32[]{:S(2)}, u32[]{:S(2)}) collective-permute-start(f32[16,8,256]{2,1,0:T(8,128)S(1)} %shard_map.92.refs_1_), channel_id=1, source_target_pairs={{0,2},{2,0},{1,3},{3,1},{4,6},{6,4},{5,7},{7,5},{8,10},{10,8},{9,1... | collective-permute-start | bytes 393224 | tf_op jit(solution)/shard_map/ppermute | solution.py:324
  9.0 13.5 %collective-permute-start.3 = (f32[16,8,256]{2,1,0:T(8,128)S(1)}, f32[16,8,256]{2,1,0:T(8,128)S(1)}, u32[]{:S(2)}, u32[]{:S(2)}) collective-permute-start(f32[16,8,256]{2,1,0:T(8,128)S(1)} %shard_map.92.refs_1_), channel_id=1, source_target_pairs={{0,1},{1,0},{2,3},{3,2},{4,5},{5,4},{6,7},{7,6},{8,9},{9,8},{10,11... | collective-permute-start | bytes 393224 | tf_op jit(solution)/shard_map/ppermute | solution.py:326
  10.5 11.3 %collective-permute-start.5 = (f32[16,16,256]{2,1,0:T(8,128)S(1)}, f32[16,16,256]{2,1,0:T(8,128)S(1)}, u32[]{:S(2)}, u32[]{:S(2)}) collective-permute-start(f32[16,16,256]{2,1,0:T(8,128)S(1)} %shard_map.91.refs_0_), channel_id=1, source_target_pairs={{0,2},{2,0},{1,3},{3,1},{4,6},{6,4},{5,7},{7,5},{8,10},{10,8},{9,1... | collective-permute-start | bytes 786440 | tf_op jit(solution)/shard_map/ppermute | solution.py:324
  21.8 11.4 %collective-permute-start.2 = (f32[16,16,256]{2,1,0:T(8,128)S(1)}, f32[16,16,256]{2,1,0:T(8,128)S(1)}, u32[]{:S(2)}, u32[]{:S(2)}) collective-permute-start(f32[16,16,256]{2,1,0:T(8,128)S(1)} %shard_map.91.refs_0_), channel_id=1, source_target_pairs={{0,1},{1,0},{2,3},{3,2},{4,5},{5,4},{6,7},{7,6},{8,9},{9,8},{10,11... | collective-permute-start | bytes 786440 | tf_op jit(solution)/shard_map/ppermute | solution.py:326
  21.8 11.4 %collective-permute-start.8 = (f32[16,16,256]{2,1,0:T(8,128)S(1)}, f32[16,16,256]{2,1,0:T(8,128)S(1)}, u32[]{:S(2)}, u32[]{:S(2)}) collective-permute-start(f32[16,16,256]{2,1,0:T(8,128)S(1)} %collective-permute-done.5.refs_6_), channel_id=1, source_target_pairs={{0,1},{1,0},{2,3},{3,2},{4,5},{5,4},{6,7},{7,6},{8,9},{9,8},{10,11... | collective-permute-start | bytes 786440 | tf_op jit(solution)/shard_map/ppermute | solution.py:326
  32.5 28.8 %collective-permute-start.15 = (s32[2,129]{1,0:T(2,128)}, s32[2,129]{1,0:T(2,128)}, u32[]{:S(2)}, u32[]{:S(2)}) collective-permute-start(s32[2,129]{1,0:T(2,128)} %pad_add_fusion.1), channel_id=1, source_target_pairs={{0,2},{2,0},{1,3},{3,1},{4,6},{6,4},{5,7},{7,5},{8,10},{10,8},{9,1... | collective-permute-start | bytes 3104 | tf_op jit(solution)/shard_map/ppermute | solution.py:276
  38.3 12.7 %collective-permute-start.22 = (f32[16,8,256]{2,1,0:T(8,128)}, f32[16,8,256]{2,1,0:T(8,128)}, u32[]{:S(2)}, u32[]{:S(2)}) collective-permute-start(f32[16,8,256]{2,1,0:T(8,128)} %bitcast.19), channel_id=1, source_target_pairs={{0,2},{2,0},{1,3},{3,1},{4,6},{6,4},{5,7},{7,5},{8,10},{10,8},{9,1... | collective-permute-start | bytes 393224 | tf_op jit(solution)/shard_map/ppermute | solution.py:360
  42.7 15.6 %collective-permute-start.18 = (f32[16,16,256]{2,1,0:T(8,128)}, f32[16,16,256]{2,1,0:T(8,128)}, u32[]{:S(2)}, u32[]{:S(2)}) collective-permute-start(f32[16,16,256]{2,1,0:T(8,128)} %bitcast.17), channel_id=1, source_target_pairs={{0,2},{2,0},{1,3},{3,1},{4,6},{6,4},{5,7},{7,5},{8,10},{10,8},{9,1... | collective-permute-start | bytes 786440 | tf_op jit(solution)/shard_map/ppermute | solution.py:360
  57.1 43.7 %collective-permute-start.16 = (f32[64,16,128]{2,1,0:T(8,128)S(1)}, f32[64,16,128]{2,1,0:T(8,128)S(1)}, u32[]{:S(2)}, u32[]{:S(2)}) collective-permute-start(f32[64,16,128]{2,1,0:T(8,128)S(1)} %get-tuple-element.168), channel_id=1, source_target_pairs={{0,2},{1,3},{2,0},{3,1},{4,6},{5,7},{6,4},{7,5},{8,10},{9,11},{10,... | collective-permute-start | bytes 1572872 | tf_op jit(solution)/shard_map/ppermute | solution.py:377
  58.3 43.0 %collective-permute-start.17 = (f32[64,16,128]{2,1,0:T(8,128)S(1)}, f32[64,16,128]{2,1,0:T(8,128)S(1)}, u32[]{:S(2)}, u32[]{:S(2)}) collective-permute-start(f32[64,16,128]{2,1,0:T(8,128)S(1)} %get-tuple-element.167), channel_id=1, source_target_pairs={{0,3},{1,2},{2,1},{3,0},{4,7},{5,6},{6,5},{7,4},{8,11},{9,10},{10,... | collective-permute-start | bytes 1572872 | tf_op jit(solution)/shard_map/ppermute | solution.py:377
  63.7 15.5 %collective-permute-start.21 = (f32[8,16,256]{2,1,0:T(8,128)S(1)}, f32[8,16,256]{2,1,0:T(8,128)S(1)}, u32[]{:S(2)}, u32[]{:S(2)}) collective-permute-start(f32[8,16,256]{2,1,0:T(8,128)S(1)} %get-tuple-element.118), channel_id=1, source_target_pairs={{0,12},{4,8},{8,4},{12,0},{1,13},{5,9},{9,5},{13,1},{2,14},{6,10},... | collective-permute-start | bytes 393224 | tf_op jit(solution)/shard_map/ppermute | solution.py:408
  69.5 11.9 %collective-permute-start.24 = (f32[8,8,256]{2,1,0:T(8,128)S(1)}, f32[8,8,256]{2,1,0:T(8,128)S(1)}, u32[]{:S(2)}, u32[]{:S(2)}) collective-permute-start(f32[8,8,256]{2,1,0:T(8,128)S(1)} %copy-done.54), channel_id=1, source_target_pairs={{0,8},{4,12},{8,0},{12,4},{1,9},{5,13},{9,1},{13,5},{2,10},{6,14},... | collective-permute-start | bytes 196616 | tf_op jit(solution)/shard_map/ppermute | solution.py:408
  69.9 13.5 %collective-permute-start.25 = (f32[8,8,256]{2,1,0:T(8,128)S(1)}, f32[8,8,256]{2,1,0:T(8,128)S(1)}, u32[]{:S(2)}, u32[]{:S(2)}) collective-permute-start(f32[8,8,256]{2,1,0:T(8,128)S(1)} %copy-done.52), channel_id=1, source_target_pairs={{0,12},{4,8},{8,4},{12,0},{1,13},{5,9},{9,5},{13,1},{2,14},{6,10},... | collective-permute-start | bytes 196616 | tf_op jit(solution)/shard_map/ppermute | solution.py:408
  83.4 13.0 %collective-permute-start.29 = (f32[16,16,256]{2,1,0:T(8,128)S(1)}, f32[16,16,256]{2,1,0:T(8,128)S(1)}, u32[]{:S(2)}, u32[]{:S(2)}) collective-permute-start(f32[16,16,256]{2,1,0:T(8,128)S(1)} %get-tuple-element.119.refs_0_), channel_id=1, source_target_pairs={{0,2},{2,0},{1,3},{3,1},{4,6},{6,4},{5,7},{7,5},{8,10},{10,8},{9,1... | collective-permute-start | bytes 786440 | tf_op jit(solution)/shard_map/ppermute | solution.py:324
  108.2 13.5 %collective-permute-start.40 = (f32[8,16,256]{2,1,0:T(8,128)S(1)}, f32[8,16,256]{2,1,0:T(8,128)S(1)}, u32[]{:S(2)}, u32[]{:S(2)}) collective-permute-start(f32[8,16,256]{2,1,0:T(8,128)S(1)} %get-tuple-element.139), channel_id=1, source_target_pairs={{0,8},{4,12},{8,0},{12,4},{1,9},{5,13},{9,1},{13,5},{2,10},{6,14},... | collective-permute-start | bytes 393224 | tf_op jit(solution)/shard_map/ppermute | solution.py:408
  112.9 14.2 %collective-permute-start.42 = (f32[16,8,256]{2,1,0:T(8,128)S(1)}, f32[16,8,256]{2,1,0:T(8,128)S(1)}, u32[]{:S(2)}, u32[]{:S(2)}) collective-permute-start(f32[16,8,256]{2,1,0:T(8,128)S(1)} %bitcast.65), channel_id=1, source_target_pairs={{0,2},{2,0},{1,3},{3,1},{4,6},{6,4},{5,7},{7,5},{8,10},{10,8},{9,1... | collective-permute-start | bytes 393224 | tf_op jit(solution)/shard_map/ppermute | solution.py:360
  123.8 24.6 %collective-permute-start.49 = (f32[16,16,256]{2,1,0:T(8,128)S(1)}, f32[16,16,256]{2,1,0:T(8,128)S(1)}, u32[]{:S(2)}, u32[]{:S(2)}) collective-permute-start(f32[16,16,256]{2,1,0:T(8,128)S(1)} %get-tuple-element.141.refs_0_), channel_id=1, source_target_pairs={{0,2},{2,0},{1,3},{3,1},{4,6},{6,4},{5,7},{7,5},{8,10},{10,8},{9,1... | collective-permute-start | bytes 786440 | tf_op jit(solution)/shard_map/ppermute | solution.py:324
  140.6 11.3 %collective-permute-start.46 = (f32[16,16,256]{2,1,0:T(8,128)S(1)}, f32[16,16,256]{2,1,0:T(8,128)S(1)}, u32[]{:S(2)}, u32[]{:S(2)}) collective-permute-start(f32[16,16,256]{2,1,0:T(8,128)S(1)} %get-tuple-element.141.refs_0_), channel_id=1, source_target_pairs={{0,1},{1,0},{2,3},{3,2},{4,5},{5,4},{6,7},{7,6},{8,9},{9,8},{10,11... | collective-permute-start | bytes 786440 | tf_op jit(solution)/shard_map/ppermute | solution.py:326
  159.5 14.4 %collective-permute-start.64 = (f32[8,16,256]{2,1,0:T(8,128)S(1)}, f32[8,16,256]{2,1,0:T(8,128)S(1)}, u32[]{:S(2)}, u32[]{:S(2)}) collective-permute-start(f32[8,16,256]{2,1,0:T(8,128)S(1)} %get-tuple-element.163), channel_id=1, source_target_pairs={{0,8},{4,12},{8,0},{12,4},{1,9},{5,13},{9,1},{13,5},{2,10},{6,14},... | collective-permute-start | bytes 393224 | tf_op jit(solution)/shard_map/ppermute | solution.py:408
  161.9 12.0 %collective-permute-start.65 = (f32[8,16,256]{2,1,0:T(8,128)S(1)}, f32[8,16,256]{2,1,0:T(8,128)S(1)}, u32[]{:S(2)}, u32[]{:S(2)}) collective-permute-start(f32[8,16,256]{2,1,0:T(8,128)S(1)} %get-tuple-element.164), channel_id=1, source_target_pairs={{0,12},{4,8},{8,4},{12,0},{1,13},{5,9},{9,5},{13,1},{2,14},{6,10},... | collective-permute-start | bytes 393224 | tf_op jit(solution)/shard_map/ppermute | solution.py:408
  164.0 15.0 %collective-permute-start.60 = (f32[8,8,256]{2,1,0:T(8,128)S(1)}, f32[8,8,256]{2,1,0:T(8,128)S(1)}, u32[]{:S(2)}, u32[]{:S(2)}) collective-permute-start(f32[8,8,256]{2,1,0:T(8,128)S(1)} %get-tuple-element.157), channel_id=1, source_target_pairs={{0,4},{4,0},{8,12},{12,8},{1,5},{5,1},{9,13},{13,9},{2,6},{6,2},{1... | collective-permute-start | bytes 196616 | tf_op jit(solution)/shard_map/ppermute | solution.py:408
  164.8 18.1 %collective-permute-start.61 = (f32[8,8,256]{2,1,0:T(8,128)S(1)}, f32[8,8,256]{2,1,0:T(8,128)S(1)}, u32[]{:S(2)}, u32[]{:S(2)}) collective-permute-start(f32[8,8,256]{2,1,0:T(8,128)S(1)} %get-tuple-element.158), channel_id=1, source_target_pairs={{0,8},{4,12},{8,0},{12,4},{1,9},{5,13},{9,1},{13,5},{2,10},{6,14},... | collective-permute-start | bytes 196616 | tf_op jit(solution)/shard_map/ppermute | solution.py:408
  168.8 14.2 %collective-permute-start.62 = (f32[8,8,256]{2,1,0:T(8,128)S(1)}, f32[8,8,256]{2,1,0:T(8,128)S(1)}, u32[]{:S(2)}, u32[]{:S(2)}) collective-permute-start(f32[8,8,256]{2,1,0:T(8,128)S(1)} %get-tuple-element.159), channel_id=1, source_target_pairs={{0,12},{4,8},{8,4},{12,0},{1,13},{5,9},{9,5},{13,1},{2,14},{6,10},... | collective-permute-start | bytes 196616 | tf_op jit(solution)/shard_map/ppermute | solution.py:408
  (105 other events, 926.9 us)

commit v2 on v1

--- a/solution.py
+++ b/solution.py
@@ -14,6 +14,7 @@
 SMEM = pl.BlockSpec(memory_space=pltpu.SMEM)
 VMEM = pl.BlockSpec(memory_space=pltpu.VMEM)
 ANY = pl.BlockSpec(memory_space=pl.ANY)
+HBM = pl.BlockSpec(memory_space=pltpu.HBM)
 
 
 def split(v):
@@ -26,8 +27,10 @@
 
 
 def dot3(a, high, low):
+    rows = a.shape[0]
     a_high, a_low = split(a)
-    return dot(a_high, high) + (dot(a_low, high) + dot(a_high, low))
+    both = dot(jnp.concatenate([a_high, a_low], axis=0), high)
+    return both[:rows] + (both[rows:] + dot(a_high, low))
 
 
 def call(kernel, outs, ins, mib, out_specs=None, scratch=(), flops=0, moved=0, alias=None, grid=()):
@@ -70,8 +73,7 @@
 def cells_kernel(sizes, ids, pats, live, mine, theirs, *refs):
     trips, subs, share, chunks, clusters = sizes
     outs, (buf, acc, sems) = refs[:-3], refs[-3:]
-    n = len(chunks)
-    rem_hi, rem_lo, loc_hi, loc_lo = (outs[i * n : (i + 1) * n] for i in range(4))
+    rem, own = outs[: len(chunks)], outs[len(chunks) :]
     x, s = ids[0], ids[1]
     slots, _, width = mine.shape
     copies = {}
@@ -94,12 +96,9 @@
             block = clusters * rc
             for d in range(trips):
                 high, low = split(acc[q, d, :, off : off + rc, :].reshape(block, width))
-                if d:
-                    rem_hi[r][(d - 1) * block : d * block, lanes] = high
-                    rem_lo[r][(d - 1) * block : d * block, lanes] = low
-                else:
-                    loc_hi[r][:, lanes] = high
-                    loc_lo[r][:, lanes] = low
+                ref, at, lows = (rem[r], (d - 1) * block, (trips - 1) * block) if d else (own[r], 0, block)
+                ref[at : at + block, lanes] = high
+                ref[lows + at : lows + at + block, lanes] = low
         return c
 
     lax.fori_loop(0, clusters, finish, 0)
@@ -107,7 +106,7 @@
 
 def early_kernel(sizes, ids, pats, live, mine, theirs, *refs):
     subs, share, off, rc, clusters = sizes
-    far, (out_hi, out_lo, buf, acc, sems) = refs[:-5], refs[-5:]
+    far, (out, buf, acc, sems) = refs[:-4], refs[-4:]
     slots, _, width = mine.shape
     start = pl.multiple_of((ids[0] * subs + ids[1]) * share + off, rc)
     copies = []
@@ -124,19 +123,26 @@
     def finish(q, c):
         lanes = pl.ds(pl.multiple_of(q * width, width), width)
         high, low = split(acc[q, 0].reshape(clusters * rc, width))
-        out_hi[:, lanes] = high
-        out_lo[:, lanes] = low
+        out[: clusters * rc, lanes] = high
+        out[clusters * rc :, lanes] = low
         return c
 
     lax.fori_loop(0, clusters, finish, 0)
 
 
-def terms(c_hi, c_lo, x_hi, x_lo):
-    return dot(c_hi[...], x_hi[...]) + (dot(c_lo[...], x_hi[...]) + dot(c_hi[...], x_lo[...]))
-
-
-def terms_kernel(c_hi, c_lo, x_hi, x_lo, out):
-    out[...] = terms(c_hi, c_lo, x_hi, x_lo)
+def terms(cells, x_hi, x_lo):
+    rows = cells.shape[0] // 2
+    both = dot(cells[...], x_hi[...])
+    return both[:rows] + (both[rows:] + dot(cells[:rows], x_lo[...]))
+
+
+def terms_kernel(x_hi, x_lo, *refs):
+    cells, out = refs[:-1], refs[-1]
+    at = 0
+    for ref in cells:
+        rows = ref.shape[0] // 2
+        out[at : at + rows] = terms(ref, x_hi, x_lo)
+        at += rows
 
 
 def pack(agg, send_src, cap, packs):
@@ -145,7 +151,7 @@
             ref[j] = agg[send_src[(k + 1) * cap + j]]
 
 
-def gather_kernel(sizes, places, whole, ids, send_src, c_hi, c_lo, *refs):
+def gather_kernel(sizes, places, whole, ids, send_src, cells, *refs):
     trips, subs, share, n, clusters, rows, cap = sizes
     count = len(places) * n
     pieces, (x_hi, x_lo, *outs) = refs[:count], refs[count:]
@@ -158,7 +164,7 @@
             spot = pl.ds(pl.multiple_of(q * rows + at, share), share)
             x_hi[spot, :] = high
             x_lo[spot, :] = low
-    out = terms(c_hi, c_lo, x_hi, x_lo)
+    out = terms(cells, x_hi, x_lo)
     if whole:
         agg, *packs = outs
         agg[...] = out.reshape(agg.shape)
@@ -168,21 +174,26 @@
 
 
 def pack_kernel(cap, arrivals, send_src, local, *refs):
-    got, agg, packs = refs[:arrivals], refs[arrivals], refs[arrivals + 1 :]
-    total = local[...]
-    for ref in got:
-        total = total + ref[...]
-    agg[...] = total
-    pack(agg, send_src, cap, packs)
-
-
-def rows_kernel(sizes, last, alias, recv_pos, counts, ids, *refs):
+    got, outs = refs[:arrivals], refs[arrivals:]
+    count = local.shape[0]
+    each = len(outs) // count
+    for i in range(count):
+        agg, packs = outs[i * each], outs[i * each + 1 : (i + 1) * each]
+        total = local[i]
+        for ref in got:
+            total = total + ref[i]
+        agg[...] = total
+        pack(agg, send_src, cap, packs)
+
+
+def rows_kernel(sizes, last, unread, recv_pos, counts, ids, *refs):
     clusters, rc, cap, steps, first_row = sizes
+    refs = refs[unread:]
     feat, agg, refs = refs[0], refs[1], refs[2:]
     got, refs = refs[:steps], refs[steps:]
     up_hi, up_lo, dense_hi, dense_lo, refs = *refs[:4], refs[4:]
     if last:
-        out, held, both = refs[1:] if alias else refs
+        out, held, both = refs
     else:
         down, (out, low_out, held, both) = refs[:2], refs[2:]
     for k, ref in enumerate(got):
@@ -207,10 +218,21 @@
         out[c] = jnp.where(row < counts[c], low[c * rc : (c + 1) * rc, :], 0.0)
 
 
-def down_kernel(first_row, counts, ids, feat, down, out):
-    high, low = split(down[...])
-    block = out.shape[0] * out.shape[1]
-    lower(feat[...].reshape(block, -1), high, low, counts, ids, first_row, out)
+def down_kernel(chunks, counts, ids, feat, down, *refs):
+    outs, (rows, weight, sems) = refs[:-3], refs[-3:]
+    start, size = chunks[0][0], rows.shape[1]
+    copies = [
+        pltpu.make_async_copy(feat.at[:, start : start + size, :], rows, sems.at[0]),
+        pltpu.make_async_copy(down.at[0], weight, sems.at[1]),
+    ]
+    for copy in copies:
+        copy.start()
+    copies[1].wait()
+    high, low = split(weight[...])
+    copies[0].wait()
+    for (off, rc), out in zip(chunks, outs):
+        part = rows[:, off - start : off - start + rc, :].reshape(out.shape[0] * rc, -1)
+        lower(part, high, low, counts, ids, off, out)
 
 
 def local(
@@ -231,7 +253,7 @@
     rows = trips * subs * share
     cap = 2 * ((clusters // 2 + edges // 2 - 1) // (edges // 2))
     half_share = share // 2
-    chunks = [(0, half_share)] + [(half_share + i, 8) for i in range(0, half_share, 8)]
+    chunks = [(0, half_share), (half_share, half_share)]
     n = len(chunks)
     depth = clusters * rows
     slots = patterns.shape[2]
@@ -250,32 +272,26 @@
     def big(rc):
         return jax.ShapeDtypeStruct((clusters, rc, feat_width), F32)
 
-    lows = [
-        call(
-            functools.partial(down_kernel, off),
-            small(rc),
-            [
-                SMEM,
-                SMEM,
-                rows_of(clusters, off, rc, feat_width),
-                pl.BlockSpec((None, feat_width, width), lambda i: (0, 0, 0)),
+    lows = []
+    for group in ([0], list(range(1, n))):
+        lows += call(
+            functools.partial(down_kernel, [chunks[r] for r in group]),
+            [small(chunks[r][1]) for r in group],
+            [SMEM, SMEM, HBM, HBM],
+            60,
+            flops=6 * clusters * half_share * feat_width * width,
+            scratch=[
+                pltpu.VMEM((clusters, half_share, feat_width), F32),
+                pltpu.VMEM((feat_width, width), F32),
+                pltpu.SemaphoreType.DMA((2,)),
             ],
-            16,
-            flops=6 * clusters * rc * feat_width * width,
-            grid=(1,),
-            out_specs=pl.BlockSpec((clusters, rc, width), lambda i: (0, 0, 0)),
         )(edge_counts, ids, edge_feat, down_weight)
-        for off, rc in chunks
-    ]
     (down_weight, up_weight, dense_weight, reverse, patterns, trip_count, *lows) = lax.optimization_barrier(
         (down_weight, up_weight, dense_weight, reverse, patterns, trip_count, *lows)
     )
 
     note = jnp.concatenate([patterns.reshape(-1), trip_count.reshape(-1)])
     note = jnp.stack([note, lax.ppermute(note, "sub", swap)])
-    notes = jnp.concatenate([note] + [lax.ppermute(note, "trip", turn(d)) for d in range(1, trips)])
-    pats, live = notes[:, :-1], notes[:, -1]
-
     here = jnp.arange(clusters, dtype=jnp.int32)
     mine = lax.dynamic_slice_in_dim(reverse, e * clusters, clusters)
     to = mine // clusters
@@ -301,18 +317,18 @@
 
     cells = call(
         functools.partial(cells_kernel, (trips, subs, share, chunks, clusters)),
-        [jax.ShapeDtypeStruct(((trips - 1) * clusters * rc, depth), BF16) for _, rc in chunks] * 2
-        + [jax.ShapeDtypeStruct((clusters * rc, depth), BF16) for _, rc in chunks] * 2,
-        [SMEM, SMEM, SMEM, ANY, ANY],
-        40,
+        [jax.ShapeDtypeStruct((2 * (trips - 1) * clusters * rc, depth), BF16) for _, rc in chunks]
+        + [jax.ShapeDtypeStruct((2 * clusters * rc, depth), BF16) for _, rc in chunks],
+        [SMEM, SMEM, SMEM, HBM, HBM],
+        58,
         scratch=[
             pltpu.VMEM((2, trips, slots, share, rows), F32),
             pltpu.VMEM((clusters, trips, clusters, share, rows), F32),
             pltpu.SemaphoreType.DMA((2, trips)),
         ],
         moved=12 << 20,
-    )(ids, pats[:2], live[:2], coef, coef2)
-    rem_hi, rem_lo, loc_hi, loc_lo = (cells[i * n : (i + 1) * n] for i in range(4))
+    )(ids, note[:, :-1], note[:, -1], coef, coef2)
+    cells = list(cells)
 
     feats, first = None, None
     for layer in range(layers):
@@ -322,63 +338,68 @@
         for r in range(n):
             for d in range(trips):
                 far = lax.ppermute(lows[r], "trip", turn(d)) if d else lows[r]
+                if layer == 0 and d:
+                    far, cells[0] = lax.optimization_barrier((far, cells[0]))
                 pieces[d, 0, r] = far
                 pieces[d, 1, r] = lax.ppermute(far, "sub", swap)
         inputs = [pieces[d, other, r] for d, other in places for r in range(n)]
+        remote, near = cells[:n], cells[n:]
         whole = layer > 0
-        order = list(range(n)) if whole else [1, 0, *range(2, n)]
-        lead = order[0]
-        lead_rc = chunks[lead][1]
-        c_hi, c_lo = first if whole else (rem_hi[lead], rem_lo[lead])
+        groups = [list(range(1, n))] if whole else [[1], [0], *[[r] for r in range(2, n)]]
+        order = [0] * whole + [r for group in groups for r in group]
+        lead_rc = chunks[order[0]][1]
+        lead = first if whole else remote[order[0]]
         if whole:
             outs = [small(lead_rc)] + [jax.ShapeDtypeStruct((cap, lead_rc, width), F32)] * (edges - 1)
         else:
-            outs = [jax.ShapeDtypeStruct(((trips - 1) * clusters * lead_rc, width), F32)]
+            outs = [jax.ShapeDtypeStruct((lead.shape[0] // 2, width), F32)]
         x_hi, x_lo, *outs = call(
             functools.partial(gather_kernel, (trips, subs, share, n, clusters, rows, cap), places, whole),
             [jax.ShapeDtypeStruct((depth, width), BF16)] * 2 + outs,
-            [SMEM, SMEM, VMEM, VMEM] + [VMEM] * len(inputs),
+            [SMEM, SMEM, VMEM] + [VMEM] * len(inputs),
             32,
-            flops=6 * c_hi.shape[0] * depth * width,
-        )(ids, send_src, c_hi, c_lo, *inputs)
-
-        def product(high, low, x_hi=x_hi, x_lo=x_lo):
+            flops=3 * lead.shape[0] * depth * width,
+        )(ids, send_src, lead, *inputs)
+
+        def product(group, x_hi=x_hi, x_lo=x_lo):
+            size = sum(c.shape[0] // 2 for c in group)
             return call(
                 terms_kernel,
-                jax.ShapeDtypeStruct((high.shape[0], width), F32),
-                [VMEM] * 4,
+                jax.ShapeDtypeStruct((size, width), F32),
+                [VMEM] * (2 + len(group)),
                 32,
-                flops=6 * high.shape[0] * depth * width,
-            )(high, low, x_hi, x_lo)
-
-        summed = order[1:] if whole else order
-        sent = {r: outs[0] if r == lead and not whole else product(rem_hi[r], rem_lo[r]) for r in summed}
-        got = {}
-        for r in summed:
-            block = clusters * chunks[r][1]
-            got[r] = [
-                lax.ppermute(
-                    sent[r][(d - 1) * block : d * block].reshape(clusters, -1, width), "trip", turn(d)
-                )
-                for d in range(1, trips)
-            ]
+                flops=6 * size * depth * width,
+            )(x_hi, x_lo, *group)
+
+        aggs, packs = {}, {}
+        if whole:
+            aggs[0], *packs[0] = outs
+        sums = []
+        for i, group in enumerate(groups):
+            rc = chunks[group[0]][1]
+            sent = outs[0] if not whole and i == 0 else product([remote[r] for r in group])
+            sent = sent.reshape(len(group), trips - 1, clusters, rc, width)
+            sums.append([lax.ppermute(sent[:, d - 1], "trip", turn(d)) for d in range(1, trips)])
         if layer == 0:
             off, rc = chunks[0]
-            base, got[summed[-1]] = lax.optimization_barrier((ids, got[summed[-1]]))
+            base, sums[-1] = lax.optimization_barrier((ids, sums[-1]))
+            marks = jnp.pad(note[0].astype(F32), (0, rc * rows - note.shape[1])).reshape(1, rc, rows)
             far = []
             for d in range(1, trips):
                 for other in range(2):
                     core = 1 - base[1] if other else base[1]
                     start = (lax.rem(base[0] + d, trips) * subs + core) * share + off
-                    part = lax.dynamic_slice_in_dim(coef, start, rc, 1)
+                    part = jnp.concatenate([lax.dynamic_slice_in_dim(coef, start, rc, 1), marks])
                     perm = [
                         (i * subs + j, (i + d) % trips * subs + (j ^ other)) for i in range(trips) for j in range(subs)
                     ]
                     far.append(lax.ppermute(part, ("trip", "sub"), perm))
+            notes = jnp.stack([part[slots].reshape(-1)[: note.shape[1]].astype(jnp.int32) for part in far])
+            notes = jnp.concatenate([note, notes])
             first = call(
                 functools.partial(early_kernel, (subs, share, off, rc, clusters)),
-                [jax.ShapeDtypeStruct((clusters * rc, depth), BF16)] * 2,
-                [SMEM, SMEM, SMEM, ANY, ANY] + [VMEM] * len(far),
+                jax.ShapeDtypeStruct((2 * clusters * rc, depth), BF16),
+                [SMEM, SMEM, SMEM, HBM, HBM] + [VMEM] * len(far),
                 40,
                 scratch=[
                     pltpu.VMEM((2, slots, rc, rows), F32),
@@ -386,41 +407,46 @@
                     pltpu.SemaphoreType.DMA((2,)),
                 ],
                 moved=6 << 20,
-            )(ids, pats, live, coef, coef2, *far)
+            )(ids, notes[:, :-1], notes[:, -1], coef, coef2, *far)
+        for group, got in zip(groups, sums):
+            rc = chunks[group[0]][1]
+            own = product([near[r] for r in group]).reshape(len(group), clusters, rc, width)
+            packed = call(
+                functools.partial(pack_kernel, cap, trips - 1),
+                ([small(rc)] + [jax.ShapeDtypeStruct((cap, rc, width), F32)] * (edges - 1)) * len(group),
+                [SMEM] + [VMEM] * trips,
+                16,
+                moved=4 << 20,
+            )(send_src, own, *got)
+            for i, r in enumerate(group):
+                aggs[r], *packs[r] = packed[i * edges : (i + 1) * edges]
         next_feats, next_lows = [None] * n, [None] * n
         result = None
-        for r in order:
+        for i, r in enumerate(order):
             off, rc = chunks[r]
-            block = clusters * rc
-            if r in summed:
-                own = product(loc_hi[r], loc_lo[r]).reshape(clusters, rc, width)
-                agg, *packs = call(
-                    functools.partial(pack_kernel, cap, trips - 1),
-                    [small(rc)] + [jax.ShapeDtypeStruct((cap, rc, width), F32)] * (edges - 1),
-                    [SMEM] + [VMEM] * trips,
-                    16,
-                    moved=4 << 20,
-                )(send_src, own, *got[r])
-            else:
-                agg, *packs = outs
             back = [None] * (edges - 1)
             for k in range(edges - 1, 0, -1):
-                back[k - 1] = lax.ppermute(packs[k - 1], "edge", [(i, i ^ k) for i in range(edges)])
-            alias = last and result is not None
+                back[k - 1] = lax.ppermute(packs[r][k - 1], "edge", [(i, i ^ k) for i in range(edges)])
             feat, feat_spec = (
                 (edge_feat, rows_of(clusters, off, rc, feat_width))
                 if layer == 0
                 else (feats[r], pl.BlockSpec((clusters, rc, feat_width), lambda i: (0, 0, 0)))
             )
-            extra = ([result] if alias else []) if last else list(down[layer])
-            before_extra = 3 + 2 + (edges - 1) + 4
+            ahead = [packs[later][0] for later in order[i + 1 :]]
+            if layer == 0 and i == n - 1:
+                ahead.append(first)
+            alias = {}
+            if last and result is not None:
+                alias = {3 + len(ahead): 0}
+                ahead.append(result)
+            extra = [] if last else down[layer]
             result = call(
-                functools.partial(rows_kernel, (clusters, rc, cap, edges - 1, off), last, alias),
+                functools.partial(rows_kernel, (clusters, rc, cap, edges - 1, off), last, len(ahead)),
                 big(share) if last else [big(rc), small(rc)],
                 [SMEM] * 3
+                + [ANY] * len(ahead)
                 + [feat_spec]
-                + [VMEM] * (1 + edges - 1 + 4)
-                + ([ANY] * len(extra) if last else [VMEM] * len(extra)),
+                + [VMEM] * (1 + edges - 1 + 4 + len(extra)),
                 32,
                 grid=(1,),
                 out_specs=rows_of(clusters, off, rc, feat_width) if last else [VMEM, VMEM],
@@ -428,9 +454,9 @@
                     pltpu.VMEM(((edges - 1) * cap, rc, width), F32),
                     pltpu.VMEM((clusters, rc, width), F32),
                 ],
-                flops=6 * block * feat_width * (2 * width + feat_width),
-                alias={before_extra: 0} if alias else None,
-            )(recv_pos, edge_counts, ids, feat, agg, *back, *up[layer], *dense[layer], *extra)
+                flops=6 * clusters * rc * feat_width * (2 * width + feat_width),
+                alias=alias,
+            )(recv_pos, edge_counts, ids, *ahead, feat, aggs[r], *back, *up[layer], *dense[layer], *extra)
             if not last:
                 next_feats[r], next_lows[r] = result
         feats, lows = next_feats, next_lows

time: 187 us -> 161 us (0.86)
  starting transfers between devices: 78.2 us -> 50.4 us
  waiting for transfers between devices: 34.9 us -> 50.3 us
  local copies, waits for them, and re-layouts: 13.4 us -> 5.31 us
  other arithmetic: 7.1 us -> 4.72 us
  Pallas kernels: 49.6 us -> 47.3 us
    ppermute x35 -> x22, starting transfers between devices: 60.7 us -> 38.7 us  [the longest x18 34.2 us: local(): lax.ppermute(packs[r][k - 1], 'edge', [(i, i ^ k) for i in range(edges)])]
    ppermute x35 -> x22, waiting for transfers between devices: 21.6 us -> 34 us  [the longest x18 28.7 us: local(): lax.ppermute(packs[r][k - 1], 'edge', [(i, i ^ k) for i in range(edges)])]
    unnamed x126 -> x40, local copies, waits for them, and re-layouts: 10.9 us -> 2.96 us
    ppermute x9 -> x6, starting transfers between devices: 12.5 us -> 7.9 us  [local(): far = lax.ppermute(lows[r], 'trip', turn(d)) if d else lows[r]]
    pallas_call x9 -> x6, Pallas kernels: 16.5 us -> 13 us  [local(): call(functools.partial(rows_kernel, (clusters, rc, cap, edges - 1, off),...]
    ppermute x18 -> x12, waiting for transfers between devices: 1.37 us -> 4.39 us  [local(): pieces[d, 1, r] = lax.ppermute(far, 'sub', swap)]
    pallas_call x1, Pallas kernels: 6.47 us -> 9.03 us  [local(): call(functools.partial(cells_kernel, (trips, subs, share, chunks, cluster...]
    concatenate x3 -> x2, other arithmetic: 2.64 us -> 0.09 us  [the longest x1 0.07 us: local(): jnp.concatenate([lax.dynamic_slice_in_dim(coef, start, rc, 1), marks])]
  transfers between devices with their start and end apart: 66 -> 44, of which waited for: 14 -> 16; matrix products, arithmetic and copies ran while one was open for 5% -> 4% of each run, Pallas kernels for 23% -> 22%
where the time goes in v2:
time: 161 us
  starting transfers between devices  50.4 us (31%)
  waiting for transfers between devices  50.3 us (31%)
  Pallas kernels  47.3 us (29%)
  local copies, waits for them, and re-layouts  5.31 us (3%)
  other arithmetic  4.72 us (3%)
  between operations  2.94 us (2%)
    ppermute x18, starting transfers between devices, local(): lax.ppermute(packs[r][k - 1], 'edge', [(i, i ^ k) for i in range(edges)])  34.2 us
    ppermute x18, waiting for transfers between devices, local(): lax.ppermute(packs[r][k - 1], 'edge', [(i, i ^ k) for i in range(edges)])  28.7 us
    pallas_call x6, Pallas kernels, local(): call(functools.partial(rows_kernel, (clusters, rc, cap, edges - 1, off),...  13 us
    ppermute x6, waiting for transfers between devices, local(): far = lax.ppermute(lows[r], 'trip', turn(d)) if d else lows[r]  10.4 us
    pallas_call x1, Pallas kernels, local(): call(functools.partial(cells_kernel, (trips, subs, share, chunks, cluster...  9.03 us
    ppermute x6, starting transfers between devices, local(): far = lax.ppermute(lows[r], 'trip', turn(d)) if d else lows[r]  7.9 us
    pallas_call x7, Pallas kernels, product(): call(terms_kernel, jax.ShapeDtypeStruct((size, width), F32), [VMEM] * (2...  6.9 us
    pallas_call x3, Pallas kernels, local(): call(functools.partial(gather_kernel, (trips, subs, share, n, clusters, r...  6.25 us
  transfers between devices with their start and end apart: 44, of which 16 were waited for; matrix products, arithmetic and copies ran while one was open for 4% of the time, Pallas kernels for 22%

profile of v2, /device:TPU:0, one launch (start us, length us, event | category | flops | bytes accessed | tf_op | source)
XLA Modules:
  0.0 161.1 jit_solution(14236427297666815685)
XLA Ops:
  1.1 3.0 %shard_map.91.refs_0_ = f32[16,16,256]{2,1,0:T(8,128)} custom-call(s32[16]{0:T(128)} %counts.15, s32[3]{0:T(128)} %pad_add_fusion.3.ids, f32[16,32,512]{2,1,0:T(8,128)} %refs_1_.3, f32[3,512,256]{2,1,0:T(8,128)} %down.3), custom_call_target="tpu_custom_call" | custom-call | flops 201326592 | tf_op jit(solution)/shard_map/pallas_call | solution.py:277
  4.2 3.2 %shard_map.92.refs_1_ = f32[16,16,256]{2,1,0:T(8,128)} custom-call(s32[16]{0:T(128)} %counts.15, s32[3]{0:T(128)} %pad_add_fusion.3.ids, f32[16,32,512]{2,1,0:T(8,128)} %refs_1_.3, f32[3,512,256]{2,1,0:T(8,128)} %down.3), custom_call_target="tpu_custom_call" | custom-call | flops 201326592 | tf_op jit(solution)/shard_map/pallas_call | solution.py:277
  7.5 2.9 %collective-permute-start.4 = (f32[16,16,256]{2,1,0:T(8,128)S(1)}, f32[16,16,256]{2,1,0:T(8,128)S(1)}, u32[]{:S(2)}, u32[]{:S(2)}) collective-permute-start(f32[16,16,256]{2,1,0:T(8,128)S(1)} %copy-done.11), channel_id=1, source_target_pairs={{0,2},{2,0},{1,3},{3,1},{4,6},{6,4},{5,7},{7,5},{8,10},{10,8},{9,1... | collective-permute-start | bytes 786440 | tf_op jit(solution)/shard_map/ppermute | solution.py:340
  14.0 9.0 %shard_map.93 = (bf16[512,2048]{1,0:T(8,128)(2,1)}, bf16[512,2048]{1,0:T(8,128)(2,1)}, bf16[512,2048]{1,0:T(8,128)(2,1)}, bf16[512,2048]{1,0:T(8,128)(2,1)}) custom-call(s32[3]{0:T(128)} %pad_add_fusion.3.ids, s32[2,128]{1,0:T(2,128)} %fusion.11.pats, s32[2]{0:T(128)} %fusion.12.live, f32[64,128,128]{2,1,0:T(8,128)} %bitcast.57, ...), custom_call_target="tpu_custom_call" | custom-call | bytes 12582912 | tf_op jit(solution)/shard_map/pallas_call | solution.py:318
  26.8 2.5 %shard_map.94 = (bf16[2048,256]{1,0:T(8,128)(2,1)S(1)}, bf16[2048,256]{1,0:T(8,128)(2,1)S(1)}, f32[256,256]{1,0:T(8,128)}) custom-call(s32[3]{0:T(128)S(1)} %copy-done.13, s32[32]{0:T(128)S(1)} %select_reduce_fusion.send_src, bf16[512,2048]{1,0:T(8,128)(2,1)S(1)} %copy-done.1, f32[16,16,256]{2,1,0:T(8,128)S(1)} %copy-done.11, f32[16,16,256]{2,1,0:T(8,128)S(1)} %copy-done.12, ...), custom_call_target="tpu_custom_call" | custom-call | flops 805306368 | tf_op jit(solution)/shard_map/pallas_call | solution.py:356
  34.3 5.2 %collective-permute-done.8.refs_0_ = f32[1,16,16,256]{3,2,1,0:T(8,128)S(1)} collective-permute-done((f32[1,16,16,256]{3,2,1,0:T(8,128)S(1)}, f32[1,16,16,256]{3,2,1,0:T(8,128)S(1)}, u32[]{:S(2)}, u32[]{:S(2)}) %collective-permute-start.8) | collective-permute-done | bytes 262176 | tf_op jit(solution)/shard_map/ppermute | solution.py:382
  47.3 2.5 %collective-permute-start.15 = (f32[8,16,256]{2,1,0:T(8,128)S(1)}, f32[8,16,256]{2,1,0:T(8,128)S(1)}, u32[]{:S(2)}, u32[]{:S(2)}) collective-permute-start(f32[8,16,256]{2,1,0:T(8,128)S(1)} %get-tuple-element.89), channel_id=1, source_target_pairs={{0,4},{4,0},{8,12},{12,8},{1,5},{5,1},{9,13},{13,9},{2,6},{6,2},{1... | collective-permute-start | bytes 393224 | tf_op jit(solution)/shard_map/ppermute | solution.py:429
  49.7 2.3 %collective-permute-start.16 = (f32[8,16,256]{2,1,0:T(8,128)S(1)}, f32[8,16,256]{2,1,0:T(8,128)S(1)}, u32[]{:S(2)}, u32[]{:S(2)}) collective-permute-start(f32[8,16,256]{2,1,0:T(8,128)S(1)} %get-tuple-element.90), channel_id=1, source_target_pairs={{0,8},{4,12},{8,0},{12,4},{1,9},{5,13},{9,1},{13,5},{2,10},{6,14},... | collective-permute-start | bytes 393224 | tf_op jit(solution)/shard_map/ppermute | solution.py:429
  56.3 6.4 %collective-permute-done.16.refs_4_ = f32[8,16,256]{2,1,0:T(8,128)S(1)} collective-permute-done((f32[8,16,256]{2,1,0:T(8,128)S(1)}, f32[8,16,256]{2,1,0:T(8,128)S(1)}, u32[]{:S(2)}, u32[]{:S(2)}) %collective-permute-start.16) | collective-permute-done | bytes 131104 | tf_op jit(solution)/shard_map/ppermute | solution.py:429
  69.3 3.0 %shard_map.96.refs_0_.cells = bf16[512,2048]{1,0:T(8,128)(2,1)S(1)} custom-call(s32[3]{0:T(128)S(1)} %copy-done.13, s32[4,128]{1,0:T(4,128)S(1)} %slice.80.pats, s32[4]{0:T(128)S(1)} %slice_reduce_fusion.live, f32[64,128,128]{2,1,0:T(8,128)S(1)} %bitcast.58, f32[64,128,128]{2,1,0:T(8,128)} %collective-permute-done.1.theirs, ...), custom_call_target="tpu_custom_call" | custom-call | bytes 6291456 | tf_op jit(solution)/shard_map/pallas_call | solution.py:399
  77.4 5.6 %collective-permute-done.20.refs_4_ = f32[16,16,256]{2,1,0:T(8,128)S(1)} collective-permute-done((f32[16,16,256]{2,1,0:T(8,128)S(1)}, f32[16,16,256]{2,1,0:T(8,128)S(1)}, u32[]{:S(2)}, u32[]{:S(2)}) %collective-permute-start.20) | collective-permute-done | bytes 262176 | tf_op jit(solution)/shard_map/ppermute | solution.py:340
  88.1 5.6 %collective-permute-start.25 = (f32[8,16,256]{2,1,0:T(8,128)S(1)}, f32[8,16,256]{2,1,0:T(8,128)S(1)}, u32[]{:S(2)}, u32[]{:S(2)}) collective-permute-start(f32[8,16,256]{2,1,0:T(8,128)S(1)} %get-tuple-element.98), channel_id=1, source_target_pairs={{0,4},{4,0},{8,12},{12,8},{1,5},{5,1},{9,13},{13,9},{2,6},{6,2},{1... | collective-permute-start | bytes 393224 | tf_op jit(solution)/shard_map/ppermute | solution.py:429
  93.7 2.4 %collective-permute-start.27 = (f32[8,16,256]{2,1,0:T(8,128)S(1)}, f32[8,16,256]{2,1,0:T(8,128)S(1)}, u32[]{:S(2)}, u32[]{:S(2)}) collective-permute-start(f32[8,16,256]{2,1,0:T(8,128)S(1)} %get-tuple-element.100), channel_id=1, source_target_pairs={{0,12},{4,8},{8,4},{12,0},{1,13},{5,9},{9,5},{13,1},{2,14},{6,10},... | collective-permute-start | bytes 393224 | tf_op jit(solution)/shard_map/ppermute | solution.py:429
  97.7 4.3 %collective-permute-start.28 = (f32[8,16,256]{2,1,0:T(8,128)S(1)}, f32[8,16,256]{2,1,0:T(8,128)S(1)}, u32[]{:S(2)}, u32[]{:S(2)}) collective-permute-start(f32[8,16,256]{2,1,0:T(8,128)S(1)} %get-tuple-element.95.refs_0_), channel_id=1, source_target_pairs={{0,4},{4,0},{8,12},{12,8},{1,5},{5,1},{9,13},{13,9},{2,6},{6,2},{1... | collective-permute-start | bytes 393224 | tf_op jit(solution)/shard_map/ppermute | solution.py:429
  102.0 2.4 %collective-permute-start.30 = (f32[8,16,256]{2,1,0:T(8,128)S(1)}, f32[8,16,256]{2,1,0:T(8,128)S(1)}, u32[]{:S(2)}, u32[]{:S(2)}) collective-permute-start(f32[8,16,256]{2,1,0:T(8,128)S(1)} %get-tuple-element.105), channel_id=1, source_target_pairs={{0,12},{4,8},{8,4},{12,0},{1,13},{5,9},{9,5},{13,1},{2,14},{6,10},... | collective-permute-start | bytes 393224 | tf_op jit(solution)/shard_map/ppermute | solution.py:429
  110.0 7.4 %collective-permute-done.29.refs_3_ = f32[8,16,256]{2,1,0:T(8,128)S(1)} collective-permute-done((f32[8,16,256]{2,1,0:T(8,128)S(1)}, f32[8,16,256]{2,1,0:T(8,128)S(1)}, u32[]{:S(2)}, u32[]{:S(2)}) %collective-permute-start.29) | collective-permute-done | bytes 131104 | tf_op jit(solution)/shard_map/ppermute | solution.py:429
  121.1 4.8 %collective-permute-done.34.refs_5_ = f32[16,16,256]{2,1,0:T(8,128)S(1)} collective-permute-done((f32[16,16,256]{2,1,0:T(8,128)S(1)}, f32[16,16,256]{2,1,0:T(8,128)S(1)}, u32[]{:S(2)}, u32[]{:S(2)}) %collective-permute-start.34) | collective-permute-done | bytes 262176 | tf_op jit(solution)/shard_map/ppermute | solution.py:340
  131.9 3.4 %collective-permute-start.38 = (f32[8,16,256]{2,1,0:T(8,128)S(1)}, f32[8,16,256]{2,1,0:T(8,128)S(1)}, u32[]{:S(2)}, u32[]{:S(2)}) collective-permute-start(f32[8,16,256]{2,1,0:T(8,128)S(1)} %get-tuple-element.112), channel_id=1, source_target_pairs={{0,4},{4,0},{8,12},{12,8},{1,5},{5,1},{9,13},{13,9},{2,6},{6,2},{1... | collective-permute-start | bytes 393224 | tf_op jit(solution)/shard_map/ppermute | solution.py:429
  135.3 2.4 %collective-permute-start.40 = (f32[8,16,256]{2,1,0:T(8,128)S(1)}, f32[8,16,256]{2,1,0:T(8,128)S(1)}, u32[]{:S(2)}, u32[]{:S(2)}) collective-permute-start(f32[8,16,256]{2,1,0:T(8,128)S(1)} %get-tuple-element.114), channel_id=1, source_target_pairs={{0,12},{4,8},{8,4},{12,0},{1,13},{5,9},{9,5},{13,1},{2,14},{6,10},... | collective-permute-start | bytes 393224 | tf_op jit(solution)/shard_map/ppermute | solution.py:429
  139.4 3.4 %collective-permute-start.41 = (f32[8,16,256]{2,1,0:T(8,128)S(1)}, f32[8,16,256]{2,1,0:T(8,128)S(1)}, u32[]{:S(2)}, u32[]{:S(2)}) collective-permute-start(f32[8,16,256]{2,1,0:T(8,128)S(1)} %get-tuple-element.109.refs_0_), channel_id=1, source_target_pairs={{0,4},{4,0},{8,12},{12,8},{1,5},{5,1},{9,13},{13,9},{2,6},{6,2},{1... | collective-permute-start | bytes 393224 | tf_op jit(solution)/shard_map/ppermute | solution.py:429
  145.2 3.3 %collective-permute-done.39.refs_4_ = f32[8,16,256]{2,1,0:T(8,128)S(1)} collective-permute-done((f32[8,16,256]{2,1,0:T(8,128)S(1)}, f32[8,16,256]{2,1,0:T(8,128)S(1)}, u32[]{:S(2)}, u32[]{:S(2)}) %collective-permute-start.39) | collective-permute-done | bytes 131104 | tf_op jit(solution)/shard_map/ppermute | solution.py:429
  148.5 2.3 %shard_map.113.refs_0_ = f32[16,32,512]{2,1,0:T(8,128)} custom-call(s32[16]{0:T(128)S(1)} %get-tuple-element.146.recv_pos, s32[16]{0:T(128)S(1)} %copy-done.14, s32[3]{0:T(128)S(1)} %copy-done.13, f32[8,16,256]{2,1,0:T(8,128)S(1)} %get-tuple-element.109.refs_0_, f32[16,16,512]{2,1,0:T(8,128)S(1)} %get-tuple-element.110.refs_1_, ...), custom_call_target="tpu_custom_call" | custom-call | flops 805306368 | tf_op jit(solution)/shard_map/pallas_call | solution.py:443
  150.9 7.8 %collective-permute-done.42.refs_4_ = f32[8,16,256]{2,1,0:T(8,128)S(1)} collective-permute-done((f32[8,16,256]{2,1,0:T(8,128)S(1)}, f32[8,16,256]{2,1,0:T(8,128)S(1)}, u32[]{:S(2)}, u32[]{:S(2)}) %collective-permute-start.42) | collective-permute-done | bytes 131104 | tf_op jit(solution)/shard_map/ppermute | solution.py:429
  158.7 2.3 %shard_map.114 = f32[16,32,512]{2,1,0:T(8,128)} custom-call(s32[16]{0:T(128)S(1)} %get-tuple-element.146.recv_pos, s32[16]{0:T(128)S(1)} %copy-done.14, s32[3]{0:T(128)S(1)} %copy-done.13, f32[16,32,512]{2,1,0:T(8,128)} %shard_map.113.refs_0_, f32[16,16,512]{2,1,0:T(8,128)S(1)} %get-tuple-element.115.refs_1_, ...), custom_call_target="tpu_custom_call", output_to_operand_aliasing={{}: (3, {})} | custom-call | flops 805306368 | tf_op jit(solution)/shard_map/pallas_call | solution.py:443
  (155 shorter events, 60.6 us)
Async XLA Ops:
  0.0 14.0 %collective-permute-start.1 = (f32[64,128,128]{2,1,0:T(8,128)}, f32[64,128,128]{2,1,0:T(8,128)}, u32[]{:S(2)}, u32[]{:S(2)}) collective-permute-start(f32[64,128,128]{2,1,0:T(8,128)} %bitcast.56), channel_id=1, source_target_pairs={{0,1},{1,0},{2,3},{3,2},{4,5},{5,4},{6,7},{7,6},{8,9},{9,8},{10,11... | collective-permute-start | bytes 12582920 | tf_op jit(solution)/shard_map/ppermute | solution.py:267
  7.4 16.5 %collective-permute-start.2 = (f32[16,16,256]{2,1,0:T(8,128)S(1)}, f32[16,16,256]{2,1,0:T(8,128)S(1)}, u32[]{:S(2)}, u32[]{:S(2)}) collective-permute-start(f32[16,16,256]{2,1,0:T(8,128)S(1)} %copy-done.11), channel_id=1, source_target_pairs={{0,1},{1,0},{2,3},{3,2},{4,5},{5,4},{6,7},{7,6},{8,9},{9,8},{10,11... | collective-permute-start | bytes 786440 | tf_op jit(solution)/shard_map/ppermute | solution.py:344
  7.5 15.6 %collective-permute-start.4 = (f32[16,16,256]{2,1,0:T(8,128)S(1)}, f32[16,16,256]{2,1,0:T(8,128)S(1)}, u32[]{:S(2)}, u32[]{:S(2)}) collective-permute-start(f32[16,16,256]{2,1,0:T(8,128)S(1)} %copy-done.11), channel_id=1, source_target_pairs={{0,2},{2,0},{1,3},{3,1},{4,6},{6,4},{5,7},{7,5},{8,10},{10,8},{9,1... | collective-permute-start | bytes 786440 | tf_op jit(solution)/shard_map/ppermute | solution.py:340
  11.4 11.6 %collective-permute-start.5 = (f32[16,16,256]{2,1,0:T(8,128)}, f32[16,16,256]{2,1,0:T(8,128)S(1)}, u32[]{:S(2)}, u32[]{:S(2)}) collective-permute-start(f32[16,16,256]{2,1,0:T(8,128)} %shard_map.92.refs_1_), channel_id=1, source_target_pairs={{0,2},{2,0},{1,3},{3,1},{4,6},{6,4},{5,7},{7,5},{8,10},{10,8},{9,1... | collective-permute-start | bytes 786440 | tf_op jit(solution)/shard_map/ppermute | solution.py:340
  12.6 11.3 %collective-permute-start.3 = (f32[16,16,256]{2,1,0:T(8,128)}, f32[16,16,256]{2,1,0:T(8,128)S(1)}, u32[]{:S(2)}, u32[]{:S(2)}) collective-permute-start(f32[16,16,256]{2,1,0:T(8,128)} %shard_map.92.refs_1_), channel_id=1, source_target_pairs={{0,1},{1,0},{2,3},{3,2},{4,5},{5,4},{6,7},{7,6},{8,9},{9,8},{10,11... | collective-permute-start | bytes 786440 | tf_op jit(solution)/shard_map/ppermute | solution.py:344
  33.5 12.6 %collective-permute-start.14 = (f32[1,16,16,256]{3,2,1,0:T(8,128)}, f32[1,16,16,256]{3,2,1,0:T(8,128)}, u32[]{:S(2)}, u32[]{:S(2)}) collective-permute-start(f32[1,16,16,256]{3,2,1,0:T(8,128)} %bitcast.22), channel_id=1, source_target_pairs={{0,2},{2,0},{1,3},{3,1},{4,6},{6,4},{5,7},{7,5},{8,10},{10,8},{9,1... | collective-permute-start | bytes 786440 | tf_op jit(solution)/shard_map/ppermute | solution.py:382
  43.4 23.2 %collective-permute-start.10 = (f32[65,16,128]{2,1,0:T(8,128)S(1)}, f32[65,16,128]{2,1,0:T(8,128)S(1)}, u32[]{:S(2)}, u32[]{:S(2)}) collective-permute-start(f32[65,16,128]{2,1,0:T(8,128)S(1)} %get-tuple-element.140), channel_id=1, source_target_pairs={{0,3},{1,2},{2,1},{3,0},{4,7},{5,6},{6,5},{7,4},{8,11},{9,10},{10,... | collective-permute-start | bytes 1597448 | tf_op jit(solution)/shard_map/ppermute | solution.py:396
  49.7 12.9 %collective-permute-start.16 = (f32[8,16,256]{2,1,0:T(8,128)S(1)}, f32[8,16,256]{2,1,0:T(8,128)S(1)}, u32[]{:S(2)}, u32[]{:S(2)}) collective-permute-start(f32[8,16,256]{2,1,0:T(8,128)S(1)} %get-tuple-element.90), channel_id=1, source_target_pairs={{0,8},{4,12},{8,0},{12,4},{1,9},{5,13},{9,1},{13,5},{2,10},{6,14},... | collective-permute-start | bytes 393224 | tf_op jit(solution)/shard_map/ppermute | solution.py:429
  52.4 16.8 %collective-permute-start.9 = (f32[65,16,128]{2,1,0:T(8,128)S(1)}, f32[65,16,128]{2,1,0:T(8,128)S(1)}, u32[]{:S(2)}, u32[]{:S(2)}) collective-permute-start(f32[65,16,128]{2,1,0:T(8,128)S(1)} %get-tuple-element.139), channel_id=1, source_target_pairs={{0,2},{1,3},{2,0},{3,1},{4,6},{5,7},{6,4},{7,5},{8,10},{9,11},{10,... | collective-permute-start | bytes 1597448 | tf_op jit(solution)/shard_map/ppermute | solution.py:396
  55.2 17.2 %collective-permute-start.11 = (f32[8,16,256]{2,1,0:T(8,128)S(1)}, f32[8,16,256]{2,1,0:T(8,128)S(1)}, u32[]{:S(2)}, u32[]{:S(2)}) collective-permute-start(f32[8,16,256]{2,1,0:T(8,128)S(1)} %get-tuple-element.79.refs_0_), channel_id=1, source_target_pairs={{0,4},{4,0},{8,12},{12,8},{1,5},{5,1},{9,13},{13,9},{2,6},{6,2},{1... | collective-permute-start | bytes 393224 | tf_op jit(solution)/shard_map/ppermute | solution.py:429
  62.7 11.2 %collective-permute-start.12 = (f32[8,16,256]{2,1,0:T(8,128)S(1)}, f32[8,16,256]{2,1,0:T(8,128)S(1)}, u32[]{:S(2)}, u32[]{:S(2)}) collective-permute-start(f32[8,16,256]{2,1,0:T(8,128)S(1)} %get-tuple-element.80), channel_id=1, source_target_pairs={{0,8},{4,12},{8,0},{12,4},{1,9},{5,13},{9,1},{13,5},{2,10},{6,14},... | collective-permute-start | bytes 393224 | tf_op jit(solution)/shard_map/ppermute | solution.py:429
  88.1 13.9 %collective-permute-start.25 = (f32[8,16,256]{2,1,0:T(8,128)S(1)}, f32[8,16,256]{2,1,0:T(8,128)S(1)}, u32[]{:S(2)}, u32[]{:S(2)}) collective-permute-start(f32[8,16,256]{2,1,0:T(8,128)S(1)} %get-tuple-element.98), channel_id=1, source_target_pairs={{0,4},{4,0},{8,12},{12,8},{1,5},{5,1},{9,13},{13,9},{2,6},{6,2},{1... | collective-permute-start | bytes 393224 | tf_op jit(solution)/shard_map/ppermute | solution.py:429
  93.7 13.0 %collective-permute-start.26 = (f32[8,16,256]{2,1,0:T(8,128)S(1)}, f32[8,16,256]{2,1,0:T(8,128)S(1)}, u32[]{:S(2)}, u32[]{:S(2)}) collective-permute-start(f32[8,16,256]{2,1,0:T(8,128)S(1)} %get-tuple-element.99), channel_id=1, source_target_pairs={{0,8},{4,12},{8,0},{12,4},{1,9},{5,13},{9,1},{13,5},{2,10},{6,14},... | collective-permute-start | bytes 393224 | tf_op jit(solution)/shard_map/ppermute | solution.py:429
  93.7 13.0 %collective-permute-start.27 = (f32[8,16,256]{2,1,0:T(8,128)S(1)}, f32[8,16,256]{2,1,0:T(8,128)S(1)}, u32[]{:S(2)}, u32[]{:S(2)}) collective-permute-start(f32[8,16,256]{2,1,0:T(8,128)S(1)} %get-tuple-element.100), channel_id=1, source_target_pairs={{0,12},{4,8},{8,4},{12,0},{1,13},{5,9},{9,5},{13,1},{2,14},{6,10},... | collective-permute-start | bytes 393224 | tf_op jit(solution)/shard_map/ppermute | solution.py:429
  97.7 12.4 %collective-permute-start.28 = (f32[8,16,256]{2,1,0:T(8,128)S(1)}, f32[8,16,256]{2,1,0:T(8,128)S(1)}, u32[]{:S(2)}, u32[]{:S(2)}) collective-permute-start(f32[8,16,256]{2,1,0:T(8,128)S(1)} %get-tuple-element.95.refs_0_), channel_id=1, source_target_pairs={{0,4},{4,0},{8,12},{12,8},{1,5},{5,1},{9,13},{13,9},{2,6},{6,2},{1... | collective-permute-start | bytes 393224 | tf_op jit(solution)/shard_map/ppermute | solution.py:429
  102.0 15.5 %collective-permute-start.29 = (f32[8,16,256]{2,1,0:T(8,128)S(1)}, f32[8,16,256]{2,1,0:T(8,128)S(1)}, u32[]{:S(2)}, u32[]{:S(2)}) collective-permute-start(f32[8,16,256]{2,1,0:T(8,128)S(1)} %get-tuple-element.104), channel_id=1, source_target_pairs={{0,8},{4,12},{8,0},{12,4},{1,9},{5,13},{9,1},{13,5},{2,10},{6,14},... | collective-permute-start | bytes 393224 | tf_op jit(solution)/shard_map/ppermute | solution.py:429
  102.0 15.5 %collective-permute-start.30 = (f32[8,16,256]{2,1,0:T(8,128)S(1)}, f32[8,16,256]{2,1,0:T(8,128)S(1)}, u32[]{:S(2)}, u32[]{:S(2)}) collective-permute-start(f32[8,16,256]{2,1,0:T(8,128)S(1)} %get-tuple-element.105), channel_id=1, source_target_pairs={{0,12},{4,8},{8,4},{12,0},{1,13},{5,9},{9,5},{13,1},{2,14},{6,10},... | collective-permute-start | bytes 393224 | tf_op jit(solution)/shard_map/ppermute | solution.py:429
  108.7 12.4 %collective-permute-start.33 = (f32[16,16,256]{2,1,0:T(8,128)S(1)}, f32[16,16,256]{2,1,0:T(8,128)S(1)}, u32[]{:S(2)}, u32[]{:S(2)}) collective-permute-start(f32[16,16,256]{2,1,0:T(8,128)S(1)} %get-tuple-element.101.refs_0_), channel_id=1, source_target_pairs={{0,2},{2,0},{1,3},{3,1},{4,6},{6,4},{5,7},{7,5},{8,10},{10,8},{9,1... | collective-permute-start | bytes 786440 | tf_op jit(solution)/shard_map/ppermute | solution.py:340
  131.9 11.4 %collective-permute-start.38 = (f32[8,16,256]{2,1,0:T(8,128)S(1)}, f32[8,16,256]{2,1,0:T(8,128)S(1)}, u32[]{:S(2)}, u32[]{:S(2)}) collective-permute-start(f32[8,16,256]{2,1,0:T(8,128)S(1)} %get-tuple-element.112), channel_id=1, source_target_pairs={{0,4},{4,0},{8,12},{12,8},{1,5},{5,1},{9,13},{13,9},{2,6},{6,2},{1... | collective-permute-start | bytes 393224 | tf_op jit(solution)/shard_map/ppermute | solution.py:429
  135.3 13.3 %collective-permute-start.39 = (f32[8,16,256]{2,1,0:T(8,128)S(1)}, f32[8,16,256]{2,1,0:T(8,128)S(1)}, u32[]{:S(2)}, u32[]{:S(2)}) collective-permute-start(f32[8,16,256]{2,1,0:T(8,128)S(1)} %get-tuple-element.113), channel_id=1, source_target_pairs={{0,8},{4,12},{8,0},{12,4},{1,9},{5,13},{9,1},{13,5},{2,10},{6,14},... | collective-permute-start | bytes 393224 | tf_op jit(solution)/shard_map/ppermute | solution.py:429
  135.3 13.3 %collective-permute-start.40 = (f32[8,16,256]{2,1,0:T(8,128)S(1)}, f32[8,16,256]{2,1,0:T(8,128)S(1)}, u32[]{:S(2)}, u32[]{:S(2)}) collective-permute-start(f32[8,16,256]{2,1,0:T(8,128)S(1)} %get-tuple-element.114), channel_id=1, source_target_pairs={{0,12},{4,8},{8,4},{12,0},{1,13},{5,9},{9,5},{13,1},{2,14},{6,10},... | collective-permute-start | bytes 393224 | tf_op jit(solution)/shard_map/ppermute | solution.py:429
  139.4 11.5 %collective-permute-start.41 = (f32[8,16,256]{2,1,0:T(8,128)S(1)}, f32[8,16,256]{2,1,0:T(8,128)S(1)}, u32[]{:S(2)}, u32[]{:S(2)}) collective-permute-start(f32[8,16,256]{2,1,0:T(8,128)S(1)} %get-tuple-element.109.refs_0_), channel_id=1, source_target_pairs={{0,4},{4,0},{8,12},{12,8},{1,5},{5,1},{9,13},{13,9},{2,6},{6,2},{1... | collective-permute-start | bytes 393224 | tf_op jit(solution)/shard_map/ppermute | solution.py:429
  142.8 15.9 %collective-permute-start.42 = (f32[8,16,256]{2,1,0:T(8,128)S(1)}, f32[8,16,256]{2,1,0:T(8,128)S(1)}, u32[]{:S(2)}, u32[]{:S(2)}) collective-permute-start(f32[8,16,256]{2,1,0:T(8,128)S(1)} %get-tuple-element.117), channel_id=1, source_target_pairs={{0,8},{4,12},{8,0},{12,4},{1,9},{5,13},{9,1},{13,5},{2,10},{6,14},... | collective-permute-start | bytes 393224 | tf_op jit(solution)/shard_map/ppermute | solution.py:429
  143.4 15.4 %collective-permute-start.43 = (f32[8,16,256]{2,1,0:T(8,128)S(1)}, f32[8,16,256]{2,1,0:T(8,128)S(1)}, u32[]{:S(2)}, u32[]{:S(2)}) collective-permute-start(f32[8,16,256]{2,1,0:T(8,128)S(1)} %get-tuple-element.118), channel_id=1, source_target_pairs={{0,12},{4,8},{8,4},{12,0},{1,13},{5,9},{9,5},{13,1},{2,14},{6,10},... | collective-permute-start | bytes 393224 | tf_op jit(solution)/shard_map/ppermute | solution.py:429
  (40 other events, 285.7 us)

commit v3 on v2

--- a/solution.py
+++ b/solution.py
@@ -70,44 +70,80 @@
     lax.fori_loop(0, acc.shape[0], one, 0)
 
 
-def cells_kernel(sizes, ids, pats, live, mine, theirs, *refs):
+def finish_cells(clusters, acc, counts, groups):
+    width = acc.shape[-1]
+
+    def finish(q, c):
+        lanes = pl.ds(pl.multiple_of(q * width, width), width)
+        for d, off, rc, ref, at in groups:
+            block = clusters * rc
+            alive = lax.broadcasted_iota(jnp.int32, (block, width), 1) < counts[q]
+            cell = acc[q, d, :, off : off + rc, :].reshape(block, width)
+            high, low = split(jnp.where(alive, cell, 0.0))
+            ref[at : at + block, lanes] = high
+            lows = ref.shape[0] // 2 + at
+            ref[lows : lows + block, lanes] = low
+        return c
+
+    lax.fori_loop(0, clusters, finish, 0)
+
+
+def near_kernel(sizes, ids, counts, pats, live, mine, theirs, *refs):
     trips, subs, share, chunks, clusters = sizes
     outs, (buf, acc, sems) = refs[:-3], refs[-3:]
-    rem, own = outs[: len(chunks)], outs[len(chunks) :]
+    slots = mine.shape[0]
+    start = pl.multiple_of((ids[0] * subs + ids[1]) * share, share)
+    copies = []
+    for half, ref in enumerate((mine, theirs)):
+        copies.append(pltpu.make_async_copy(ref.at[:, pl.ds(start, share), :], buf.at[half], sems.at[half]))
+        copies[-1].start()
+    clear(acc)
+    for half in range(2):
+        copies[half].wait()
+        add_cells(acc, 0, pats, live, half, lambda p, half=half: buf[half, p], slots)
+    finish_cells(clusters, acc, counts, [(0, off, rc, outs[r], 0) for r, (off, rc) in enumerate(chunks)])
+
+
+def remote_kernel(sizes, ids, counts, pats, live, marks, mine, theirs, *refs):
+    trips, subs, share, chunks, clusters = sizes
+    n = len(chunks)
+    outs, parts, (buf, acc, sems, part_sems) = refs[:n], refs[n:-4], refs[-4:]
     x, s = ids[0], ids[1]
-    slots, _, width = mine.shape
-    copies = {}
+    slots = mine.shape[0]
+    copies, part_copies = {}, []
     for half, ref in enumerate((mine, theirs)):
-        for d in range(trips):
+        for d in range(1, trips):
             start = pl.multiple_of((lax.rem(x + d, trips) * subs + s) * share, share)
             copies[half, d] = pltpu.make_async_copy(
-                ref.at[:, pl.ds(start, share), :], buf.at[half, d], sems.at[half, d]
+                ref.at[:, pl.ds(start, share), :], buf.at[half, d - 1], sems.at[half, d - 1]
             )
             copies[half, d].start()
+    off, rc = chunks[0]
+    for i, part in enumerate(parts):
+        core = 1 - s if i % 2 else s
+        start = pl.multiple_of((lax.rem(x + 1 + i // 2, trips) * subs + core) * share + off, rc)
+        for k, (src, at, size) in enumerate(((mine.at[:, pl.ds(start, rc), :], 0, slots), (marks, slots, 1))):
+            part_copies.append(pltpu.make_async_copy(src, part.at[at : at + size], part_sems.at[i, k]))
+            part_copies[-1].start()
     clear(acc)
     for half in range(2):
-        for d in range(trips):
+        for d in range(1, trips):
             copies[half, d].wait()
-            add_cells(acc, d, pats, live, half, lambda p, half=half, d=d: buf[half, d, p], slots)
-
-    def finish(q, c):
-        lanes = pl.ds(pl.multiple_of(q * width, width), width)
-        for r, (off, rc) in enumerate(chunks):
-            block = clusters * rc
-            for d in range(trips):
-                high, low = split(acc[q, d, :, off : off + rc, :].reshape(block, width))
-                ref, at, lows = (rem[r], (d - 1) * block, (trips - 1) * block) if d else (own[r], 0, block)
-                ref[at : at + block, lanes] = high
-                ref[lows + at : lows + at + block, lanes] = low
-        return c
-
-    lax.fori_loop(0, clusters, finish, 0)
-
-
-def early_kernel(sizes, ids, pats, live, mine, theirs, *refs):
+            add_cells(acc, d - 1, pats, live, half, lambda p, half=half, d=d: buf[half, d - 1, p], slots)
+    groups = [
+        (d - 1, off, rc, outs[r], (d - 1) * clusters * rc)
+        for r, (off, rc) in enumerate(chunks)
+        for d in range(1, trips)
+    ]
+    finish_cells(clusters, acc, counts, groups)
+    for copy in part_copies:
+        copy.wait()
+
+
+def early_kernel(sizes, ids, counts, pats, live, mine, theirs, *refs):
     subs, share, off, rc, clusters = sizes
     far, (out, buf, acc, sems) = refs[:-4], refs[-4:]
-    slots, _, width = mine.shape
+    slots = mine.shape[0]
     start = pl.multiple_of((ids[0] * subs + ids[1]) * share + off, rc)
     copies = []
     for half, ref in enumerate((mine, theirs)):
@@ -119,15 +155,7 @@
     for half in range(2):
         copies[half].wait()
         add_cells(acc, 0, pats, live, half, lambda p, half=half: buf[half, p], slots)
-
-    def finish(q, c):
-        lanes = pl.ds(pl.multiple_of(q * width, width), width)
-        high, low = split(acc[q, 0].reshape(clusters * rc, width))
-        out[: clusters * rc, lanes] = high
-        out[clusters * rc :, lanes] = low
-        return c
-
-    lax.fori_loop(0, clusters, finish, 0)
+    finish_cells(clusters, acc, counts, [(0, 0, rc, out, 0)])
 
 
 def terms(cells, x_hi, x_lo):
@@ -186,18 +214,19 @@
         pack(agg, send_src, cap, packs)
 
 
-def rows_kernel(sizes, last, unread, recv_pos, counts, ids, *refs):
-    clusters, rc, cap, steps, first_row = sizes
+def rows_kernel(sizes, last, unread, recv_pos, *refs):
+    clusters, rc, cap, steps = sizes
+    count = len(steps)
     refs = refs[unread:]
     feat, agg, refs = refs[0], refs[1], refs[2:]
-    got, refs = refs[:steps], refs[steps:]
+    got, refs = refs[:count], refs[count:]
     up_hi, up_lo, dense_hi, dense_lo, refs = *refs[:4], refs[4:]
     if last:
         out, held, both = refs
     else:
         down, (out, low_out, held, both) = refs[:2], refs[2:]
-    for k, ref in enumerate(got):
-        held[k * cap : (k + 1) * cap] = ref[...]
+    for k, ref in zip(steps, got):
+        held[(k - 1) * cap : k * cap] = ref[...]
     for c in range(clusters):
         both[c] = agg[c] + held[recv_pos[c] - cap]
     block = clusters * rc
@@ -207,32 +236,23 @@
     result = (merged + v / (1.0 + jnp.exp(-v))) * INV_TWO
     out[...] = result.reshape(out.shape)
     if not last:
-        lower(result, down[0][...], down[1][...], counts, ids, first_row, low_out)
-
-
-def lower(feat, down_hi, down_lo, counts, ids, first_row, out):
-    clusters, rc, width = out.shape
-    low = dot3(feat, down_hi, down_lo)
-    row = ids[2] + first_row + lax.broadcasted_iota(jnp.int32, (rc, width), 0)
-    for c in range(clusters):
-        out[c] = jnp.where(row < counts[c], low[c * rc : (c + 1) * rc, :], 0.0)
-
-
-def down_kernel(chunks, counts, ids, feat, down, *refs):
+        low_out[...] = dot3(result, down[0][...], down[1][...]).reshape(low_out.shape)
+
+
+def down_kernel(chunks, feat, down, *refs):
     outs, (rows, weight, sems) = refs[:-3], refs[-3:]
-    start, size = chunks[0][0], rows.shape[1]
-    copies = [
-        pltpu.make_async_copy(feat.at[:, start : start + size, :], rows, sems.at[0]),
-        pltpu.make_async_copy(down.at[0], weight, sems.at[1]),
-    ]
+    copies = [pltpu.make_async_copy(down.at[0], weight, sems.at[0])]
+    for r, (off, rc) in enumerate(chunks):
+        part = slice(off, off + rc)
+        copies.append(pltpu.make_async_copy(feat.at[:, part, :], rows.at[:, part, :], sems.at[1 + r]))
     for copy in copies:
         copy.start()
-    copies[1].wait()
+    copies[0].wait()
     high, low = split(weight[...])
-    copies[0].wait()
-    for (off, rc), out in zip(chunks, outs):
-        part = rows[:, off - start : off - start + rc, :].reshape(out.shape[0] * rc, -1)
-        lower(part, high, low, counts, ids, off, out)
+    for r, (off, rc) in enumerate(chunks):
+        copies[1 + r].wait()
+        part = rows[:, off : off + rc, :].reshape(-1, rows.shape[-1])
+        outs[r][...] = dot3(part, high, low).reshape(outs[r].shape)
 
 
 def local(
@@ -262,7 +282,7 @@
     def turn(d):
         return [(i, (i + d) % trips) for i in range(trips)]
 
-    ids = jnp.stack([x, s, (x * subs + s) * share]).astype(jnp.int32)
+    ids = jnp.stack([x, s]).astype(jnp.int32)
     coef = coef.reshape(coef.shape[2:])
     coef2 = lax.ppermute(coef, "sub", swap)
 
@@ -272,20 +292,18 @@
     def big(rc):
         return jax.ShapeDtypeStruct((clusters, rc, feat_width), F32)
 
-    lows = []
-    for group in ([0], list(range(1, n))):
-        lows += call(
-            functools.partial(down_kernel, [chunks[r] for r in group]),
-            [small(chunks[r][1]) for r in group],
-            [SMEM, SMEM, HBM, HBM],
-            60,
-            flops=6 * clusters * half_share * feat_width * width,
-            scratch=[
-                pltpu.VMEM((clusters, half_share, feat_width), F32),
-                pltpu.VMEM((feat_width, width), F32),
-                pltpu.SemaphoreType.DMA((2,)),
-            ],
-        )(edge_counts, ids, edge_feat, down_weight)
+    lows = call(
+        functools.partial(down_kernel, chunks),
+        [small(rc) for _, rc in chunks],
+        [HBM, HBM],
+        60,
+        flops=6 * clusters * share * feat_width * width,
+        scratch=[
+            pltpu.VMEM((clusters, share, feat_width), F32),
+            pltpu.VMEM((feat_width, width), F32),
+            pltpu.SemaphoreType.DMA((1 + n,)),
+        ],
+    )(edge_feat, down_weight)
     (down_weight, up_weight, dense_weight, reverse, patterns, trip_count, *lows) = lax.optimization_barrier(
         (down_weight, up_weight, dense_weight, reverse, patterns, trip_count, *lows)
     )
@@ -315,20 +333,23 @@
     up = [parts(up_weight[i]) for i in range(layers)]
     dense = [parts(dense_weight[i]) for i in range(layers)]
 
-    cells = call(
-        functools.partial(cells_kernel, (trips, subs, share, chunks, clusters)),
+    lead_rows = chunks[0][1]
+    marks = jnp.pad(note[0].astype(F32), (0, lead_rows * rows - note.shape[1])).reshape(1, lead_rows, rows)
+    remote = call(
+        functools.partial(remote_kernel, (trips, subs, share, chunks, clusters)),
         [jax.ShapeDtypeStruct((2 * (trips - 1) * clusters * rc, depth), BF16) for _, rc in chunks]
-        + [jax.ShapeDtypeStruct((2 * clusters * rc, depth), BF16) for _, rc in chunks],
-        [SMEM, SMEM, SMEM, HBM, HBM],
-        58,
+        + [jax.ShapeDtypeStruct((slots + 1, lead_rows, rows), F32)] * (2 * (trips - 1)),
+        [SMEM] * 4 + [HBM] * 3,
+        40,
         scratch=[
-            pltpu.VMEM((2, trips, slots, share, rows), F32),
-            pltpu.VMEM((clusters, trips, clusters, share, rows), F32),
-            pltpu.SemaphoreType.DMA((2, trips)),
+            pltpu.VMEM((2, trips - 1, slots, share, rows), F32),
+            pltpu.VMEM((clusters, trips - 1, clusters, share, rows), F32),
+            pltpu.SemaphoreType.DMA((2, trips - 1)),
+            pltpu.SemaphoreType.DMA((2 * (trips - 1), 2)),
         ],
         moved=12 << 20,
-    )(ids, note[:, :-1], note[:, -1], coef, coef2)
-    cells = list(cells)
+    )(ids, edge_counts, note[:, :-1], note[:, -1], marks, coef, coef2)
+    remote, parts = list(remote[:n]), remote[n:]
 
     feats, first = None, None
     for layer in range(layers):
@@ -339,11 +360,10 @@
             for d in range(trips):
                 far = lax.ppermute(lows[r], "trip", turn(d)) if d else lows[r]
                 if layer == 0 and d:
-                    far, cells[0] = lax.optimization_barrier((far, cells[0]))
+                    far, remote[0] = lax.optimization_barrier((far, remote[0]))
                 pieces[d, 0, r] = far
                 pieces[d, 1, r] = lax.ppermute(far, "sub", swap)
         inputs = [pieces[d, other, r] for d, other in places for r in range(n)]
-        remote, near = cells[:n], cells[n:]
         whole = layer > 0
         groups = [list(range(1, n))] if whole else [[1], [0], *[[r] for r in range(2, n)]]
         order = [0] * whole + [r for group in groups for r in group]
@@ -381,33 +401,18 @@
             sent = sent.reshape(len(group), trips - 1, clusters, rc, width)
             sums.append([lax.ppermute(sent[:, d - 1], "trip", turn(d)) for d in range(1, trips)])
         if layer == 0:
-            off, rc = chunks[0]
-            base, sums[-1] = lax.optimization_barrier((ids, sums[-1]))
-            marks = jnp.pad(note[0].astype(F32), (0, rc * rows - note.shape[1])).reshape(1, rc, rows)
-            far = []
-            for d in range(1, trips):
-                for other in range(2):
-                    core = 1 - base[1] if other else base[1]
-                    start = (lax.rem(base[0] + d, trips) * subs + core) * share + off
-                    part = jnp.concatenate([lax.dynamic_slice_in_dim(coef, start, rc, 1), marks])
-                    perm = [
-                        (i * subs + j, (i + d) % trips * subs + (j ^ other)) for i in range(trips) for j in range(subs)
-                    ]
-                    far.append(lax.ppermute(part, ("trip", "sub"), perm))
-            notes = jnp.stack([part[slots].reshape(-1)[: note.shape[1]].astype(jnp.int32) for part in far])
-            notes = jnp.concatenate([note, notes])
-            first = call(
-                functools.partial(early_kernel, (subs, share, off, rc, clusters)),
-                jax.ShapeDtypeStruct((2 * clusters * rc, depth), BF16),
-                [SMEM, SMEM, SMEM, HBM, HBM] + [VMEM] * len(far),
+            near = call(
+                functools.partial(near_kernel, (trips, subs, share, chunks, clusters)),
+                [jax.ShapeDtypeStruct((2 * clusters * rc, depth), BF16) for _, rc in chunks],
+                [SMEM] * 4 + [HBM] * 2,
                 40,
                 scratch=[
-                    pltpu.VMEM((2, slots, rc, rows), F32),
-                    pltpu.VMEM((clusters, 1, clusters, rc, rows), F32),
+                    pltpu.VMEM((2, slots, share, rows), F32),
+                    pltpu.VMEM((clusters, 1, clusters, share, rows), F32),
                     pltpu.SemaphoreType.DMA((2,)),
                 ],
-                moved=6 << 20,
-            )(ids, notes[:, :-1], notes[:, -1], coef, coef2, *far)
+                moved=8 << 20,
+            )(ids, edge_counts, note[:, :-1], note[:, -1], coef, coef2)
         for group, got in zip(groups, sums):
             rc = chunks[group[0]][1]
             own = product([near[r] for r in group]).reshape(len(group), clusters, rc, width)
@@ -420,13 +425,36 @@
             )(send_src, own, *got)
             for i, r in enumerate(group):
                 aggs[r], *packs[r] = packed[i * edges : (i + 1) * edges]
+        if layer == 0:
+            off, rc = chunks[0]
+            parts, packs[order[-1]] = lax.optimization_barrier((parts, packs[order[-1]]))
+            far = []
+            for d in range(1, trips):
+                for other in range(2):
+                    perm = [
+                        (i * subs + j, (i + d) % trips * subs + (j ^ other)) for i in range(trips) for j in range(subs)
+                    ]
+                    far.append(lax.ppermute(parts[2 * (d - 1) + other], ("trip", "sub"), perm))
+            notes = jnp.stack([part[slots].reshape(-1)[: note.shape[1]].astype(jnp.int32) for part in far])
+            notes = jnp.concatenate([note, notes])
+            first = call(
+                functools.partial(early_kernel, (subs, share, off, rc, clusters)),
+                jax.ShapeDtypeStruct((2 * clusters * rc, depth), BF16),
+                [SMEM] * 4 + [HBM] * 2 + [VMEM] * len(far),
+                40,
+                scratch=[
+                    pltpu.VMEM((2, slots, rc, rows), F32),
+                    pltpu.VMEM((clusters, 1, clusters, rc, rows), F32),
+                    pltpu.SemaphoreType.DMA((2,)),
+                ],
+                moved=6 << 20,
+            )(ids, edge_counts, notes[:, :-1], notes[:, -1], coef, coef2, *far)
         next_feats, next_lows = [None] * n, [None] * n
         result = None
         for i, r in enumerate(order):
             off, rc = chunks[r]
-            back = [None] * (edges - 1)
-            for k in range(edges - 1, 0, -1):
-                back[k - 1] = lax.ppermute(packs[r][k - 1], "edge", [(i, i ^ k) for i in range(edges)])
+            steps = list(range(edges - 1, 0, -1))
+            back = [lax.ppermute(packs[r][k - 1], "edge", [(i, i ^ k) for i in range(edges)]) for k in steps]
             feat, feat_spec = (
                 (edge_feat, rows_of(clusters, off, rc, feat_width))
                 if layer == 0
@@ -437,13 +465,13 @@
                 ahead.append(first)
             alias = {}
             if last and result is not None:
-                alias = {3 + len(ahead): 0}
+                alias = {1 + len(ahead): 0}
                 ahead.append(result)
             extra = [] if last else down[layer]
             result = call(
-                functools.partial(rows_kernel, (clusters, rc, cap, edges - 1, off), last, len(ahead)),
+                functools.partial(rows_kernel, (clusters, rc, cap, steps), last, len(ahead)),
                 big(share) if last else [big(rc), small(rc)],
-                [SMEM] * 3
+                [SMEM]
                 + [ANY] * len(ahead)
                 + [feat_spec]
                 + [VMEM] * (1 + edges - 1 + 4 + len(extra)),
@@ -456,7 +484,7 @@
                 ],
                 flops=6 * clusters * rc * feat_width * (2 * width + feat_width),
                 alias=alias,
-            )(recv_pos, edge_counts, ids, *ahead, feat, aggs[r], *back, *up[layer], *dense[layer], *extra)
+            )(recv_pos, *ahead, feat, aggs[r], *back, *up[layer], *dense[layer], *extra)
             if not last:
                 next_feats[r], next_lows[r] = result
         feats, lows = next_feats, next_lows

time: 161 us -> 148 us (0.919)
  Pallas kernels: 47.3 us -> 42.4 us
  starting transfers between devices: 50.4 us -> 45.7 us
  waiting for transfers between devices: 50.3 us -> 54.8 us
  other arithmetic: 4.72 us -> 1.74 us
  local copies, waits for them, and re-layouts: 5.31 us -> 2.64 us
  between operations: 2.94 us -> 1.16 us
    ppermute x18, starting transfers between devices: 34.2 us -> 29.4 us  [local(): lax.ppermute(packs[r][k - 1], 'edge', [(i, i ^ k) for i in range(edges)])]
    pallas_call x9, Pallas kernels: 28.2 us -> 23.9 us  [the longest x6 12.8 us: local(): call(functools.partial(rows_kernel, (clusters, rc, cap, steps), last, len...]
    ppermute x6, waiting for transfers between devices: 10.4 us -> 13.8 us  [local(): far = lax.ppermute(lows[r], 'trip', turn(d)) if d else lows[r]]
    ppermute x6, starting transfers between devices: 7.9 us -> 5.74 us  [local(): far = lax.ppermute(lows[r], 'trip', turn(d)) if d else lows[r]]
    ppermute x4, starting transfers between devices: 4.54 us -> 6.42 us  [local(): lax.ppermute(sent[:, d - 1], 'trip', turn(d))]
  transfers between devices with their start and end apart: 44 -> 44, of which waited for: 16 -> 19; matrix products, arithmetic and copies ran while one was open for 4% -> 1% of each run, Pallas kernels for 22% -> 21%
where the time goes in v3:
time: 148 us
  waiting for transfers between devices  54.8 us (37%)
  starting transfers between devices  45.7 us (31%)
  Pallas kernels  42.4 us (29%)
  local copies, waits for them, and re-layouts  2.64 us (2%)
  other arithmetic  1.74 us (1%)
    ppermute x18, waiting for transfers between devices, local(): lax.ppermute(packs[r][k - 1], 'edge', [(i, i ^ k) for i in range(edges)])  29.8 us
    ppermute x18, starting transfers between devices, local(): lax.ppermute(packs[r][k - 1], 'edge', [(i, i ^ k) for i in range(edges)])  29.4 us
    ppermute x6, waiting for transfers between devices, local(): far = lax.ppermute(lows[r], 'trip', turn(d)) if d else lows[r]  13.8 us
    pallas_call x6, Pallas kernels, local(): call(functools.partial(rows_kernel, (clusters, rc, cap, steps), last, len...  12.8 us
    pallas_call x7, Pallas kernels, product(): call(terms_kernel, jax.ShapeDtypeStruct((size, width), F32), [VMEM] * (2...  6.89 us
    ppermute x4, starting transfers between devices, local(): lax.ppermute(sent[:, d - 1], 'trip', turn(d))  6.42 us
    ppermute x4, waiting for transfers between devices, local(): lax.ppermute(sent[:, d - 1], 'trip', turn(d))  6.31 us
    ppermute x6, starting transfers between devices, local(): far = lax.ppermute(lows[r], 'trip', turn(d)) if d else lows[r]  5.74 us
  transfers between devices with their start and end apart: 44, of which 19 were waited for; matrix products, arithmetic and copies ran while one was open for 1% of the time, Pallas kernels for 21%

profile of v3, /device:TPU:0, one launch (start us, length us, event | category | flops | bytes accessed | tf_op | source)
XLA Modules:
  0.0 148.4 jit_solution(8868292549486179625)
XLA Ops:
  0.5 3.0 %shard_map.91 = (f32[16,16,256]{2,1,0:T(8,128)}, f32[16,16,256]{2,1,0:T(8,128)}) custom-call(f32[16,32,512]{2,1,0:T(8,128)} %refs_1_.3, f32[3,512,256]{2,1,0:T(8,128)} %down.1), custom_call_target="tpu_custom_call" | custom-call | flops 402653184 | tf_op jit(solution)/shard_map/pallas_call | solution.py:295
  3.7 3.0 %collective-permute-start.4 = (f32[16,16,256]{2,1,0:T(8,128)}, f32[16,16,256]{2,1,0:T(8,128)S(1)}, u32[]{:S(2)}, u32[]{:S(2)}) collective-permute-start(f32[16,16,256]{2,1,0:T(8,128)} %get-tuple-element.77.refs_0_), channel_id=1, source_target_pairs={{0,2},{2,0},{1,3},{3,1},{4,6},{6,4},{5,7},{7,5},{8,10},{10,8},{9,1... | collective-permute-start | bytes 786440 | tf_op jit(solution)/shard_map/ppermute | solution.py:361
  11.3 4.4 %shard_map.92 = (bf16[512,2048]{1,0:T(8,128)(2,1)S(1)}, bf16[512,2048]{1,0:T(8,128)(2,1)S(1)}, f32[65,16,128]{2,1,0:T(8,128)S(1)}, f32[65,16,128]{2,1,0:T(8,128)}) custom-call(s32[2]{0:T(128)S(1)} %pad_add_fusion.3.ids, s32[16]{0:T(128)S(1)} %copy-done.5, s32[2,128]{1,0:T(2,128)S(1)} %fusion.11.pats, s32[2]{0:T(128)S(1)} %fusion.12.live, ...), custom_call_target="tpu_custom_call" | custom-call | bytes 12582912 | tf_op jit(solution)/shard_map/pallas_call | solution.py:338
  15.7 3.3 %collective-permute-done.5.refs_5_ = f32[16,16,256]{2,1,0:T(8,128)S(1)} collective-permute-done((f32[16,16,256]{2,1,0:T(8,128)}, f32[16,16,256]{2,1,0:T(8,128)S(1)}, u32[]{:S(2)}, u32[]{:S(2)}) %collective-permute-start.5) | collective-permute-done | bytes 262176 | tf_op jit(solution)/shard_map/ppermute | solution.py:361
  26.2 3.6 %shard_map.94 = (bf16[512,2048]{1,0:T(8,128)(2,1)S(1)}, bf16[512,2048]{1,0:T(8,128)(2,1)S(1)}) custom-call(s32[2]{0:T(128)S(1)} %pad_add_fusion.3.ids, s32[16]{0:T(128)S(1)} %copy-done.5, s32[2,128]{1,0:T(2,128)S(1)} %fusion.11.pats, s32[2]{0:T(128)S(1)} %fusion.12.live, f32[64,128,128]{2,1,0:T(8,128)S(1)} %bitcast.51, ...), custom_call_target="tpu_custom_call" | custom-call | bytes 8388608 | tf_op jit(solution)/shard_map/pallas_call | solution.py:404
  36.4 2.6 %collective-permute-done.14.refs_0_ = f32[1,16,16,256]{3,2,1,0:T(8,128)S(1)} collective-permute-done((f32[1,16,16,256]{3,2,1,0:T(8,128)S(1)}, f32[1,16,16,256]{3,2,1,0:T(8,128)S(1)}, u32[]{:S(2)}, u32[]{:S(2)}) %collective-permute-start.14) | collective-permute-done | bytes 262176 | tf_op jit(solution)/shard_map/ppermute | solution.py:402
  39.6 3.8 %collective-permute-start.15 = (f32[8,16,256]{2,1,0:T(8,128)S(1)}, f32[8,16,256]{2,1,0:T(8,128)S(1)}, u32[]{:S(2)}, u32[]{:S(2)}) collective-permute-start(f32[8,16,256]{2,1,0:T(8,128)S(1)} %get-tuple-element.103), channel_id=1, source_target_pairs={{0,12},{4,8},{8,4},{12,0},{1,13},{5,9},{9,5},{13,1},{2,14},{6,10},... | collective-permute-start | bytes 393224 | tf_op jit(solution)/shard_map/ppermute | solution.py:457
  44.2 3.7 %collective-permute-done.15.refs_3_ = f32[8,16,256]{2,1,0:T(8,128)S(1)} collective-permute-done((f32[8,16,256]{2,1,0:T(8,128)S(1)}, f32[8,16,256]{2,1,0:T(8,128)S(1)}, u32[]{:S(2)}, u32[]{:S(2)}) %collective-permute-start.15) | collective-permute-done | bytes 131104 | tf_op jit(solution)/shard_map/ppermute | solution.py:457
  47.9 3.7 %collective-permute-start.11 = (f32[8,16,256]{2,1,0:T(8,128)S(1)}, f32[8,16,256]{2,1,0:T(8,128)S(1)}, u32[]{:S(2)}, u32[]{:S(2)}) collective-permute-start(f32[8,16,256]{2,1,0:T(8,128)S(1)} %get-tuple-element.93), channel_id=1, source_target_pairs={{0,12},{4,8},{8,4},{12,0},{1,13},{5,9},{9,5},{13,1},{2,14},{6,10},... | collective-permute-start | bytes 393224 | tf_op jit(solution)/shard_map/ppermute | solution.py:457
  51.6 7.4 %collective-permute-done.16.refs_4_ = f32[8,16,256]{2,1,0:T(8,128)S(1)} collective-permute-done((f32[8,16,256]{2,1,0:T(8,128)S(1)}, f32[8,16,256]{2,1,0:T(8,128)S(1)}, u32[]{:S(2)}, u32[]{:S(2)}) %collective-permute-start.16) | collective-permute-done | bytes 131104 | tf_op jit(solution)/shard_map/ppermute | solution.py:457
  59.0 3.7 %collective-permute-start.13 = (f32[8,16,256]{2,1,0:T(8,128)S(1)}, f32[8,16,256]{2,1,0:T(8,128)S(1)}, u32[]{:S(2)}, u32[]{:S(2)}) collective-permute-start(f32[8,16,256]{2,1,0:T(8,128)S(1)} %get-tuple-element.95.refs_0_), channel_id=1, source_target_pairs={{0,4},{4,0},{8,12},{12,8},{1,5},{5,1},{9,13},{13,9},{2,6},{6,2},{1... | collective-permute-start | bytes 393224 | tf_op jit(solution)/shard_map/ppermute | solution.py:457
  65.0 3.7 %shard_map.98.refs_0_.cells = bf16[512,2048]{1,0:T(8,128)(2,1)S(1)} custom-call(s32[2]{0:T(128)S(1)} %pad_add_fusion.3.ids, s32[16]{0:T(128)S(1)} %copy-done.5, s32[4,128]{1,0:T(4,128)S(1)} %slice.72.pats, s32[4]{0:T(128)S(1)} %slice_reduce_fusion.live, f32[64,128,128]{2,1,0:T(8,128)S(1)} %bitcast.52, f32[64,128,128]{2,1,0:T(8,128)} %collective-permute-done.1.theirs, ...), custom_call_target="tpu_custom_call" | custom-call | bytes 6291456 | tf_op jit(solution)/shard_map/pallas_call | solution.py:440
  73.4 3.8 %collective-permute-done.20.refs_4_ = f32[16,16,256]{2,1,0:T(8,128)S(1)} collective-permute-done((f32[16,16,256]{2,1,0:T(8,128)S(1)}, f32[16,16,256]{2,1,0:T(8,128)S(1)}, u32[]{:S(2)}, u32[]{:S(2)}) %collective-permute-start.20) | collective-permute-done | bytes 262176 | tf_op jit(solution)/shard_map/ppermute | solution.py:361
  84.6 3.5 %collective-permute-start.27 = (f32[8,16,256]{2,1,0:T(8,128)S(1)}, f32[8,16,256]{2,1,0:T(8,128)S(1)}, u32[]{:S(2)}, u32[]{:S(2)}) collective-permute-start(f32[8,16,256]{2,1,0:T(8,128)S(1)} %get-tuple-element.114), channel_id=1, source_target_pairs={{0,4},{4,0},{8,12},{12,8},{1,5},{5,1},{9,13},{13,9},{2,6},{6,2},{1... | collective-permute-start | bytes 393224 | tf_op jit(solution)/shard_map/ppermute | solution.py:457
  91.9 3.4 %collective-permute-start.30 = (f32[8,16,256]{2,1,0:T(8,128)S(1)}, f32[8,16,256]{2,1,0:T(8,128)S(1)}, u32[]{:S(2)}, u32[]{:S(2)}) collective-permute-start(f32[8,16,256]{2,1,0:T(8,128)S(1)} %get-tuple-element.109.refs_0_), channel_id=1, source_target_pairs={{0,4},{4,0},{8,12},{12,8},{1,5},{5,1},{9,13},{13,9},{2,6},{6,2},{1... | collective-permute-start | bytes 393224 | tf_op jit(solution)/shard_map/ppermute | solution.py:457
  95.4 6.6 %collective-permute-done.26.refs_4_ = f32[8,16,256]{2,1,0:T(8,128)S(1)} collective-permute-done((f32[8,16,256]{2,1,0:T(8,128)S(1)}, f32[8,16,256]{2,1,0:T(8,128)S(1)}, u32[]{:S(2)}, u32[]{:S(2)}) %collective-permute-start.26) | collective-permute-done | bytes 131104 | tf_op jit(solution)/shard_map/ppermute | solution.py:457
  104.2 3.3 %collective-permute-done.29.refs_3_ = f32[8,16,256]{2,1,0:T(8,128)S(1)} collective-permute-done((f32[8,16,256]{2,1,0:T(8,128)S(1)}, f32[8,16,256]{2,1,0:T(8,128)S(1)}, u32[]{:S(2)}, u32[]{:S(2)}) %collective-permute-start.29) | collective-permute-done | bytes 131104 | tf_op jit(solution)/shard_map/ppermute | solution.py:457
  110.5 6.6 %collective-permute-done.34.refs_5_ = f32[16,16,256]{2,1,0:T(8,128)S(1)} collective-permute-done((f32[16,16,256]{2,1,0:T(8,128)S(1)}, f32[16,16,256]{2,1,0:T(8,128)S(1)}, u32[]{:S(2)}, u32[]{:S(2)}) %collective-permute-start.34) | collective-permute-done | bytes 262176 | tf_op jit(solution)/shard_map/ppermute | solution.py:361
  124.2 2.4 %collective-permute-start.40 = (f32[8,16,256]{2,1,0:T(8,128)S(1)}, f32[8,16,256]{2,1,0:T(8,128)S(1)}, u32[]{:S(2)}, u32[]{:S(2)}) collective-permute-start(f32[8,16,256]{2,1,0:T(8,128)S(1)} %get-tuple-element.128), channel_id=1, source_target_pairs={{0,4},{4,0},{8,12},{12,8},{1,5},{5,1},{9,13},{13,9},{2,6},{6,2},{1... | collective-permute-start | bytes 393224 | tf_op jit(solution)/shard_map/ppermute | solution.py:457
  127.5 2.5 %collective-permute-done.37.refs_0_ = f32[1,16,16,256]{3,2,1,0:T(8,128)S(1)} collective-permute-done((f32[1,16,16,256]{3,2,1,0:T(8,128)S(1)}, f32[1,16,16,256]{3,2,1,0:T(8,128)S(1)}, u32[]{:S(2)}, u32[]{:S(2)}) %collective-permute-start.37) | collective-permute-done | bytes 262176 | tf_op jit(solution)/shard_map/ppermute | solution.py:402
  132.6 2.4 %collective-permute-start.43 = (f32[8,16,256]{2,1,0:T(8,128)S(1)}, f32[8,16,256]{2,1,0:T(8,128)S(1)}, u32[]{:S(2)}, u32[]{:S(2)}) collective-permute-start(f32[8,16,256]{2,1,0:T(8,128)S(1)} %get-tuple-element.123.refs_0_), channel_id=1, source_target_pairs={{0,4},{4,0},{8,12},{12,8},{1,5},{5,1},{9,13},{13,9},{2,6},{6,2},{1... | collective-permute-start | bytes 393224 | tf_op jit(solution)/shard_map/ppermute | solution.py:457
  135.4 2.3 %shard_map.113.refs_0_ = f32[16,32,512]{2,1,0:T(8,128)} custom-call(s32[16]{0:T(128)S(1)} %get-tuple-element.154.recv_pos, f32[8,16,256]{2,1,0:T(8,128)S(1)} %get-tuple-element.123.refs_0_, f32[16,16,512]{2,1,0:T(8,128)S(1)} %get-tuple-element.124.refs_1_, f32[16,16,256]{2,1,0:T(8,128)S(1)} %get-tuple-element.125.refs_2_, ...), custom_call_target="tpu_custom_call" | custom-call | flops 805306368 | tf_op jit(solution)/shard_map/pallas_call | solution.py:471
  139.0 7.1 %collective-permute-done.42.refs_4_ = f32[8,16,256]{2,1,0:T(8,128)S(1)} collective-permute-done((f32[8,16,256]{2,1,0:T(8,128)S(1)}, f32[8,16,256]{2,1,0:T(8,128)S(1)}, u32[]{:S(2)}, u32[]{:S(2)}) %collective-permute-start.42) | collective-permute-done | bytes 131104 | tf_op jit(solution)/shard_map/ppermute | solution.py:457
  146.0 2.4 %shard_map.114 = f32[16,32,512]{2,1,0:T(8,128)} custom-call(s32[16]{0:T(128)S(1)} %get-tuple-element.154.recv_pos, f32[16,32,512]{2,1,0:T(8,128)} %shard_map.113.refs_0_, f32[16,16,512]{2,1,0:T(8,128)S(1)} %get-tuple-element.129.refs_1_, f32[16,16,256]{2,1,0:T(8,128)S(1)} %get-tuple-element.130.refs_2_, ...), custom_call_target="tpu_custom_call", output_to_operand_aliasing={{}: (1, {})} | custom-call | flops 805306368 | tf_op jit(solution)/shard_map/pallas_call | solution.py:471
  (134 shorter events, 55.0 us)
Async XLA Ops:
  0.0 9.1 %collective-permute-start.1 = (f32[64,128,128]{2,1,0:T(8,128)}, f32[64,128,128]{2,1,0:T(8,128)}, u32[]{:S(2)}, u32[]{:S(2)}) collective-permute-start(f32[64,128,128]{2,1,0:T(8,128)} %bitcast.49), channel_id=1, source_target_pairs={{0,1},{1,0},{2,3},{3,2},{4,5},{5,4},{6,7},{7,6},{8,9},{9,8},{10,11... | collective-permute-start | bytes 12582920 | tf_op jit(solution)/shard_map/ppermute | solution.py:287
  3.6 16.0 %collective-permute-start.2 = (f32[16,16,256]{2,1,0:T(8,128)}, f32[16,16,256]{2,1,0:T(8,128)S(1)}, u32[]{:S(2)}, u32[]{:S(2)}) collective-permute-start(f32[16,16,256]{2,1,0:T(8,128)} %get-tuple-element.77.refs_0_), channel_id=1, source_target_pairs={{0,1},{1,0},{2,3},{3,2},{4,5},{5,4},{6,7},{7,6},{8,9},{9,8},{10,11... | collective-permute-start | bytes 786440 | tf_op jit(solution)/shard_map/ppermute | solution.py:365
  3.7 12.0 %collective-permute-start.4 = (f32[16,16,256]{2,1,0:T(8,128)}, f32[16,16,256]{2,1,0:T(8,128)S(1)}, u32[]{:S(2)}, u32[]{:S(2)}) collective-permute-start(f32[16,16,256]{2,1,0:T(8,128)} %get-tuple-element.77.refs_0_), channel_id=1, source_target_pairs={{0,2},{2,0},{1,3},{3,1},{4,6},{6,4},{5,7},{7,5},{8,10},{10,8},{9,1... | collective-permute-start | bytes 786440 | tf_op jit(solution)/shard_map/ppermute | solution.py:361
  7.6 11.4 %collective-permute-start.5 = (f32[16,16,256]{2,1,0:T(8,128)}, f32[16,16,256]{2,1,0:T(8,128)S(1)}, u32[]{:S(2)}, u32[]{:S(2)}) collective-permute-start(f32[16,16,256]{2,1,0:T(8,128)} %get-tuple-element.78.refs_1_), channel_id=1, source_target_pairs={{0,2},{2,0},{1,3},{3,1},{4,6},{6,4},{5,7},{7,5},{8,10},{10,8},{9,1... | collective-permute-start | bytes 786440 | tf_op jit(solution)/shard_map/ppermute | solution.py:361
  8.8 10.9 %collective-permute-start.3 = (f32[16,16,256]{2,1,0:T(8,128)}, f32[16,16,256]{2,1,0:T(8,128)S(1)}, u32[]{:S(2)}, u32[]{:S(2)}) collective-permute-start(f32[16,16,256]{2,1,0:T(8,128)} %get-tuple-element.78.refs_1_), channel_id=1, source_target_pairs={{0,1},{1,0},{2,3},{3,2},{4,5},{5,4},{6,7},{7,6},{8,9},{9,8},{10,11... | collective-permute-start | bytes 786440 | tf_op jit(solution)/shard_map/ppermute | solution.py:365
  23.8 9.0 %collective-permute-start.8 = (f32[1,16,16,256]{3,2,1,0:T(8,128)S(1)}, f32[1,16,16,256]{3,2,1,0:T(8,128)S(1)}, u32[]{:S(2)}, u32[]{:S(2)}) collective-permute-start(f32[1,16,16,256]{3,2,1,0:T(8,128)S(1)} %bitcast.57), channel_id=1, source_target_pairs={{0,2},{2,0},{1,3},{3,1},{4,6},{6,4},{5,7},{7,5},{8,10},{10,8},{9,1... | collective-permute-start | bytes 786440 | tf_op jit(solution)/shard_map/ppermute | solution.py:402
  29.8 9.2 %collective-permute-start.14 = (f32[1,16,16,256]{3,2,1,0:T(8,128)S(1)}, f32[1,16,16,256]{3,2,1,0:T(8,128)S(1)}, u32[]{:S(2)}, u32[]{:S(2)}) collective-permute-start(f32[1,16,16,256]{3,2,1,0:T(8,128)S(1)} %bitcast.60), channel_id=1, source_target_pairs={{0,2},{2,0},{1,3},{3,1},{4,6},{6,4},{5,7},{7,5},{8,10},{10,8},{9,1... | collective-permute-start | bytes 786440 | tf_op jit(solution)/shard_map/ppermute | solution.py:402
  33.4 31.4 %collective-permute-start.10 = (f32[65,16,128]{2,1,0:T(8,128)}, f32[65,16,128]{2,1,0:T(8,128)S(1)}, u32[]{:S(2)}, u32[]{:S(2)}) collective-permute-start(f32[65,16,128]{2,1,0:T(8,128)} %get-tuple-element.91), channel_id=1, source_target_pairs={{0,3},{1,2},{2,1},{3,0},{4,7},{5,6},{6,5},{7,4},{8,11},{9,10},{10,... | collective-permute-start | bytes 1597448 | tf_op jit(solution)/shard_map/ppermute | solution.py:437
  34.8 30.0 %collective-permute-start.9 = (f32[65,16,128]{2,1,0:T(8,128)S(1)}, f32[65,16,128]{2,1,0:T(8,128)S(1)}, u32[]{:S(2)}, u32[]{:S(2)}) collective-permute-start(f32[65,16,128]{2,1,0:T(8,128)S(1)} %get-tuple-element.90), channel_id=1, source_target_pairs={{0,2},{1,3},{2,0},{3,1},{4,6},{5,7},{6,4},{7,5},{8,10},{9,11},{10,... | collective-permute-start | bytes 1597448 | tf_op jit(solution)/shard_map/ppermute | solution.py:437
  43.4 15.6 %collective-permute-start.16 = (f32[8,16,256]{2,1,0:T(8,128)S(1)}, f32[8,16,256]{2,1,0:T(8,128)S(1)}, u32[]{:S(2)}, u32[]{:S(2)}) collective-permute-start(f32[8,16,256]{2,1,0:T(8,128)S(1)} %get-tuple-element.104), channel_id=1, source_target_pairs={{0,8},{4,12},{8,0},{12,4},{1,9},{5,13},{9,1},{13,5},{2,10},{6,14},... | collective-permute-start | bytes 393224 | tf_op jit(solution)/shard_map/ppermute | solution.py:457
  43.4 15.6 %collective-permute-start.17 = (f32[8,16,256]{2,1,0:T(8,128)S(1)}, f32[8,16,256]{2,1,0:T(8,128)S(1)}, u32[]{:S(2)}, u32[]{:S(2)}) collective-permute-start(f32[8,16,256]{2,1,0:T(8,128)S(1)} %get-tuple-element.105), channel_id=1, source_target_pairs={{0,4},{4,0},{8,12},{12,8},{1,5},{5,1},{9,13},{13,9},{2,6},{6,2},{1... | collective-permute-start | bytes 393224 | tf_op jit(solution)/shard_map/ppermute | solution.py:457
  47.9 20.8 %collective-permute-start.11 = (f32[8,16,256]{2,1,0:T(8,128)S(1)}, f32[8,16,256]{2,1,0:T(8,128)S(1)}, u32[]{:S(2)}, u32[]{:S(2)}) collective-permute-start(f32[8,16,256]{2,1,0:T(8,128)S(1)} %get-tuple-element.93), channel_id=1, source_target_pairs={{0,12},{4,8},{8,4},{12,0},{1,13},{5,9},{9,5},{13,1},{2,14},{6,10},... | collective-permute-start | bytes 393224 | tf_op jit(solution)/shard_map/ppermute | solution.py:457
  59.0 9.7 %collective-permute-start.12 = (f32[8,16,256]{2,1,0:T(8,128)S(1)}, f32[8,16,256]{2,1,0:T(8,128)S(1)}, u32[]{:S(2)}, u32[]{:S(2)}) collective-permute-start(f32[8,16,256]{2,1,0:T(8,128)S(1)} %get-tuple-element.94), channel_id=1, source_target_pairs={{0,8},{4,12},{8,0},{12,4},{1,9},{5,13},{9,1},{13,5},{2,10},{6,14},... | collective-permute-start | bytes 393224 | tf_op jit(solution)/shard_map/ppermute | solution.py:457
  59.0 9.7 %collective-permute-start.13 = (f32[8,16,256]{2,1,0:T(8,128)S(1)}, f32[8,16,256]{2,1,0:T(8,128)S(1)}, u32[]{:S(2)}, u32[]{:S(2)}) collective-permute-start(f32[8,16,256]{2,1,0:T(8,128)S(1)} %get-tuple-element.95.refs_0_), channel_id=1, source_target_pairs={{0,4},{4,0},{8,12},{12,8},{1,5},{5,1},{9,13},{13,9},{2,6},{6,2},{1... | collective-permute-start | bytes 393224 | tf_op jit(solution)/shard_map/ppermute | solution.py:457
  83.9 18.1 %collective-permute-start.26 = (f32[8,16,256]{2,1,0:T(8,128)S(1)}, f32[8,16,256]{2,1,0:T(8,128)S(1)}, u32[]{:S(2)}, u32[]{:S(2)}) collective-permute-start(f32[8,16,256]{2,1,0:T(8,128)S(1)} %get-tuple-element.113), channel_id=1, source_target_pairs={{0,8},{4,12},{8,0},{12,4},{1,9},{5,13},{9,1},{13,5},{2,10},{6,14},... | collective-permute-start | bytes 393224 | tf_op jit(solution)/shard_map/ppermute | solution.py:457
  84.6 17.5 %collective-permute-start.27 = (f32[8,16,256]{2,1,0:T(8,128)S(1)}, f32[8,16,256]{2,1,0:T(8,128)S(1)}, u32[]{:S(2)}, u32[]{:S(2)}) collective-permute-start(f32[8,16,256]{2,1,0:T(8,128)S(1)} %get-tuple-element.114), channel_id=1, source_target_pairs={{0,4},{4,0},{8,12},{12,8},{1,5},{5,1},{9,13},{13,9},{2,6},{6,2},{1... | collective-permute-start | bytes 393224 | tf_op jit(solution)/shard_map/ppermute | solution.py:457
  90.9 13.3 %collective-permute-start.28 = (f32[8,16,256]{2,1,0:T(8,128)S(1)}, f32[8,16,256]{2,1,0:T(8,128)S(1)}, u32[]{:S(2)}, u32[]{:S(2)}) collective-permute-start(f32[8,16,256]{2,1,0:T(8,128)S(1)} %get-tuple-element.118), channel_id=1, source_target_pairs={{0,12},{4,8},{8,4},{12,0},{1,13},{5,9},{9,5},{13,1},{2,14},{6,10},... | collective-permute-start | bytes 393224 | tf_op jit(solution)/shard_map/ppermute | solution.py:457
  91.2 16.3 %collective-permute-start.29 = (f32[8,16,256]{2,1,0:T(8,128)S(1)}, f32[8,16,256]{2,1,0:T(8,128)S(1)}, u32[]{:S(2)}, u32[]{:S(2)}) collective-permute-start(f32[8,16,256]{2,1,0:T(8,128)S(1)} %get-tuple-element.119), channel_id=1, source_target_pairs={{0,8},{4,12},{8,0},{12,4},{1,9},{5,13},{9,1},{13,5},{2,10},{6,14},... | collective-permute-start | bytes 393224 | tf_op jit(solution)/shard_map/ppermute | solution.py:457
  91.9 15.5 %collective-permute-start.30 = (f32[8,16,256]{2,1,0:T(8,128)S(1)}, f32[8,16,256]{2,1,0:T(8,128)S(1)}, u32[]{:S(2)}, u32[]{:S(2)}) collective-permute-start(f32[8,16,256]{2,1,0:T(8,128)S(1)} %get-tuple-element.109.refs_0_), channel_id=1, source_target_pairs={{0,4},{4,0},{8,12},{12,8},{1,5},{5,1},{9,13},{13,9},{2,6},{6,2},{1... | collective-permute-start | bytes 393224 | tf_op jit(solution)/shard_map/ppermute | solution.py:457
  122.1 10.5 %collective-permute-start.38 = (f32[8,16,256]{2,1,0:T(8,128)S(1)}, f32[8,16,256]{2,1,0:T(8,128)S(1)}, u32[]{:S(2)}, u32[]{:S(2)}) collective-permute-start(f32[8,16,256]{2,1,0:T(8,128)S(1)} %get-tuple-element.126), channel_id=1, source_target_pairs={{0,12},{4,8},{8,4},{12,0},{1,13},{5,9},{9,5},{13,1},{2,14},{6,10},... | collective-permute-start | bytes 393224 | tf_op jit(solution)/shard_map/ppermute | solution.py:457
  124.2 11.2 %collective-permute-start.39 = (f32[8,16,256]{2,1,0:T(8,128)S(1)}, f32[8,16,256]{2,1,0:T(8,128)S(1)}, u32[]{:S(2)}, u32[]{:S(2)}) collective-permute-start(f32[8,16,256]{2,1,0:T(8,128)S(1)} %get-tuple-element.127), channel_id=1, source_target_pairs={{0,8},{4,12},{8,0},{12,4},{1,9},{5,13},{9,1},{13,5},{2,10},{6,14},... | collective-permute-start | bytes 393224 | tf_op jit(solution)/shard_map/ppermute | solution.py:457
  124.2 11.2 %collective-permute-start.40 = (f32[8,16,256]{2,1,0:T(8,128)S(1)}, f32[8,16,256]{2,1,0:T(8,128)S(1)}, u32[]{:S(2)}, u32[]{:S(2)}) collective-permute-start(f32[8,16,256]{2,1,0:T(8,128)S(1)} %get-tuple-element.128), channel_id=1, source_target_pairs={{0,4},{4,0},{8,12},{12,8},{1,5},{5,1},{9,13},{13,9},{2,6},{6,2},{1... | collective-permute-start | bytes 393224 | tf_op jit(solution)/shard_map/ppermute | solution.py:457
  132.6 13.5 %collective-permute-start.42 = (f32[8,16,256]{2,1,0:T(8,128)S(1)}, f32[8,16,256]{2,1,0:T(8,128)S(1)}, u32[]{:S(2)}, u32[]{:S(2)}) collective-permute-start(f32[8,16,256]{2,1,0:T(8,128)S(1)} %get-tuple-element.132), channel_id=1, source_target_pairs={{0,8},{4,12},{8,0},{12,4},{1,9},{5,13},{9,1},{13,5},{2,10},{6,14},... | collective-permute-start | bytes 393224 | tf_op jit(solution)/shard_map/ppermute | solution.py:457
  132.6 13.5 %collective-permute-start.43 = (f32[8,16,256]{2,1,0:T(8,128)S(1)}, f32[8,16,256]{2,1,0:T(8,128)S(1)}, u32[]{:S(2)}, u32[]{:S(2)}) collective-permute-start(f32[8,16,256]{2,1,0:T(8,128)S(1)} %get-tuple-element.123.refs_0_), channel_id=1, source_target_pairs={{0,4},{4,0},{8,12},{12,8},{1,5},{5,1},{9,13},{13,9},{2,6},{6,2},{1... | collective-permute-start | bytes 393224 | tf_op jit(solution)/shard_map/ppermute | solution.py:457
  (31 other events, 202.7 us)

commit v4 on v3

v4 whole, which is shorter than its diff:
```python
import functools

import jax
import jax.numpy as jnp
from jax import lax
from jax.experimental import pallas as pl
from jax.experimental.pallas import tpu as pltpu
from jax.sharding import PartitionSpec as P

INV_THREE = 1.0 / 3.0**0.5
INV_TWO = 1.0 / 2.0**0.5
F32 = jnp.float32
BF16 = jnp.bfloat16
SMEM = pl.BlockSpec(memory_space=pltpu.SMEM)
VMEM = pl.BlockSpec(memory_space=pltpu.VMEM)
ANY = pl.BlockSpec(memory_space=pl.ANY)
HBM = pl.BlockSpec(memory_space=pltpu.HBM)


def split(v):
    high = v.astype(BF16)
    return high, (v - high.astype(F32)).astype(BF16)


def dot(a, b):
    return jnp.dot(a, b, preferred_element_type=F32)


def dot3(a, high, low):
    rows = a.shape[0]
    a_high, a_low = split(a)
    both = dot(jnp.concatenate([a_high, a_low], axis=0), high)
    return both[:rows] + (both[rows:] + dot(a_high, low))


def call(kernel, outs, ins, mib, out_specs=None, scratch=(), flops=0, moved=0, alias=None, grid=()):
    return pl.pallas_call(
        kernel,
        grid=grid,
        out_shape=outs,
        in_specs=ins,
        out_specs=jax.tree.map(lambda _: VMEM, outs) if out_specs is None else out_specs,
        scratch_shapes=list(scratch),
        input_output_aliases=alias or {},
        compiler_params=pltpu.CompilerParams(vmem_limit_bytes=mib << 20),
        cost_estimate=pl.CostEstimate(flops=flops, bytes_accessed=moved, transcendentals=0),
    )


def rows_of(clusters, start, size, width):
    return pl.BlockSpec((clusters, size, width), lambda i: (0, start // size, 0))


def add_cells(acc, pats, live, half, count, slots, load):
    many = 4 if slots % 4 == 0 else 1
    alive = jnp.minimum(live[half], slots)

    def add(i, c):
        found = []
        for p in [many * i + u for u in range(many)]:
            values = [jnp.where(p < alive, load(p, d), 0.0) for d in range(count)]
            found.append((pats[half, 2 * p], pats[half, 2 * p + 1], values))
        for t, q, values in found:
            for d, value in enumerate(values):
                acc[q, d, t] += value
        return c

    lax.fori_loop(0, lax.div(alive + (many - 1), many), add, 0)


def clear(acc):
    zero = jnp.zeros(acc.shape[1:], F32)

    def one(q, c):
        acc[q] = zero
        return c

    lax.fori_loop(0, acc.shape[0], one, 0)


def finish_cells(sizes, x, acc, counts, groups):
    trips, subs, share, clusters = sizes
    width, chip = trips * subs * share, subs * share
    step = clusters // 2

    def finish(g, c):
        for d, off, rc, ref, at in groups:
            block = step * rc
            lane = lax.broadcasted_iota(jnp.int32, (block, width), 1)
            for t in range(0, clusters, step):
                cells = []
                for j in range(trips):
                    cell = acc[g * trips + j, d, t : t + step, off : off + rc, :].reshape(block, width)
                    cells.append(jnp.where(lane < counts[g * trips + j], cell, 0.0))
                bit = 1
                while bit < trips:
                    low_half = lane // chip % (2 * bit) < bit
                    for i in range(trips):
                        if not i & bit:
                            a, b = cells[i], cells[i | bit]
                            cells[i] = jnp.where(low_half, a, pltpu.roll(b, bit * chip, 1))
                            cells[i | bit] = jnp.where(low_half, pltpu.roll(a, width - bit * chip, 1), b)
                    bit *= 2
                for i, cell in enumerate(cells):
                    place = lax.rem(x + trips - i, trips) * clusters * chip + g * width
                    lanes = pl.ds(pl.multiple_of(place, width), width)
                    row = at + t * rc
                    high, low = split(cell)
                    ref[row : row + block, lanes] = high
                    row += ref.shape[0] // 2
                    ref[row : row + block, lanes] = low
        return c

    lax.fori_loop(0, clusters // trips, finish, 0)


def cells_kernel(sizes, ids, counts, pats, live, marks, mine, theirs, *refs):
    trips, subs, share, chunks, clusters = sizes
    n = len(chunks)
    near, remote, parts, (buf, acc, sems, part_sems) = refs[:n], refs[n : 2 * n], refs[2 * n : -4], refs[-4:]
    x, s = ids[0], ids[1]
    slots = mine.shape[0]
    copies, part_copies = [], []
    for half, ref in enumerate((mine, theirs)):
        for d in range(trips):
            start = pl.multiple_of((lax.rem(x + d, trips) * subs + s) * share, share)
            copies.append(
                pltpu.make_async_copy(ref.at[:, pl.ds(start, share), :], buf.at[half, d], sems.at[half, d])
            )
            copies[-1].start()
    off, rc = chunks[0]
    for i, part in enumerate(parts):
        core = 1 - s if i % 2 else s
        start = pl.multiple_of((lax.rem(x + 1 + i // 2, trips) * subs + core) * share + off, rc)
        for k, (src, at, size) in enumerate(((mine.at[:, pl.ds(start, rc), :], 0, slots), (marks, slots, 1))):
            part_copies.append(pltpu.make_async_copy(src, part.at[at : at + size], part_sems.at[i, k]))
            part_copies[-1].start()
    clear(acc)
    for half in range(2):
        for d in range(trips):
            copies[half * trips + d].wait()
        add_cells(acc, pats, live, half, trips, slots, lambda p, d, half=half: buf[half, d, p])
    groups = []
    for r, (off, rc) in enumerate(chunks):
        groups.append((0, off, rc, near[r], 0))
        groups += [(d, off, rc, remote[r], (d - 1) * clusters * rc) for d in range(1, trips)]
    finish_cells((trips, subs, share, clusters), x, acc, counts, groups)
    for copy in part_copies:
        copy.wait()


def early_kernel(sizes, ids, counts, pats, live, mine, theirs, *refs):
    trips, subs, share, off, rc, clusters = sizes
    far, (out, buf, acc, sems) = refs[:-4], refs[-4:]
    slots = mine.shape[0]
    start = pl.multiple_of((ids[0] * subs + ids[1]) * share + off, rc)
    copies = []
    for half, ref in enumerate((mine, theirs)):
        copies.append(pltpu.make_async_copy(ref.at[:, pl.ds(start, rc), :], buf.at[half], sems.at[half]))
        copies[-1].start()
    clear(acc)
    for i, ref in enumerate(far):
        add_cells(acc, pats, live, 2 + i, 1, slots, lambda p, d, ref=ref: ref[p])
    for half in range(2):
        copies[half].wait()
        add_cells(acc, pats, live, half, 1, slots, lambda p, d, half=half: buf[half, p])
    finish_cells((trips, subs, share, clusters), ids[0], acc, counts, [(0, 0, rc, out, 0)])


def terms(cells, x_hi, x_lo, first=0):
    rows = cells.shape[0] // 2
    columns = slice(first, first + x_hi.shape[0])
    both = dot(cells[:, columns], x_hi[...])
    return both[:rows] + (both[rows:] + dot(cells[:rows, columns], x_lo[...]))


def spread(s, n, pieces, x_hi, x_lo):
    clusters = pieces[0].shape[0]
    share = sum(ref.shape[1] for ref in pieces[:n])
    for i in range(0, len(pieces) // n):
        core = 1 - s if i % 2 else s
        for q in range(clusters):
            high, low = split(jnp.concatenate([ref[q] for ref in pieces[i * n : (i + 1) * n]], axis=0))
            at = (i // 2 * clusters + q) * 2 * share + core * share
            spot = pl.ds(pl.multiple_of(at, share), share)
            x_hi[spot, :] = high
            x_lo[spot, :] = low


def near_kernel(home_hi, home_lo, far_hi, far_lo, cells, out):
    out[...] = terms(cells, home_hi, home_lo) + terms(cells, far_hi, far_lo, home_hi.shape[0])


def home_kernel(n, ids, one, two, *refs):
    pieces, (x_hi, x_lo, one_out, two_out) = refs[:-4], refs[-4:]
    spread(ids[1], n, pieces, x_hi, x_lo)
    one_out[...] = terms(one, x_hi, x_lo)
    two_out[...] = terms(two, x_hi, x_lo)


def pack(agg, send_src, cap, packs):
    for k, ref in enumerate(packs):
        for j in range(cap):
            ref[j] = agg[send_src[(k + 1) * cap + j]]


def far_kernel(n, count, cap, whole, ids, send_src, one, two, one_in, two_in, *refs):
    pieces, (x_hi, x_lo, two_out, *outs) = refs[:count], refs[count:]
    first = one.shape[1] - x_hi.shape[0]
    spread(ids[1], n, pieces, x_hi, x_lo)
    out = one_in[...] + terms(one, x_hi, x_lo, first)
    two_out[...] = two_in[...] + terms(two, x_hi, x_lo, first)
    if whole:
        agg, *packs = outs
        agg[...] = out.reshape(agg.shape)
        pack(agg, send_src, cap, packs)
    else:
        outs[0][...] = out


def pack_kernel(cap, arrivals, send_src, local, *refs):
    got, (agg, *packs) = refs[:arrivals], refs[arrivals:]
    total = local[...]
    for ref in got:
        total = total + ref[...]
    agg[...] = total
    pack(agg, send_src, cap, packs)


def rows_kernel(sizes, last, unread, recv_pos, *refs):
    clusters, rc, cap, steps = sizes
    refs = refs[unread:]
    feat, agg, refs = refs[0], refs[1], refs[2:]
    got, refs = refs[: len(steps)], refs[len(steps) :]
    up_hi, up_lo, dense_hi, dense_lo, refs = *refs[:4], refs[4:]
    if last:
        out, held, both = refs
    else:
        down, (out, low_out, held, both) = refs[:2], refs[2:]
    for k, ref in zip(steps, got):
        held[(k - 1) * cap : k * cap] = ref[...]
    for c in range(clusters):
        both[c] = agg[c] + held[recv_pos[c] - cap]
    block = clusters * rc
    lifted = dot3(both[...].reshape(block, -1), up_hi[...], up_lo[...])
    merged = (feat[...].reshape(block, -1) + lifted) * INV_THREE
    v = dot3(merged, dense_hi[...], dense_lo[...])
    result = (merged + v / (1.0 + jnp.exp(-v))) * INV_TWO
    out[...] = result.reshape(out.shape)
    if not last:
        low_out[...] = dot3(result, down[0][...], down[1][...]).reshape(low_out.shape)


def down_kernel(chunks, feat, down, *refs):
    outs, (rows, weight, sems) = refs[:-3], refs[-3:]
    copies = [pltpu.make_async_copy(down.at[0], weight, sems.at[0])]
    for r, (off, rc) in enumerate(chunks):
        part = slice(off, off + rc)
        copies.append(pltpu.make_async_copy(feat.at[:, part, :], rows.at[:, part, :], sems.at[1 + r]))
    for copy in copies:
        copy.start()
    copies[0].wait()
    high, low = split(weight[...])
    for r, (off, rc) in enumerate(chunks):
        copies[1 + r].wait()
        part = rows[:, off : off + rc, :].reshape(-1, rows.shape[-1])
        result = dot3(part, high, low).reshape(-1, rc, weight.shape[-1])
        outs[r][...] = result


def local(
    edge_feat,
    edge_counts,
    reverse,
    patterns,
    trip_count,
    coef,
    down_weight,
    up_weight,
    dense_weight,
):
    clusters, share, feat_width = edge_feat.shape
    layers, _, width = down_weight.shape
    edges, trips, subs = (lax.axis_size(a) for a in ("edge", "trip", "sub"))
    e, x, s = (lax.axis_index(a) for a in ("edge", "trip", "sub"))
    rows = trips * subs * share
    cap = 2 * ((clusters // 2 + edges // 2 - 1) // (edges // 2))
    half_share = share // 2
    chunks = [(0, half_share), (half_share, half_share)]
    n = len(chunks)
    depth = clusters * rows
    slots = patterns.shape[2]
    swap = [(0, 1), (1, 0)]

    def turn(d):
        return [(i, (i + d) % trips) for i in range(trips)]

    ids = jnp.stack([x, s]).astype(jnp.int32)
    coef = coef.reshape(coef.shape[2:])
    coef2 = lax.ppermute(coef, "sub", swap)

    def small(rc):
        return jax.ShapeDtypeStruct((clusters, rc, width), F32)

    def big(rc):
        return jax.ShapeDtypeStruct((clusters, rc, feat_width), F32)

    lows = call(
        functools.partial(down_kernel, chunks),
        [small(rc) for _, rc in chunks],
        [HBM, HBM],
        60,
        flops=6 * clusters * share * feat_width * width,
        scratch=[
            pltpu.VMEM((clusters, share, feat_width), F32),
            pltpu.VMEM((feat_width, width), F32),
            pltpu.SemaphoreType.DMA((1 + n,)),
        ],
    )(edge_feat, down_weight)
    (down_weight, up_weight, dense_weight, reverse, patterns, trip_count, *lows) = lax.optimization_barrier(
        (down_weight, up_weight, dense_weight, reverse, patterns, trip_count, *lows)
    )

    note = jnp.concatenate([patterns.reshape(-1), trip_count.reshape(-1)])
    note = jnp.stack([note, lax.ppermute(note, "sub", swap)])
    here = jnp.arange(clusters, dtype=jnp.int32)
    mine = lax.dynamic_slice_in_dim(reverse, e * clusters, clusters)
    to = mine // clusters
    earlier = (to[:, None] == to[None, :]) & (here[None, :] < here[:, None])
    send_pos = (to ^ e) * cap + jnp.sum(earlier.astype(jnp.int32), axis=1)
    places = jnp.arange(edges * cap, dtype=jnp.int32)
    send_src = jnp.sum(jnp.where(places[:, None] == send_pos[None, :], here[None, :], 0), axis=1)
    everyone = jnp.arange(reverse.shape[0], dtype=jnp.int32)
    before = (
        (everyone[None, :] // clusters == to[:, None])
        & (everyone[None, :] < mine[:, None])
        & ((reverse // clusters)[None, :] == e)
    )
    recv_pos = (to ^ e) * cap + jnp.sum(before.astype(jnp.int32), axis=1)

    def parts(w):
        high = lax.reduce_precision(w, 8, 7)
        return high.astype(BF16), (w - high).astype(BF16)

    down = [parts(down_weight[i]) for i in range(1, layers)]
    up = [parts(up_weight[i]) for i in range(layers)]
    dense = [parts(dense_weight[i]) for i in range(layers)]

    lead_rows = chunks[0][1]
    marks = jnp.pad(note[0].astype(F32), (0, lead_rows * rows - note.shape[1])).reshape(1, lead_rows, rows)

    cells = call(
        functools.partial(cells_kernel, (trips, subs, share, chunks, clusters)),
        [jax.ShapeDtypeStruct((2 * clusters * rc, depth), BF16) for _, rc in chunks]
        + [jax.ShapeDtypeStruct((2 * (trips - 1) * clusters * rc, depth), BF16) for _, rc in chunks]
        + [jax.ShapeDtypeStruct((slots + 1, lead_rows, rows), F32)] * (2 * (trips - 1)),
        [SMEM] * 4 + [HBM] * 3,
        40,
        scratch=[
            pltpu.VMEM((2, trips, slots, share, rows), F32),
            pltpu.VMEM((clusters, trips, clusters, share, rows), F32),
            pltpu.SemaphoreType.DMA((2, trips)),
            pltpu.SemaphoreType.DMA((2 * (trips - 1), 2)),
        ],
        moved=12 << 20,
    )(ids, edge_counts, note[:, :-1], note[:, -1], marks, coef, coef2)
    near, remote, parts = cells[:n], cells[n : 2 * n], cells[2 * n :]

    feats, first = None, None
    for layer in range(layers):
        last = layer == layers - 1
        whole = layer > 0
        order = [0, 1] if whole else [1, 0]
        one, two = first if whole else remote[order[0]], remote[order[1]]
        sizes = [cell.shape[0] // 2 for cell in (one, two)]
        home_depth = subs * clusters * share

        far = [[lax.ppermute(low, "trip", turn(d)) for low in lows] for d in range(1, trips)]
        home = lows + [lax.ppermute(low, "sub", swap) for low in lows]
        home_hi, home_lo, *sides = call(
            functools.partial(home_kernel, n),
            [jax.ShapeDtypeStruct((home_depth, width), BF16)] * 2
            + [jax.ShapeDtypeStruct((size, width), F32) for size in sizes],
            [SMEM] + [VMEM] * (2 + len(home)),
            32,
            flops=6 * sum(sizes) * home_depth * width,
        )(ids, one, two, *home)
        for got in far:
            for r in range(n):
                if layer == 0:
                    got[r], sides[0] = lax.optimization_barrier((got[r], sides[0]))
        far = sum((got + [lax.ppermute(low, "sub", swap) for low in got] for got in far), [])
        if whole:
            outs = [small(chunks[0][1])] + [jax.ShapeDtypeStruct((cap, chunks[0][1], width), F32)] * (edges - 1)
        else:
            outs = [jax.ShapeDtypeStruct((sizes[0], width), F32)]
        far_hi, far_lo, second, *outs = call(
            functools.partial(far_kernel, n, len(far), cap, whole),
            [jax.ShapeDtypeStruct((depth - home_depth, width), BF16)] * 2
            + [jax.ShapeDtypeStruct((sizes[1], width), F32)]
            + outs,
            [SMEM] * 2 + [VMEM] * (4 + len(far)),
            32,
            flops=6 * sum(sizes) * (depth - home_depth) * width,
        )(ids, send_src, one, two, *sides, *far)

        aggs, packs, sums = {}, {}, {}
        if whole:
            aggs[0], *packs[0] = outs
        else:
            sums[order[0]] = outs[0]
        sums[order[1]] = second
        for r, sent in sums.items():
            sent = sent.reshape(trips - 1, clusters, chunks[r][1], width)
            sums[r] = [lax.ppermute(sent[d - 1], "trip", turn(d)) for d in range(1, trips)]
        for r, got in sums.items():
            rc = chunks[r][1]
            own = call(
                near_kernel,
                jax.ShapeDtypeStruct((clusters * rc, width), F32),
                [VMEM] * 5,
                32,
                flops=6 * clusters * rc * depth * width,
            )(home_hi, home_lo, far_hi, far_lo, near[r]).reshape(clusters, rc, width)
            aggs[r], *packs[r] = call(
                functools.partial(pack_kernel, cap, trips - 1),
                [small(rc)] + [jax.ShapeDtypeStruct((cap, rc, width), F32)] * (edges - 1),
                [SMEM] + [VMEM] * trips,
                16,
                moved=4 << 20,
            )(send_src, own, *got)
        if layer == 0:
            off, rc = chunks[0]
            parts, packs[order[-1]] = lax.optimization_barrier((parts, packs[order[-1]]))
            far = []
            for d in range(1, trips):
                for other in range(2):
                    perm = [
                        (i * subs + j, (i + d) % trips * subs + (j ^ other)) for i in range(trips) for j in range(subs)
                    ]
                    far.append(lax.ppermute(parts[2 * (d - 1) + other], ("trip", "sub"), perm))
            notes = jnp.stack([part[slots].reshape(-1)[: note.shape[1]].astype(jnp.int32) for part in far])
            notes = jnp.concatenate([note, notes])
            first = call(
                functools.partial(early_kernel, (trips, subs, share, off, rc, clusters)),
                jax.ShapeDtypeStruct((2 * clusters * rc, depth), BF16),
                [SMEM] * 4 + [HBM] * 2 + [VMEM] * len(far),
                40,
                scratch=[
                    pltpu.VMEM((2, slots, rc, rows), F32),
                    pltpu.VMEM((clusters, 1, clusters, rc, rows), F32),
                    pltpu.SemaphoreType.DMA((2,)),
                ],
                moved=6 << 20,
            )(ids, edge_counts, notes[:, :-1], notes[:, -1], coef, coef2, *far)
        next_feats, next_lows = [None] * n, [None] * n
        result = None
        steps = list(range(edges - 1, 0, -1))
        for i, r in enumerate(order):
            off, rc = chunks[r]
            back = [lax.ppermute(packs[r][k - 1], "edge", [(i, i ^ k) for i in range(edges)]) for k in steps]
            if layer == 0:
                feat, feat_spec = edge_feat, rows_of(clusters, off, rc, feat_width)
            else:
                feat, feat_spec = feats[r], VMEM
            ahead = [packs[later][0] for later in order[i + 1 :]]
            if layer == 0 and i == n - 1:
                ahead.append(first)
            alias = {}
            if last and result is not None:
                alias = {1 + len(ahead): 0}
                ahead.append(result)
            extra = [] if last else down[layer]
            result = call(
                functools.partial(rows_kernel, (clusters, rc, cap, steps), last, len(ahead)),
                big(share) if last else [big(rc), small(rc)],
                [SMEM] + [ANY] * len(ahead) + [feat_spec] + [VMEM] * (1 + edges - 1 + 4 + len(extra)),
                32,
                grid=(1,),
                out_specs=rows_of(clusters, off, rc, feat_width) if last else [VMEM, VMEM],
                scratch=[
                    pltpu.VMEM(((edges - 1) * cap, rc, width), F32),
                    pltpu.VMEM((clusters, rc, width), F32),
                ],
                flops=6 * clusters * rc * feat_width * (2 * width + feat_width),
                alias=alias,
            )(recv_pos, *ahead, feat, aggs[r], *back, *up[layer], *dense[layer], *extra)
            if not last:
                next_feats[r], next_lows[r] = result
        feats, lows = next_feats, next_lows
    return result


def solution(mesh):
    placed = (
        P(("groups", "edge"), ("trip", "sub"), None),
        P(("groups", "edge")),
        P("groups"),
        P(("groups", "edge"), ("trip", "sub"), None, None),
        P(("groups", "edge"), ("trip", "sub")),
        P(("groups", "edge"), ("trip", "sub"), None, None, None),
        P(),
        P(),
        P(),
    )
    return jax.shard_map(
        local,
        mesh=mesh,
        in_specs=placed,
        out_specs=P(("groups", "edge"), ("trip", "sub"), None),
        check_vma=False,
    )
```

time: 148 us -> 148 us (level)
    ppermute x18, waiting for transfers between devices: 29.8 us -> 28.2 us  [local(): lax.ppermute(packs[r][k - 1], 'edge', [(i, i ^ k) for i in range(edges)])]
    pallas_call x17 -> x16, Pallas kernels: 26.5 us -> 26.5 us  [the longest x1 6.15 us: local(): call(functools.partial(cells_kernel, (trips, subs, share, chunks, cluster...]
  transfers between devices with their start and end apart: 44 -> 44, of which waited for: 19 -> 16; matrix products, arithmetic and copies ran while one was open for 1% -> 1% of each run, Pallas kernels for 21% -> 23%
where the time goes in v4:
time: 148 us
  waiting for transfers between devices  53.4 us (36%)
  starting transfers between devices  46.9 us (32%)
  Pallas kernels  42.3 us (29%)
  local copies, waits for them, and re-layouts  2.58 us (2%)
  other arithmetic  1.76 us (1%)
    ppermute x18, starting transfers between devices, local(): lax.ppermute(packs[r][k - 1], 'edge', [(i, i ^ k) for i in range(edges)])  30.2 us
    ppermute x18, waiting for transfers between devices, local(): lax.ppermute(packs[r][k - 1], 'edge', [(i, i ^ k) for i in range(edges)])  28.2 us
    ppermute x4, waiting for transfers between devices, local(): lax.ppermute(sent[d - 1], 'trip', turn(d))  12.9 us
    pallas_call x6, Pallas kernels, local(): call(functools.partial(rows_kernel, (clusters, rc, cap, steps), last, len...  12.8 us
    ppermute x6, waiting for transfers between devices, local(): lax.ppermute(low, 'trip', turn(d))  10.9 us
    ppermute x6, starting transfers between devices, local(): lax.ppermute(low, 'trip', turn(d))  8.57 us
    pallas_call x1, Pallas kernels, local(): call(functools.partial(cells_kernel, (trips, subs, share, chunks, cluster...  6.15 us
    pallas_call x3, Pallas kernels, local(): call(functools.partial(far_kernel, n, len(far), cap, whole), [jax.ShapeDt...  5.25 us
  transfers between devices with their start and end apart: 44, of which 16 were waited for; matrix products, arithmetic and copies ran while one was open for 1% of the time, Pallas kernels for 23%

profile of v4, /device:TPU:0, one launch (start us, length us, event | category | flops | bytes accessed | tf_op | source)
XLA Modules:
  0.0 148.1 jit_solution(16374652898247920398)
XLA Ops:
  0.5 3.0 %shard_map.91 = (f32[16,16,256]{2,1,0:T(8,128)}, f32[16,16,256]{2,1,0:T(8,128)}) custom-call(f32[16,32,512]{2,1,0:T(8,128)} %refs_1_.3, f32[3,512,256]{2,1,0:T(8,128)} %down.1), custom_call_target="tpu_custom_call" | custom-call | flops 402653184 | tf_op jit(solution)/shard_map/pallas_call | solution.py:308
  3.7 3.0 %collective-permute-start.4 = (f32[16,16,256]{2,1,0:T(8,128)}, f32[16,16,256]{2,1,0:T(8,128)S(1)}, u32[]{:S(2)}, u32[]{:S(2)}) collective-permute-start(f32[16,16,256]{2,1,0:T(8,128)} %get-tuple-element.94.refs_1_), channel_id=1, source_target_pairs={{0,2},{2,0},{1,3},{3,1},{4,6},{6,4},{5,7},{7,5},{8,10},{10,8},{9,1... | collective-permute-start | bytes 786440 | tf_op jit(solution)/shard_map/ppermute | solution.py:378
  10.4 2.2 %copy-done = f32[1,1,64,128,128]{4,3,2,1,0:T(8,128)S(1)} copy-done((f32[1,1,64,128,128]{4,3,2,1,0:T(8,128)S(1)}, f32[1,1,64,128,128]{4,3,2,1,0:T(8,128)}, u32[]{:S(2)}) %copy-start) | copy-done | bytes 4194328
  12.6 6.1 %shard_map.92 = (bf16[512,2048]{1,0:T(8,128)(2,1)S(1)}, bf16[512,2048]{1,0:T(8,128)(2,1)S(1)}, bf16[512,2048]{1,0:T(8,128)(2,1)S(1)}, bf16[512,2048]{1,0:T(8,128...) custom-call(s32[2]{0:T(128)S(1)} %pad_add_fusion.3.ids, s32[16]{0:T(128)S(1)} %copy-done.5, ...), custom_call_target="tpu_custom_call" | custom-call | bytes 12582912 | tf_op jit(solution)/shard_map/pallas_call | solution.py:352
  27.9 5.5 %collective-permute-done.8.refs_0_ = f32[16,16,256]{2,1,0:T(8,128)S(1)} collective-permute-done((f32[16,16,256]{2,1,0:T(8,128)S(1)}, f32[16,16,256]{2,1,0:T(8,128)S(1)}, u32[]{:S(2)}, u32[]{:S(2)}) %collective-permute-start.8) | collective-permute-done | bytes 262176 | tf_op jit(solution)/shard_map/ppermute | solution.py:415
  36.2 2.8 %collective-permute-done.14.refs_0_ = f32[16,16,256]{2,1,0:T(8,128)S(1)} collective-permute-done((f32[16,16,256]{2,1,0:T(8,128)S(1)}, f32[16,16,256]{2,1,0:T(8,128)S(1)}, u32[]{:S(2)}, u32[]{:S(2)}) %collective-permute-start.14) | collective-permute-done | bytes 262176 | tf_op jit(solution)/shard_map/ppermute | solution.py:415
  39.6 3.7 %collective-permute-start.15 = (f32[8,16,256]{2,1,0:T(8,128)S(1)}, f32[8,16,256]{2,1,0:T(8,128)S(1)}, u32[]{:S(2)}, u32[]{:S(2)}) collective-permute-start(f32[8,16,256]{2,1,0:T(8,128)S(1)} %get-tuple-element.123), channel_id=1, source_target_pairs={{0,12},{4,8},{8,4},{12,0},{1,13},{5,9},{9,5},{13,1},{2,14},{6,10},... | collective-permute-start | bytes 393224 | tf_op jit(solution)/shard_map/ppermute | solution.py:461
  44.2 3.4 %collective-permute-done.15.refs_3_ = f32[8,16,256]{2,1,0:T(8,128)S(1)} collective-permute-done((f32[8,16,256]{2,1,0:T(8,128)S(1)}, f32[8,16,256]{2,1,0:T(8,128)S(1)}, u32[]{:S(2)}, u32[]{:S(2)}) %collective-permute-start.15) | collective-permute-done | bytes 131104 | tf_op jit(solution)/shard_map/ppermute | solution.py:461
  47.6 3.9 %collective-permute-start.11 = (f32[8,16,256]{2,1,0:T(8,128)S(1)}, f32[8,16,256]{2,1,0:T(8,128)S(1)}, u32[]{:S(2)}, u32[]{:S(2)}) collective-permute-start(f32[8,16,256]{2,1,0:T(8,128)S(1)} %get-tuple-element.113), channel_id=1, source_target_pairs={{0,12},{4,8},{8,4},{12,0},{1,13},{5,9},{9,5},{13,1},{2,14},{6,10},... | collective-permute-start | bytes 393224 | tf_op jit(solution)/shard_map/ppermute | solution.py:461
  51.5 6.7 %collective-permute-done.16.refs_4_ = f32[8,16,256]{2,1,0:T(8,128)S(1)} collective-permute-done((f32[8,16,256]{2,1,0:T(8,128)S(1)}, f32[8,16,256]{2,1,0:T(8,128)S(1)}, u32[]{:S(2)}, u32[]{:S(2)}) %collective-permute-start.16) | collective-permute-done | bytes 131104 | tf_op jit(solution)/shard_map/ppermute | solution.py:461
  58.2 4.2 %collective-permute-start.13 = (f32[8,16,256]{2,1,0:T(8,128)S(1)}, f32[8,16,256]{2,1,0:T(8,128)S(1)}, u32[]{:S(2)}, u32[]{:S(2)}) collective-permute-start(f32[8,16,256]{2,1,0:T(8,128)S(1)} %get-tuple-element.115.refs_0_), channel_id=1, source_target_pairs={{0,4},{4,0},{8,12},{12,8},{1,5},{5,1},{9,13},{13,9},{2,6},{6,2},{1... | collective-permute-start | bytes 393224 | tf_op jit(solution)/shard_map/ppermute | solution.py:461
  65.6 3.7 %shard_map.97.refs_0_.one = bf16[512,2048]{1,0:T(8,128)(2,1)S(1)} custom-call(s32[2]{0:T(128)S(1)} %pad_add_fusion.3.ids, s32[16]{0:T(128)S(1)} %copy-done.5, s32[4,128]{1,0:T(4,128)S(1)} %slice.70.pats, s32[4]{0:T(128)S(1)} %slice_reduce_fusion.live, f32[64,128,128]{2,1,0:T(8,128)S(1)} %bitcast.51, f32[64,128,128]{2,1,0:T(8,128)} %collective-permute-done.1.theirs, ...), custom_call_target="tpu_custom_call" | custom-call | bytes 6291456 | tf_op jit(solution)/shard_map/pallas_call | solution.py:444
  73.1 4.8 %collective-permute-done.20.refs_0_ = f32[16,16,256]{2,1,0:T(8,128)S(1)} collective-permute-done((f32[16,16,256]{2,1,0:T(8,128)S(1)}, f32[16,16,256]{2,1,0:T(8,128)S(1)}, u32[]{:S(2)}, u32[]{:S(2)}) %collective-permute-start.20) | collective-permute-done | bytes 262176 | tf_op jit(solution)/shard_map/ppermute | solution.py:378
  83.9 3.1 %collective-permute-start.27 = (f32[8,16,256]{2,1,0:T(8,128)S(1)}, f32[8,16,256]{2,1,0:T(8,128)S(1)}, u32[]{:S(2)}, u32[]{:S(2)}) collective-permute-start(f32[8,16,256]{2,1,0:T(8,128)S(1)} %get-tuple-element.139), channel_id=1, source_target_pairs={{0,4},{4,0},{8,12},{12,8},{1,5},{5,1},{9,13},{13,9},{2,6},{6,2},{1... | collective-permute-start | bytes 393224 | tf_op jit(solution)/shard_map/ppermute | solution.py:461
  87.9 2.3 %collective-permute-done.24.refs_0_ = f32[16,16,256]{2,1,0:T(8,128)S(1)} collective-permute-done((f32[16,16,256]{2,1,0:T(8,128)S(1)}, f32[16,16,256]{2,1,0:T(8,128)S(1)}, u32[]{:S(2)}, u32[]{:S(2)}) %collective-permute-start.24) | collective-permute-done | bytes 262176 | tf_op jit(solution)/shard_map/ppermute | solution.py:415
  92.2 3.0 %collective-permute-start.30 = (f32[8,16,256]{2,1,0:T(8,128)S(1)}, f32[8,16,256]{2,1,0:T(8,128)S(1)}, u32[]{:S(2)}, u32[]{:S(2)}) collective-permute-start(f32[8,16,256]{2,1,0:T(8,128)S(1)} %get-tuple-element.134.refs_0_), channel_id=1, source_target_pairs={{0,4},{4,0},{8,12},{12,8},{1,5},{5,1},{9,13},{13,9},{2,6},{6,2},{1... | collective-permute-start | bytes 393224 | tf_op jit(solution)/shard_map/ppermute | solution.py:461
  95.2 7.0 %collective-permute-done.26.refs_4_ = f32[8,16,256]{2,1,0:T(8,128)S(1)} collective-permute-done((f32[8,16,256]{2,1,0:T(8,128)S(1)}, f32[8,16,256]{2,1,0:T(8,128)S(1)}, u32[]{:S(2)}, u32[]{:S(2)}) %collective-permute-start.26) | collective-permute-done | bytes 131104 | tf_op jit(solution)/shard_map/ppermute | solution.py:461
  110.8 6.1 %collective-permute-done.34.refs_1_ = f32[16,16,256]{2,1,0:T(8,128)S(1)} collective-permute-done((f32[16,16,256]{2,1,0:T(8,128)S(1)}, f32[16,16,256]{2,1,0:T(8,128)S(1)}, u32[]{:S(2)}, u32[]{:S(2)}) %collective-permute-start.34) | collective-permute-done | bytes 262176 | tf_op jit(solution)/shard_map/ppermute | solution.py:378
  122.8 3.1 %collective-permute-start.40 = (f32[8,16,256]{2,1,0:T(8,128)S(1)}, f32[8,16,256]{2,1,0:T(8,128)S(1)}, u32[]{:S(2)}, u32[]{:S(2)}) collective-permute-start(f32[8,16,256]{2,1,0:T(8,128)S(1)} %get-tuple-element.158), channel_id=1, source_target_pairs={{0,4},{4,0},{8,12},{12,8},{1,5},{5,1},{9,13},{13,9},{2,6},{6,2},{1... | collective-permute-start | bytes 393224 | tf_op jit(solution)/shard_map/ppermute | solution.py:461
  126.8 2.3 %collective-permute-done.37.refs_0_ = f32[16,16,256]{2,1,0:T(8,128)S(1)} collective-permute-done((f32[16,16,256]{2,1,0:T(8,128)S(1)}, f32[16,16,256]{2,1,0:T(8,128)S(1)}, u32[]{:S(2)}, u32[]{:S(2)}) %collective-permute-start.37) | collective-permute-done | bytes 262176 | tf_op jit(solution)/shard_map/ppermute | solution.py:415
  131.4 2.8 %collective-permute-start.43 = (f32[8,16,256]{2,1,0:T(8,128)S(1)}, f32[8,16,256]{2,1,0:T(8,128)S(1)}, u32[]{:S(2)}, u32[]{:S(2)}) collective-permute-start(f32[8,16,256]{2,1,0:T(8,128)S(1)} %get-tuple-element.153.refs_0_), channel_id=1, source_target_pairs={{0,4},{4,0},{8,12},{12,8},{1,5},{5,1},{9,13},{13,9},{2,6},{6,2},{1... | collective-permute-start | bytes 393224 | tf_op jit(solution)/shard_map/ppermute | solution.py:461
  135.2 2.3 %shard_map.112.refs_0_ = f32[16,32,512]{2,1,0:T(8,128)} custom-call(s32[16]{0:T(128)S(1)} %get-tuple-element.184.recv_pos, f32[8,16,256]{2,1,0:T(8,128)S(1)} %get-tuple-element.153.refs_0_, f32[16,16,512]{2,1,0:T(8,128)S(1)} %get-tuple-element.154.refs_1_, f32[16,16,256]{2,1,0:T(8,128)S(1)} %get-tuple-element.155.refs_2_, ...), custom_call_target="tpu_custom_call" | custom-call | flops 805306368 | tf_op jit(solution)/shard_map/pallas_call | solution.py:474
  138.1 7.6 %collective-permute-done.42.refs_4_ = f32[8,16,256]{2,1,0:T(8,128)S(1)} collective-permute-done((f32[8,16,256]{2,1,0:T(8,128)S(1)}, f32[8,16,256]{2,1,0:T(8,128)S(1)}, u32[]{:S(2)}, u32[]{:S(2)}) %collective-permute-start.42) | collective-permute-done | bytes 131104 | tf_op jit(solution)/shard_map/ppermute | solution.py:461
  145.8 2.3 %shard_map.113 = f32[16,32,512]{2,1,0:T(8,128)} custom-call(s32[16]{0:T(128)S(1)} %get-tuple-element.184.recv_pos, f32[16,32,512]{2,1,0:T(8,128)} %shard_map.112.refs_0_, f32[16,16,512]{2,1,0:T(8,128)S(1)} %get-tuple-element.159.refs_1_, f32[16,16,256]{2,1,0:T(8,128)S(1)} %get-tuple-element.160.refs_2_, ...), custom_call_target="tpu_custom_call", output_to_operand_aliasing={{}: (1, {})} | custom-call | flops 805306368 | tf_op jit(solution)/shard_map/pallas_call | solution.py:474
  (133 shorter events, 52.0 us)
Async XLA Ops:
  0.0 10.4 %collective-permute-start.1 = (f32[64,128,128]{2,1,0:T(8,128)}, f32[64,128,128]{2,1,0:T(8,128)}, u32[]{:S(2)}, u32[]{:S(2)}) collective-permute-start(f32[64,128,128]{2,1,0:T(8,128)} %bitcast.49), channel_id=1, source_target_pairs={{0,1},{1,0},{2,3},{3,2},{4,5},{5,4},{6,7},{7,6},{8,9},{9,8},{10,11... | collective-permute-start | bytes 12582920 | tf_op jit(solution)/shard_map/ppermute | solution.py:300
  3.6 15.2 %collective-permute-start.3 = (f32[16,16,256]{2,1,0:T(8,128)}, f32[16,16,256]{2,1,0:T(8,128)S(1)}, u32[]{:S(2)}, u32[]{:S(2)}) collective-permute-start(f32[16,16,256]{2,1,0:T(8,128)} %get-tuple-element.94.refs_1_), channel_id=1, source_target_pairs={{0,1},{1,0},{2,3},{3,2},{4,5},{5,4},{6,7},{7,6},{8,9},{9,8},{10,11... | collective-permute-start | bytes 786440 | tf_op jit(solution)/shard_map/ppermute | solution.py:379
  3.7 16.8 %collective-permute-start.4 = (f32[16,16,256]{2,1,0:T(8,128)}, f32[16,16,256]{2,1,0:T(8,128)S(1)}, u32[]{:S(2)}, u32[]{:S(2)}) collective-permute-start(f32[16,16,256]{2,1,0:T(8,128)} %get-tuple-element.94.refs_1_), channel_id=1, source_target_pairs={{0,2},{2,0},{1,3},{3,1},{4,6},{6,4},{5,7},{7,5},{8,10},{10,8},{9,1... | collective-permute-start | bytes 786440 | tf_op jit(solution)/shard_map/ppermute | solution.py:378
  7.6 11.1 %collective-permute-start.2 = (f32[16,16,256]{2,1,0:T(8,128)}, f32[16,16,256]{2,1,0:T(8,128)S(1)}, u32[]{:S(2)}, u32[]{:S(2)}) collective-permute-start(f32[16,16,256]{2,1,0:T(8,128)} %get-tuple-element.93.refs_0_), channel_id=1, source_target_pairs={{0,1},{1,0},{2,3},{3,2},{4,5},{5,4},{6,7},{7,6},{8,9},{9,8},{10,11... | collective-permute-start | bytes 786440 | tf_op jit(solution)/shard_map/ppermute | solution.py:379
  8.8 11.7 %collective-permute-start.5 = (f32[16,16,256]{2,1,0:T(8,128)}, f32[16,16,256]{2,1,0:T(8,128)S(1)}, u32[]{:S(2)}, u32[]{:S(2)}) collective-permute-start(f32[16,16,256]{2,1,0:T(8,128)} %get-tuple-element.93.refs_0_), channel_id=1, source_target_pairs={{0,2},{2,0},{1,3},{3,1},{4,6},{6,4},{5,7},{7,5},{8,10},{10,8},{9,1... | collective-permute-start | bytes 786440 | tf_op jit(solution)/shard_map/ppermute | solution.py:378
  25.5 13.4 %collective-permute-start.14 = (f32[16,16,256]{2,1,0:T(8,128)S(1)}, f32[16,16,256]{2,1,0:T(8,128)S(1)}, u32[]{:S(2)}, u32[]{:S(2)}) collective-permute-start(f32[16,16,256]{2,1,0:T(8,128)S(1)} %bitcast.56), channel_id=1, source_target_pairs={{0,2},{2,0},{1,3},{3,1},{4,6},{6,4},{5,7},{7,5},{8,10},{10,8},{9,1... | collective-permute-start | bytes 786440 | tf_op jit(solution)/shard_map/ppermute | solution.py:415
  34.0 30.5 %collective-permute-start.10 = (f32[65,16,128]{2,1,0:T(8,128)S(1)}, f32[65,16,128]{2,1,0:T(8,128)S(1)}, u32[]{:S(2)}, u32[]{:S(2)}) collective-permute-start(f32[65,16,128]{2,1,0:T(8,128)S(1)} %get-tuple-element.111), channel_id=1, source_target_pairs={{0,3},{1,2},{2,1},{3,0},{4,7},{5,6},{6,5},{7,4},{8,11},{9,10},{10,... | collective-permute-start | bytes 1597448 | tf_op jit(solution)/shard_map/ppermute | solution.py:441
  35.4 30.1 %collective-permute-start.9 = (f32[65,16,128]{2,1,0:T(8,128)S(1)}, f32[65,16,128]{2,1,0:T(8,128)S(1)}, u32[]{:S(2)}, u32[]{:S(2)}) collective-permute-start(f32[65,16,128]{2,1,0:T(8,128)S(1)} %get-tuple-element.110), channel_id=1, source_target_pairs={{0,2},{1,3},{2,0},{3,1},{4,6},{5,7},{6,4},{7,5},{8,10},{9,11},{10,... | collective-permute-start | bytes 1597448 | tf_op jit(solution)/shard_map/ppermute | solution.py:441
  43.3 15.0 %collective-permute-start.16 = (f32[8,16,256]{2,1,0:T(8,128)S(1)}, f32[8,16,256]{2,1,0:T(8,128)S(1)}, u32[]{:S(2)}, u32[]{:S(2)}) collective-permute-start(f32[8,16,256]{2,1,0:T(8,128)S(1)} %get-tuple-element.124), channel_id=1, source_target_pairs={{0,8},{4,12},{8,0},{12,4},{1,9},{5,13},{9,1},{13,5},{2,10},{6,14},... | collective-permute-start | bytes 393224 | tf_op jit(solution)/shard_map/ppermute | solution.py:461
  43.3 15.0 %collective-permute-start.17 = (f32[8,16,256]{2,1,0:T(8,128)S(1)}, f32[8,16,256]{2,1,0:T(8,128)S(1)}, u32[]{:S(2)}, u32[]{:S(2)}) collective-permute-start(f32[8,16,256]{2,1,0:T(8,128)S(1)} %get-tuple-element.125), channel_id=1, source_target_pairs={{0,4},{4,0},{8,12},{12,8},{1,5},{5,1},{9,13},{13,9},{2,6},{6,2},{1... | collective-permute-start | bytes 393224 | tf_op jit(solution)/shard_map/ppermute | solution.py:461
  47.6 21.8 %collective-permute-start.11 = (f32[8,16,256]{2,1,0:T(8,128)S(1)}, f32[8,16,256]{2,1,0:T(8,128)S(1)}, u32[]{:S(2)}, u32[]{:S(2)}) collective-permute-start(f32[8,16,256]{2,1,0:T(8,128)S(1)} %get-tuple-element.113), channel_id=1, source_target_pairs={{0,12},{4,8},{8,4},{12,0},{1,13},{5,9},{9,5},{13,1},{2,14},{6,10},... | collective-permute-start | bytes 393224 | tf_op jit(solution)/shard_map/ppermute | solution.py:461
  58.2 11.2 %collective-permute-start.12 = (f32[8,16,256]{2,1,0:T(8,128)S(1)}, f32[8,16,256]{2,1,0:T(8,128)S(1)}, u32[]{:S(2)}, u32[]{:S(2)}) collective-permute-start(f32[8,16,256]{2,1,0:T(8,128)S(1)} %get-tuple-element.114), channel_id=1, source_target_pairs={{0,8},{4,12},{8,0},{12,4},{1,9},{5,13},{9,1},{13,5},{2,10},{6,14},... | collective-permute-start | bytes 393224 | tf_op jit(solution)/shard_map/ppermute | solution.py:461
  58.2 11.2 %collective-permute-start.13 = (f32[8,16,256]{2,1,0:T(8,128)S(1)}, f32[8,16,256]{2,1,0:T(8,128)S(1)}, u32[]{:S(2)}, u32[]{:S(2)}) collective-permute-start(f32[8,16,256]{2,1,0:T(8,128)S(1)} %get-tuple-element.115.refs_0_), channel_id=1, source_target_pairs={{0,4},{4,0},{8,12},{12,8},{1,5},{5,1},{9,13},{13,9},{2,6},{6,2},{1... | collective-permute-start | bytes 393224 | tf_op jit(solution)/shard_map/ppermute | solution.py:461
  82.5 9.7 %collective-permute-start.25 = (f32[8,16,256]{2,1,0:T(8,128)S(1)}, f32[8,16,256]{2,1,0:T(8,128)S(1)}, u32[]{:S(2)}, u32[]{:S(2)}) collective-permute-start(f32[8,16,256]{2,1,0:T(8,128)S(1)} %get-tuple-element.137), channel_id=1, source_target_pairs={{0,12},{4,8},{8,4},{12,0},{1,13},{5,9},{9,5},{13,1},{2,14},{6,10},... | collective-permute-start | bytes 393224 | tf_op jit(solution)/shard_map/ppermute | solution.py:461
  82.8 19.5 %collective-permute-start.26 = (f32[8,16,256]{2,1,0:T(8,128)S(1)}, f32[8,16,256]{2,1,0:T(8,128)S(1)}, u32[]{:S(2)}, u32[]{:S(2)}) collective-permute-start(f32[8,16,256]{2,1,0:T(8,128)S(1)} %get-tuple-element.138), channel_id=1, source_target_pairs={{0,8},{4,12},{8,0},{12,4},{1,9},{5,13},{9,1},{13,5},{2,10},{6,14},... | collective-permute-start | bytes 393224 | tf_op jit(solution)/shard_map/ppermute | solution.py:461
  83.9 18.4 %collective-permute-start.27 = (f32[8,16,256]{2,1,0:T(8,128)S(1)}, f32[8,16,256]{2,1,0:T(8,128)S(1)}, u32[]{:S(2)}, u32[]{:S(2)}) collective-permute-start(f32[8,16,256]{2,1,0:T(8,128)S(1)} %get-tuple-element.139), channel_id=1, source_target_pairs={{0,4},{4,0},{8,12},{12,8},{1,5},{5,1},{9,13},{13,9},{2,6},{6,2},{1... | collective-permute-start | bytes 393224 | tf_op jit(solution)/shard_map/ppermute | solution.py:461
  90.8 14.6 %collective-permute-start.28 = (f32[8,16,256]{2,1,0:T(8,128)S(1)}, f32[8,16,256]{2,1,0:T(8,128)S(1)}, u32[]{:S(2)}, u32[]{:S(2)}) collective-permute-start(f32[8,16,256]{2,1,0:T(8,128)S(1)} %get-tuple-element.143), channel_id=1, source_target_pairs={{0,12},{4,8},{8,4},{12,0},{1,13},{5,9},{9,5},{13,1},{2,14},{6,10},... | collective-permute-start | bytes 393224 | tf_op jit(solution)/shard_map/ppermute | solution.py:461
  91.1 16.1 %collective-permute-start.29 = (f32[8,16,256]{2,1,0:T(8,128)S(1)}, f32[8,16,256]{2,1,0:T(8,128)S(1)}, u32[]{:S(2)}, u32[]{:S(2)}) collective-permute-start(f32[8,16,256]{2,1,0:T(8,128)S(1)} %get-tuple-element.144), channel_id=1, source_target_pairs={{0,8},{4,12},{8,0},{12,4},{1,9},{5,13},{9,1},{13,5},{2,10},{6,14},... | collective-permute-start | bytes 393224 | tf_op jit(solution)/shard_map/ppermute | solution.py:461
  92.2 15.0 %collective-permute-start.30 = (f32[8,16,256]{2,1,0:T(8,128)S(1)}, f32[8,16,256]{2,1,0:T(8,128)S(1)}, u32[]{:S(2)}, u32[]{:S(2)}) collective-permute-start(f32[8,16,256]{2,1,0:T(8,128)S(1)} %get-tuple-element.134.refs_0_), channel_id=1, source_target_pairs={{0,4},{4,0},{8,12},{12,8},{1,5},{5,1},{9,13},{13,9},{2,6},{6,2},{1... | collective-permute-start | bytes 393224 | tf_op jit(solution)/shard_map/ppermute | solution.py:461
  121.4 9.9 %collective-permute-start.38 = (f32[8,16,256]{2,1,0:T(8,128)S(1)}, f32[8,16,256]{2,1,0:T(8,128)S(1)}, u32[]{:S(2)}, u32[]{:S(2)}) collective-permute-start(f32[8,16,256]{2,1,0:T(8,128)S(1)} %get-tuple-element.156), channel_id=1, source_target_pairs={{0,12},{4,8},{8,4},{12,0},{1,13},{5,9},{9,5},{13,1},{2,14},{6,10},... | collective-permute-start | bytes 393224 | tf_op jit(solution)/shard_map/ppermute | solution.py:461
  122.8 12.4 %collective-permute-start.39 = (f32[8,16,256]{2,1,0:T(8,128)S(1)}, f32[8,16,256]{2,1,0:T(8,128)S(1)}, u32[]{:S(2)}, u32[]{:S(2)}) collective-permute-start(f32[8,16,256]{2,1,0:T(8,128)S(1)} %get-tuple-element.157), channel_id=1, source_target_pairs={{0,8},{4,12},{8,0},{12,4},{1,9},{5,13},{9,1},{13,5},{2,10},{6,14},... | collective-permute-start | bytes 393224 | tf_op jit(solution)/shard_map/ppermute | solution.py:461
  122.8 12.4 %collective-permute-start.40 = (f32[8,16,256]{2,1,0:T(8,128)S(1)}, f32[8,16,256]{2,1,0:T(8,128)S(1)}, u32[]{:S(2)}, u32[]{:S(2)}) collective-permute-start(f32[8,16,256]{2,1,0:T(8,128)S(1)} %get-tuple-element.158), channel_id=1, source_target_pairs={{0,4},{4,0},{8,12},{12,8},{1,5},{5,1},{9,13},{13,9},{2,6},{6,2},{1... | collective-permute-start | bytes 393224 | tf_op jit(solution)/shard_map/ppermute | solution.py:461
  131.4 14.4 %collective-permute-start.42 = (f32[8,16,256]{2,1,0:T(8,128)S(1)}, f32[8,16,256]{2,1,0:T(8,128)S(1)}, u32[]{:S(2)}, u32[]{:S(2)}) collective-permute-start(f32[8,16,256]{2,1,0:T(8,128)S(1)} %get-tuple-element.162), channel_id=1, source_target_pairs={{0,8},{4,12},{8,0},{12,4},{1,9},{5,13},{9,1},{13,5},{2,10},{6,14},... | collective-permute-start | bytes 393224 | tf_op jit(solution)/shard_map/ppermute | solution.py:461
  131.4 14.4 %collective-permute-start.43 = (f32[8,16,256]{2,1,0:T(8,128)S(1)}, f32[8,16,256]{2,1,0:T(8,128)S(1)}, u32[]{:S(2)}, u32[]{:S(2)}) collective-permute-start(f32[8,16,256]{2,1,0:T(8,128)S(1)} %get-tuple-element.153.refs_0_), channel_id=1, source_target_pairs={{0,4},{4,0},{8,12},{12,8},{1,5},{5,1},{9,13},{13,9},{2,6},{6,2},{1... | collective-permute-start | bytes 393224 | tf_op jit(solution)/shard_map/ppermute | solution.py:461
  (31 other events, 227.1 us)

commit v5 on v4

--- a/solution.py
+++ b/solution.py
@@ -389,6 +389,8 @@
             for r in range(n):
                 if layer == 0:
                     got[r], sides[0] = lax.optimization_barrier((got[r], sides[0]))
+                elif layer == 1 and r == n - 1:
+                    got[r], first = lax.optimization_barrier((got[r], first))
         far = sum((got + [lax.ppermute(low, "sub", swap) for low in got] for got in far), [])
         if whole:
             outs = [small(chunks[0][1])] + [jax.ShapeDtypeStruct((cap, chunks[0][1], width), F32)] * (edges - 1)
@@ -453,6 +455,7 @@
                 ],
                 moved=6 << 20,
             )(ids, edge_counts, notes[:, :-1], notes[:, -1], coef, coef2, *far)
+            fetched = far
         next_feats, next_lows = [None] * n, [None] * n
         result = None
         steps = list(range(edges - 1, 0, -1))
@@ -465,7 +468,7 @@
                 feat, feat_spec = feats[r], VMEM
             ahead = [packs[later][0] for later in order[i + 1 :]]
             if layer == 0 and i == n - 1:
-                ahead.append(first)
+                ahead.append(notes)
             alias = {}
             if last and result is not None:
                 alias = {1 + len(ahead): 0}

time: 148 us -> 146 us (0.986)
    ppermute x6, waiting for transfers between devices: 10.9 us -> 7.49 us  [local(): lax.ppermute(low, 'trip', turn(d))]
  transfers between devices with their start and end apart: 44 -> 44, of which waited for: 16 -> 19; matrix products, arithmetic and copies ran while one was open for 1% -> 1% of each run, Pallas kernels for 23% -> 24%
where the time goes in v5:
time: 146 us
  waiting for transfers between devices  52.5 us (36%)
  starting transfers between devices  45.5 us (31%)
  Pallas kernels  42.2 us (29%)
  local copies, waits for them, and re-layouts  2.58 us (2%)
  other arithmetic  1.79 us (1%)
    ppermute x18, starting transfers between devices, local(): lax.ppermute(packs[r][k - 1], 'edge', [(i, i ^ k) for i in range(edges)])  29.8 us
    ppermute x18, waiting for transfers between devices, local(): lax.ppermute(packs[r][k - 1], 'edge', [(i, i ^ k) for i in range(edges)])  29.4 us
    ppermute x4, waiting for transfers between devices, local(): lax.ppermute(sent[d - 1], 'trip', turn(d))  14.1 us
    pallas_call x6, Pallas kernels, local(): call(functools.partial(rows_kernel, (clusters, rc, cap, steps), last, len...  12.8 us
    ppermute x6, starting transfers between devices, local(): lax.ppermute(low, 'trip', turn(d))  8.33 us
    ppermute x6, waiting for transfers between devices, local(): lax.ppermute(low, 'trip', turn(d))  7.49 us
    pallas_call x1, Pallas kernels, local(): call(functools.partial(cells_kernel, (trips, subs, share, chunks, cluster...  6.25 us
    pallas_call x3, Pallas kernels, local(): call(functools.partial(far_kernel, n, len(far), cap, whole), [jax.ShapeDt...  5.2 us
  transfers between devices with their start and end apart: 44, of which 19 were waited for; matrix products, arithmetic and copies ran while one was open for 1% of the time, Pallas kernels for 24%

profile of v5, /device:TPU:0, one launch (start us, length us, event | category | flops | bytes accessed | tf_op | source)
XLA Modules:
  0.0 145.8 jit_solution(8648488777828404249)
XLA Ops:
  0.5 3.0 %shard_map.91 = (f32[16,16,256]{2,1,0:T(8,128)}, f32[16,16,256]{2,1,0:T(8,128)}) custom-call(f32[16,32,512]{2,1,0:T(8,128)} %refs_1_.3, f32[3,512,256]{2,1,0:T(8,128)} %down.1), custom_call_target="tpu_custom_call" | custom-call | flops 402653184 | tf_op jit(solution)/shard_map/pallas_call | solution.py:308
  3.7 3.0 %collective-permute-start.4 = (f32[16,16,256]{2,1,0:T(8,128)}, f32[16,16,256]{2,1,0:T(8,128)S(1)}, u32[]{:S(2)}, u32[]{:S(2)}) collective-permute-start(f32[16,16,256]{2,1,0:T(8,128)} %get-tuple-element.96.refs_1_), channel_id=1, source_target_pairs={{0,2},{2,0},{1,3},{3,1},{4,6},{6,4},{5,7},{7,5},{8,10},{10,8},{9,1... | collective-permute-start | bytes 786440 | tf_op jit(solution)/shard_map/ppermute | solution.py:378
  10.4 2.2 %copy-done = f32[1,1,64,128,128]{4,3,2,1,0:T(8,128)S(1)} copy-done((f32[1,1,64,128,128]{4,3,2,1,0:T(8,128)S(1)}, f32[1,1,64,128,128]{4,3,2,1,0:T(8,128)}, u32[]{:S(2)}) %copy-start) | copy-done | bytes 4194328
  12.6 6.3 %shard_map.92 = (bf16[512,2048]{1,0:T(8,128)(2,1)S(1)}, bf16[512,2048]{1,0:T(8,128)(2,1)S(1)}, bf16[512,2048]{1,0:T(8,128)(2,1)S(1)}, bf16[512,2048]{1,0:T(8,128...) custom-call(s32[2]{0:T(128)S(1)} %pad_add_fusion.3.ids, s32[16]{0:T(128)S(1)} %copy-done.5, ...), custom_call_target="tpu_custom_call" | custom-call | bytes 12582912 | tf_op jit(solution)/shard_map/pallas_call | solution.py:352
  28.0 5.5 %collective-permute-done.8.refs_0_ = f32[16,16,256]{2,1,0:T(8,128)S(1)} collective-permute-done((f32[16,16,256]{2,1,0:T(8,128)S(1)}, f32[16,16,256]{2,1,0:T(8,128)S(1)}, u32[]{:S(2)}, u32[]{:S(2)}) %collective-permute-start.8) | collective-permute-done | bytes 262176 | tf_op jit(solution)/shard_map/ppermute | solution.py:417
  35.5 3.6 %collective-permute-done.9.refs_0_ = f32[16,16,256]{2,1,0:T(8,128)S(1)} collective-permute-done((f32[16,16,256]{2,1,0:T(8,128)S(1)}, f32[16,16,256]{2,1,0:T(8,128)S(1)}, u32[]{:S(2)}, u32[]{:S(2)}) %collective-permute-start.9) | collective-permute-done | bytes 262176 | tf_op jit(solution)/shard_map/ppermute | solution.py:417
  39.7 3.4 %collective-permute-start.10 = (f32[8,16,256]{2,1,0:T(8,128)S(1)}, f32[8,16,256]{2,1,0:T(8,128)S(1)}, u32[]{:S(2)}, u32[]{:S(2)}) collective-permute-start(f32[8,16,256]{2,1,0:T(8,128)S(1)} %get-tuple-element.116), channel_id=1, source_target_pairs={{0,12},{4,8},{8,4},{12,0},{1,13},{5,9},{9,5},{13,1},{2,14},{6,10},... | collective-permute-start | bytes 393224 | tf_op jit(solution)/shard_map/ppermute | solution.py:464
  44.9 3.1 %collective-permute-done.10.refs_3_ = f32[8,16,256]{2,1,0:T(8,128)S(1)} collective-permute-done((f32[8,16,256]{2,1,0:T(8,128)S(1)}, f32[8,16,256]{2,1,0:T(8,128)S(1)}, u32[]{:S(2)}, u32[]{:S(2)}) %collective-permute-start.10) | collective-permute-done | bytes 131104 | tf_op jit(solution)/shard_map/ppermute | solution.py:464
  48.0 3.3 %collective-permute-start.16 = (f32[8,16,256]{2,1,0:T(8,128)S(1)}, f32[8,16,256]{2,1,0:T(8,128)S(1)}, u32[]{:S(2)}, u32[]{:S(2)}) collective-permute-start(f32[8,16,256]{2,1,0:T(8,128)S(1)} %get-tuple-element.127), channel_id=1, source_target_pairs={{0,12},{4,8},{8,4},{12,0},{1,13},{5,9},{9,5},{13,1},{2,14},{6,10},... | collective-permute-start | bytes 393224 | tf_op jit(solution)/shard_map/ppermute | solution.py:464
  51.3 7.0 %collective-permute-done.11.refs_4_ = f32[8,16,256]{2,1,0:T(8,128)S(1)} collective-permute-done((f32[8,16,256]{2,1,0:T(8,128)S(1)}, f32[8,16,256]{2,1,0:T(8,128)S(1)}, u32[]{:S(2)}, u32[]{:S(2)}) %collective-permute-start.11) | collective-permute-done | bytes 131104 | tf_op jit(solution)/shard_map/ppermute | solution.py:464
  58.3 3.8 %collective-permute-start.18 = (f32[8,16,256]{2,1,0:T(8,128)S(1)}, f32[8,16,256]{2,1,0:T(8,128)S(1)}, u32[]{:S(2)}, u32[]{:S(2)}) collective-permute-start(f32[8,16,256]{2,1,0:T(8,128)S(1)} %get-tuple-element.112.refs_0_), channel_id=1, source_target_pairs={{0,4},{4,0},{8,12},{12,8},{1,5},{5,1},{9,13},{13,9},{2,6},{6,2},{1... | collective-permute-start | bytes 393224 | tf_op jit(solution)/shard_map/ppermute | solution.py:464
  69.6 3.6 %shard_map.100.one = bf16[512,2048]{1,0:T(8,128)(2,1)S(1)} custom-call(s32[2]{0:T(128)S(1)} %pad_add_fusion.3.ids, s32[16]{0:T(128)S(1)} %copy-done.5, s32[4,128]{1,0:T(4,128)S(1)} %slice.70.pats, s32[4]{0:T(128)S(1)} %slice_reduce_fusion.live, f32[64,128,128]{2,1,0:T(8,128)S(1)} %bitcast.51, f32[64,128,128]{2,1,0:T(8,128)} %collective-permute-done.1.theirs, ...), custom_call_target="tpu_custom_call" | custom-call | bytes 6291456 | tf_op jit(solution)/shard_map/pallas_call | solution.py:446
  78.8 2.3 %collective-permute-start.25 = (f32[8,16,256]{2,1,0:T(8,128)S(1)}, f32[8,16,256]{2,1,0:T(8,128)S(1)}, u32[]{:S(2)}, u32[]{:S(2)}) collective-permute-start(f32[8,16,256]{2,1,0:T(8,128)S(1)} %get-tuple-element.141), channel_id=1, source_target_pairs={{0,12},{4,8},{8,4},{12,0},{1,13},{5,9},{9,5},{13,1},{2,14},{6,10},... | collective-permute-start | bytes 393224 | tf_op jit(solution)/shard_map/ppermute | solution.py:464
  84.2 2.5 %collective-permute-done.24.refs_0_ = f32[16,16,256]{2,1,0:T(8,128)S(1)} collective-permute-done((f32[16,16,256]{2,1,0:T(8,128)S(1)}, f32[16,16,256]{2,1,0:T(8,128)S(1)}, u32[]{:S(2)}, u32[]{:S(2)}) %collective-permute-start.24) | collective-permute-done | bytes 262176 | tf_op jit(solution)/shard_map/ppermute | solution.py:417
  87.3 2.4 %collective-permute-start.28 = (f32[8,16,256]{2,1,0:T(8,128)S(1)}, f32[8,16,256]{2,1,0:T(8,128)S(1)}, u32[]{:S(2)}, u32[]{:S(2)}) collective-permute-start(f32[8,16,256]{2,1,0:T(8,128)S(1)} %get-tuple-element.147), channel_id=1, source_target_pairs={{0,12},{4,8},{8,4},{12,0},{1,13},{5,9},{9,5},{13,1},{2,14},{6,10},... | collective-permute-start | bytes 393224 | tf_op jit(solution)/shard_map/ppermute | solution.py:464
  89.9 2.3 %collective-permute-start.30 = (f32[8,16,256]{2,1,0:T(8,128)S(1)}, f32[8,16,256]{2,1,0:T(8,128)S(1)}, u32[]{:S(2)}, u32[]{:S(2)}) collective-permute-start(f32[8,16,256]{2,1,0:T(8,128)S(1)} %get-tuple-element.138.refs_0_), channel_id=1, source_target_pairs={{0,4},{4,0},{8,12},{12,8},{1,5},{5,1},{9,13},{13,9},{2,6},{6,2},{1... | collective-permute-start | bytes 393224 | tf_op jit(solution)/shard_map/ppermute | solution.py:464
  92.2 7.8 %collective-permute-done.26.refs_4_ = f32[8,16,256]{2,1,0:T(8,128)S(1)} collective-permute-done((f32[8,16,256]{2,1,0:T(8,128)S(1)}, f32[8,16,256]{2,1,0:T(8,128)S(1)}, u32[]{:S(2)}, u32[]{:S(2)}) %collective-permute-start.26) | collective-permute-done | bytes 131104 | tf_op jit(solution)/shard_map/ppermute | solution.py:464
  109.1 5.6 %collective-permute-done.34.refs_1_ = f32[16,16,256]{2,1,0:T(8,128)S(1)} collective-permute-done((f32[16,16,256]{2,1,0:T(8,128)S(1)}, f32[16,16,256]{2,1,0:T(8,128)S(1)}, u32[]{:S(2)}, u32[]{:S(2)}) %collective-permute-start.34) | collective-permute-done | bytes 262176 | tf_op jit(solution)/shard_map/ppermute | solution.py:378
  121.3 2.2 %collective-permute-start.40 = (f32[8,16,256]{2,1,0:T(8,128)S(1)}, f32[8,16,256]{2,1,0:T(8,128)S(1)}, u32[]{:S(2)}, u32[]{:S(2)}) collective-permute-start(f32[8,16,256]{2,1,0:T(8,128)S(1)} %get-tuple-element.162), channel_id=1, source_target_pairs={{0,4},{4,0},{8,12},{12,8},{1,5},{5,1},{9,13},{13,9},{2,6},{6,2},{1... | collective-permute-start | bytes 393224 | tf_op jit(solution)/shard_map/ppermute | solution.py:464
  124.5 2.5 %collective-permute-done.37.refs_0_ = f32[16,16,256]{2,1,0:T(8,128)S(1)} collective-permute-done((f32[16,16,256]{2,1,0:T(8,128)S(1)}, f32[16,16,256]{2,1,0:T(8,128)S(1)}, u32[]{:S(2)}, u32[]{:S(2)}) %collective-permute-start.37) | collective-permute-done | bytes 262176 | tf_op jit(solution)/shard_map/ppermute | solution.py:417
  129.5 2.5 %collective-permute-start.43 = (f32[8,16,256]{2,1,0:T(8,128)S(1)}, f32[8,16,256]{2,1,0:T(8,128)S(1)}, u32[]{:S(2)}, u32[]{:S(2)}) collective-permute-start(f32[8,16,256]{2,1,0:T(8,128)S(1)} %get-tuple-element.157.refs_0_), channel_id=1, source_target_pairs={{0,4},{4,0},{8,12},{12,8},{1,5},{5,1},{9,13},{13,9},{2,6},{6,2},{1... | collective-permute-start | bytes 393224 | tf_op jit(solution)/shard_map/ppermute | solution.py:464
  132.8 2.3 %shard_map.112.refs_0_ = f32[16,32,512]{2,1,0:T(8,128)} custom-call(s32[16]{0:T(128)S(1)} %get-tuple-element.188.recv_pos, f32[8,16,256]{2,1,0:T(8,128)S(1)} %get-tuple-element.157.refs_0_, f32[16,16,512]{2,1,0:T(8,128)S(1)} %get-tuple-element.158.refs_1_, f32[16,16,256]{2,1,0:T(8,128)S(1)} %get-tuple-element.159.refs_2_, ...), custom_call_target="tpu_custom_call" | custom-call | flops 805306368 | tf_op jit(solution)/shard_map/pallas_call | solution.py:477
  136.0 7.5 %collective-permute-done.42.refs_4_ = f32[8,16,256]{2,1,0:T(8,128)S(1)} collective-permute-done((f32[8,16,256]{2,1,0:T(8,128)S(1)}, f32[8,16,256]{2,1,0:T(8,128)S(1)}, u32[]{:S(2)}, u32[]{:S(2)}) %collective-permute-start.42) | collective-permute-done | bytes 131104 | tf_op jit(solution)/shard_map/ppermute | solution.py:464
  143.5 2.3 %shard_map.113 = f32[16,32,512]{2,1,0:T(8,128)} custom-call(s32[16]{0:T(128)S(1)} %get-tuple-element.188.recv_pos, f32[16,32,512]{2,1,0:T(8,128)} %shard_map.112.refs_0_, f32[16,16,512]{2,1,0:T(8,128)S(1)} %get-tuple-element.163.refs_1_, f32[16,16,256]{2,1,0:T(8,128)S(1)} %get-tuple-element.164.refs_2_, ...), custom_call_target="tpu_custom_call", output_to_operand_aliasing={{}: (1, {})} | custom-call | flops 805306368 | tf_op jit(solution)/shard_map/pallas_call | solution.py:477
  (133 shorter events, 54.6 us)
Async XLA Ops:
  0.0 10.4 %collective-permute-start.1 = (f32[64,128,128]{2,1,0:T(8,128)}, f32[64,128,128]{2,1,0:T(8,128)}, u32[]{:S(2)}, u32[]{:S(2)}) collective-permute-start(f32[64,128,128]{2,1,0:T(8,128)} %bitcast.49), channel_id=1, source_target_pairs={{0,1},{1,0},{2,3},{3,2},{4,5},{5,4},{6,7},{7,6},{8,9},{9,8},{10,11... | collective-permute-start | bytes 12582920 | tf_op jit(solution)/shard_map/ppermute | solution.py:300
  3.6 15.3 %collective-permute-start.3 = (f32[16,16,256]{2,1,0:T(8,128)}, f32[16,16,256]{2,1,0:T(8,128)S(1)}, u32[]{:S(2)}, u32[]{:S(2)}) collective-permute-start(f32[16,16,256]{2,1,0:T(8,128)} %get-tuple-element.96.refs_1_), channel_id=1, source_target_pairs={{0,1},{1,0},{2,3},{3,2},{4,5},{5,4},{6,7},{7,6},{8,9},{9,8},{10,11... | collective-permute-start | bytes 786440 | tf_op jit(solution)/shard_map/ppermute | solution.py:379
  3.7 16.9 %collective-permute-start.4 = (f32[16,16,256]{2,1,0:T(8,128)}, f32[16,16,256]{2,1,0:T(8,128)S(1)}, u32[]{:S(2)}, u32[]{:S(2)}) collective-permute-start(f32[16,16,256]{2,1,0:T(8,128)} %get-tuple-element.96.refs_1_), channel_id=1, source_target_pairs={{0,2},{2,0},{1,3},{3,1},{4,6},{6,4},{5,7},{7,5},{8,10},{10,8},{9,1... | collective-permute-start | bytes 786440 | tf_op jit(solution)/shard_map/ppermute | solution.py:378
  7.6 11.2 %collective-permute-start.2 = (f32[16,16,256]{2,1,0:T(8,128)}, f32[16,16,256]{2,1,0:T(8,128)S(1)}, u32[]{:S(2)}, u32[]{:S(2)}) collective-permute-start(f32[16,16,256]{2,1,0:T(8,128)} %get-tuple-element.95.refs_0_), channel_id=1, source_target_pairs={{0,1},{1,0},{2,3},{3,2},{4,5},{5,4},{6,7},{7,6},{8,9},{9,8},{10,11... | collective-permute-start | bytes 786440 | tf_op jit(solution)/shard_map/ppermute | solution.py:379
  8.8 11.8 %collective-permute-start.5 = (f32[16,16,256]{2,1,0:T(8,128)}, f32[16,16,256]{2,1,0:T(8,128)S(1)}, u32[]{:S(2)}, u32[]{:S(2)}) collective-permute-start(f32[16,16,256]{2,1,0:T(8,128)} %get-tuple-element.95.refs_0_), channel_id=1, source_target_pairs={{0,2},{2,0},{1,3},{3,1},{4,6},{6,4},{5,7},{7,5},{8,10},{10,8},{9,1... | collective-permute-start | bytes 786440 | tf_op jit(solution)/shard_map/ppermute | solution.py:378
  24.2 9.2 %collective-permute-start.8 = (f32[16,16,256]{2,1,0:T(8,128)S(1)}, f32[16,16,256]{2,1,0:T(8,128)S(1)}, u32[]{:S(2)}, u32[]{:S(2)}) collective-permute-start(f32[16,16,256]{2,1,0:T(8,128)S(1)} %bitcast.59), channel_id=1, source_target_pairs={{0,2},{2,0},{1,3},{3,1},{4,6},{6,4},{5,7},{7,5},{8,10},{10,8},{9,1... | collective-permute-start | bytes 786440 | tf_op jit(solution)/shard_map/ppermute | solution.py:417
  25.4 13.7 %collective-permute-start.9 = (f32[16,16,256]{2,1,0:T(8,128)S(1)}, f32[16,16,256]{2,1,0:T(8,128)S(1)}, u32[]{:S(2)}, u32[]{:S(2)}) collective-permute-start(f32[16,16,256]{2,1,0:T(8,128)S(1)} %bitcast.56), channel_id=1, source_target_pairs={{0,2},{2,0},{1,3},{3,1},{4,6},{6,4},{5,7},{7,5},{8,10},{10,8},{9,1... | collective-permute-start | bytes 786440 | tf_op jit(solution)/shard_map/ppermute | solution.py:417
  34.1 30.1 %collective-permute-start.15 = (f32[65,16,128]{2,1,0:T(8,128)S(1)}, f32[65,16,128]{2,1,0:T(8,128)S(1)}, u32[]{:S(2)}, u32[]{:S(2)}) collective-permute-start(f32[65,16,128]{2,1,0:T(8,128)S(1)} %get-tuple-element.124), channel_id=1, source_target_pairs={{0,3},{1,2},{2,1},{3,0},{4,7},{5,6},{6,5},{7,4},{8,11},{9,10},{10,... | collective-permute-start | bytes 1597448 | tf_op jit(solution)/shard_map/ppermute | solution.py:443
  43.1 15.2 %collective-permute-start.11 = (f32[8,16,256]{2,1,0:T(8,128)S(1)}, f32[8,16,256]{2,1,0:T(8,128)S(1)}, u32[]{:S(2)}, u32[]{:S(2)}) collective-permute-start(f32[8,16,256]{2,1,0:T(8,128)S(1)} %get-tuple-element.117), channel_id=1, source_target_pairs={{0,8},{4,12},{8,0},{12,4},{1,9},{5,13},{9,1},{13,5},{2,10},{6,14},... | collective-permute-start | bytes 393224 | tf_op jit(solution)/shard_map/ppermute | solution.py:464
  43.1 15.2 %collective-permute-start.12 = (f32[8,16,256]{2,1,0:T(8,128)S(1)}, f32[8,16,256]{2,1,0:T(8,128)S(1)}, u32[]{:S(2)}, u32[]{:S(2)}) collective-permute-start(f32[8,16,256]{2,1,0:T(8,128)S(1)} %get-tuple-element.118), channel_id=1, source_target_pairs={{0,4},{4,0},{8,12},{12,8},{1,5},{5,1},{9,13},{13,9},{2,6},{6,2},{1... | collective-permute-start | bytes 393224 | tf_op jit(solution)/shard_map/ppermute | solution.py:464
  44.1 21.3 %collective-permute-start.14 = (f32[65,16,128]{2,1,0:T(8,128)S(1)}, f32[65,16,128]{2,1,0:T(8,128)S(1)}, u32[]{:S(2)}, u32[]{:S(2)}) collective-permute-start(f32[65,16,128]{2,1,0:T(8,128)S(1)} %get-tuple-element.123), channel_id=1, source_target_pairs={{0,2},{1,3},{2,0},{3,1},{4,6},{5,7},{6,4},{7,5},{8,10},{9,11},{10,... | collective-permute-start | bytes 1597448 | tf_op jit(solution)/shard_map/ppermute | solution.py:443
  48.0 17.5 %collective-permute-start.16 = (f32[8,16,256]{2,1,0:T(8,128)S(1)}, f32[8,16,256]{2,1,0:T(8,128)S(1)}, u32[]{:S(2)}, u32[]{:S(2)}) collective-permute-start(f32[8,16,256]{2,1,0:T(8,128)S(1)} %get-tuple-element.127), channel_id=1, source_target_pairs={{0,12},{4,8},{8,4},{12,0},{1,13},{5,9},{9,5},{13,1},{2,14},{6,10},... | collective-permute-start | bytes 393224 | tf_op jit(solution)/shard_map/ppermute | solution.py:464
  64.2 9.0 %collective-permute-start.13 = (f32[16,16,256]{2,1,0:T(8,128)S(1)}, f32[16,16,256]{2,1,0:T(8,128)S(1)}, u32[]{:S(2)}, u32[]{:S(2)}) collective-permute-start(f32[16,16,256]{2,1,0:T(8,128)S(1)} %get-tuple-element.122.refs_1_), channel_id=1, source_target_pairs={{0,2},{2,0},{1,3},{3,1},{4,6},{6,4},{5,7},{7,5},{8,10},{10,8},{9,1... | collective-permute-start | bytes 786440 | tf_op jit(solution)/shard_map/ppermute | solution.py:378
  78.8 11.1 %collective-permute-start.25 = (f32[8,16,256]{2,1,0:T(8,128)S(1)}, f32[8,16,256]{2,1,0:T(8,128)S(1)}, u32[]{:S(2)}, u32[]{:S(2)}) collective-permute-start(f32[8,16,256]{2,1,0:T(8,128)S(1)} %get-tuple-element.141), channel_id=1, source_target_pairs={{0,12},{4,8},{8,4},{12,0},{1,13},{5,9},{9,5},{13,1},{2,14},{6,10},... | collective-permute-start | bytes 393224 | tf_op jit(solution)/shard_map/ppermute | solution.py:464
  81.1 19.0 %collective-permute-start.26 = (f32[8,16,256]{2,1,0:T(8,128)S(1)}, f32[8,16,256]{2,1,0:T(8,128)S(1)}, u32[]{:S(2)}, u32[]{:S(2)}) collective-permute-start(f32[8,16,256]{2,1,0:T(8,128)S(1)} %get-tuple-element.142), channel_id=1, source_target_pairs={{0,8},{4,12},{8,0},{12,4},{1,9},{5,13},{9,1},{13,5},{2,10},{6,14},... | collective-permute-start | bytes 393224 | tf_op jit(solution)/shard_map/ppermute | solution.py:464
  81.7 18.4 %collective-permute-start.27 = (f32[8,16,256]{2,1,0:T(8,128)S(1)}, f32[8,16,256]{2,1,0:T(8,128)S(1)}, u32[]{:S(2)}, u32[]{:S(2)}) collective-permute-start(f32[8,16,256]{2,1,0:T(8,128)S(1)} %get-tuple-element.143), channel_id=1, source_target_pairs={{0,4},{4,0},{8,12},{12,8},{1,5},{5,1},{9,13},{13,9},{2,6},{6,2},{1... | collective-permute-start | bytes 393224 | tf_op jit(solution)/shard_map/ppermute | solution.py:464
  87.3 15.8 %collective-permute-start.28 = (f32[8,16,256]{2,1,0:T(8,128)S(1)}, f32[8,16,256]{2,1,0:T(8,128)S(1)}, u32[]{:S(2)}, u32[]{:S(2)}) collective-permute-start(f32[8,16,256]{2,1,0:T(8,128)S(1)} %get-tuple-element.147), channel_id=1, source_target_pairs={{0,12},{4,8},{8,4},{12,0},{1,13},{5,9},{9,5},{13,1},{2,14},{6,10},... | collective-permute-start | bytes 393224 | tf_op jit(solution)/shard_map/ppermute | solution.py:464
  89.7 15.3 %collective-permute-start.29 = (f32[8,16,256]{2,1,0:T(8,128)S(1)}, f32[8,16,256]{2,1,0:T(8,128)S(1)}, u32[]{:S(2)}, u32[]{:S(2)}) collective-permute-start(f32[8,16,256]{2,1,0:T(8,128)S(1)} %get-tuple-element.148), channel_id=1, source_target_pairs={{0,8},{4,12},{8,0},{12,4},{1,9},{5,13},{9,1},{13,5},{2,10},{6,14},... | collective-permute-start | bytes 393224 | tf_op jit(solution)/shard_map/ppermute | solution.py:464
  89.9 15.1 %collective-permute-start.30 = (f32[8,16,256]{2,1,0:T(8,128)S(1)}, f32[8,16,256]{2,1,0:T(8,128)S(1)}, u32[]{:S(2)}, u32[]{:S(2)}) collective-permute-start(f32[8,16,256]{2,1,0:T(8,128)S(1)} %get-tuple-element.138.refs_0_), channel_id=1, source_target_pairs={{0,4},{4,0},{8,12},{12,8},{1,5},{5,1},{9,13},{13,9},{2,6},{6,2},{1... | collective-permute-start | bytes 393224 | tf_op jit(solution)/shard_map/ppermute | solution.py:464
  119.1 10.4 %collective-permute-start.38 = (f32[8,16,256]{2,1,0:T(8,128)S(1)}, f32[8,16,256]{2,1,0:T(8,128)S(1)}, u32[]{:S(2)}, u32[]{:S(2)}) collective-permute-start(f32[8,16,256]{2,1,0:T(8,128)S(1)} %get-tuple-element.160), channel_id=1, source_target_pairs={{0,12},{4,8},{8,4},{12,0},{1,13},{5,9},{9,5},{13,1},{2,14},{6,10},... | collective-permute-start | bytes 393224 | tf_op jit(solution)/shard_map/ppermute | solution.py:464
  121.3 11.5 %collective-permute-start.39 = (f32[8,16,256]{2,1,0:T(8,128)S(1)}, f32[8,16,256]{2,1,0:T(8,128)S(1)}, u32[]{:S(2)}, u32[]{:S(2)}) collective-permute-start(f32[8,16,256]{2,1,0:T(8,128)S(1)} %get-tuple-element.161), channel_id=1, source_target_pairs={{0,8},{4,12},{8,0},{12,4},{1,9},{5,13},{9,1},{13,5},{2,10},{6,14},... | collective-permute-start | bytes 393224 | tf_op jit(solution)/shard_map/ppermute | solution.py:464
  121.3 11.5 %collective-permute-start.40 = (f32[8,16,256]{2,1,0:T(8,128)S(1)}, f32[8,16,256]{2,1,0:T(8,128)S(1)}, u32[]{:S(2)}, u32[]{:S(2)}) collective-permute-start(f32[8,16,256]{2,1,0:T(8,128)S(1)} %get-tuple-element.162), channel_id=1, source_target_pairs={{0,4},{4,0},{8,12},{12,8},{1,5},{5,1},{9,13},{13,9},{2,6},{6,2},{1... | collective-permute-start | bytes 393224 | tf_op jit(solution)/shard_map/ppermute | solution.py:464
  129.5 14.0 %collective-permute-start.42 = (f32[8,16,256]{2,1,0:T(8,128)S(1)}, f32[8,16,256]{2,1,0:T(8,128)S(1)}, u32[]{:S(2)}, u32[]{:S(2)}) collective-permute-start(f32[8,16,256]{2,1,0:T(8,128)S(1)} %get-tuple-element.166), channel_id=1, source_target_pairs={{0,8},{4,12},{8,0},{12,4},{1,9},{5,13},{9,1},{13,5},{2,10},{6,14},... | collective-permute-start | bytes 393224 | tf_op jit(solution)/shard_map/ppermute | solution.py:464
  129.5 14.0 %collective-permute-start.43 = (f32[8,16,256]{2,1,0:T(8,128)S(1)}, f32[8,16,256]{2,1,0:T(8,128)S(1)}, u32[]{:S(2)}, u32[]{:S(2)}) collective-permute-start(f32[8,16,256]{2,1,0:T(8,128)S(1)} %get-tuple-element.157.refs_0_), channel_id=1, source_target_pairs={{0,4},{4,0},{8,12},{12,8},{1,5},{5,1},{9,13},{13,9},{2,6},{6,2},{1... | collective-permute-start | bytes 393224 | tf_op jit(solution)/shard_map/ppermute | solution.py:464
  (31 other events, 207.9 us)

commit v6 on v5

--- a/solution.py
+++ b/solution.py
@@ -364,7 +364,7 @@
         ],
         moved=12 << 20,
     )(ids, edge_counts, note[:, :-1], note[:, -1], marks, coef, coef2)
-    near, remote, parts = cells[:n], cells[n : 2 * n], cells[2 * n :]
+    near, remote, parts = list(cells[:n]), cells[n : 2 * n], cells[2 * n :]
 
     feats, first = None, None
     for layer in range(layers):
@@ -388,7 +388,7 @@
         for got in far:
             for r in range(n):
                 if layer == 0:
-                    got[r], sides[0] = lax.optimization_barrier((got[r], sides[0]))
+                    got[r], near[0] = lax.optimization_barrier((got[r], near[0]))
                 elif layer == 1 and r == n - 1:
                     got[r], first = lax.optimization_barrier((got[r], first))
         far = sum((got + [lax.ppermute(low, "sub", swap) for low in got] for got in far), [])
@@ -458,7 +458,7 @@
             fetched = far
         next_feats, next_lows = [None] * n, [None] * n
         result = None
-        steps = list(range(edges - 1, 0, -1))
+        steps = sorted(range(1, edges), key=lambda k: (layer == 0 or k != edges // 2, -k))
         for i, r in enumerate(order):
             off, rc = chunks[r]
             back = [lax.ppermute(packs[r][k - 1], "edge", [(i, i ^ k) for i in range(edges)]) for k in steps]

time: 146 us -> 144 us (0.986)
  waiting for transfers between devices: 52.5 us -> 48 us
  starting transfers between devices: 45.5 us -> 47.7 us
    ppermute x18, waiting for transfers between devices: 29.4 us -> 26.7 us  [local(): lax.ppermute(packs[r][k - 1], 'edge', [(i, i ^ k) for i in range(edges)])]
    ppermute x18, starting transfers between devices: 29.8 us -> 31.8 us  [local(): lax.ppermute(packs[r][k - 1], 'edge', [(i, i ^ k) for i in range(edges)])]
  transfers between devices with their start and end apart: 44 -> 44, of which waited for: 19 -> 14; matrix products, arithmetic and copies ran while one was open for 1% -> 1% of each run, Pallas kernels for 24% -> 24%
where the time goes in v6:
time: 144 us
  waiting for transfers between devices  48 us (33%)
  starting transfers between devices  47.7 us (33%)
  Pallas kernels  42.4 us (29%)
  local copies, waits for them, and re-layouts  2.58 us (2%)
  other arithmetic  1.79 us (1%)
    ppermute x18, starting transfers between devices, local(): lax.ppermute(packs[r][k - 1], 'edge', [(i, i ^ k) for i in range(edges)])  31.8 us
    ppermute x18, waiting for transfers between devices, local(): lax.ppermute(packs[r][k - 1], 'edge', [(i, i ^ k) for i in range(edges)])  26.7 us
    ppermute x4, waiting for transfers between devices, local(): lax.ppermute(sent[d - 1], 'trip', turn(d))  13.1 us
    pallas_call x6, Pallas kernels, local(): call(functools.partial(rows_kernel, (clusters, rc, cap, steps), last, len...  12.9 us
    ppermute x6, waiting for transfers between devices, local(): lax.ppermute(low, 'trip', turn(d))  7.79 us
    ppermute x6, starting transfers between devices, local(): lax.ppermute(low, 'trip', turn(d))  7.38 us
    pallas_call x1, Pallas kernels, local(): call(functools.partial(cells_kernel, (trips, subs, share, chunks, cluster...  6.25 us
    pallas_call x3, Pallas kernels, local(): call(functools.partial(far_kernel, n, len(far), cap, whole), [jax.ShapeDt...  5.21 us
  transfers between devices with their start and end apart: 44, of which 14 were waited for; matrix products, arithmetic and copies ran while one was open for 1% of the time, Pallas kernels for 24%

profile of v6, /device:TPU:0, one launch (start us, length us, event | category | flops | bytes accessed | tf_op | source)
XLA Modules:
  0.0 143.7 jit_solution(14188194892272352009)
XLA Ops:
  0.5 3.0 %shard_map.91 = (f32[16,16,256]{2,1,0:T(8,128)}, f32[16,16,256]{2,1,0:T(8,128)}) custom-call(f32[16,32,512]{2,1,0:T(8,128)} %refs_1_.3, f32[3,512,256]{2,1,0:T(8,128)} %down.1), custom_call_target="tpu_custom_call" | custom-call | flops 402653184 | tf_op jit(solution)/shard_map/pallas_call | solution.py:308
  3.7 3.0 %collective-permute-start.4 = (f32[16,16,256]{2,1,0:T(8,128)}, f32[16,16,256]{2,1,0:T(8,128)S(1)}, u32[]{:S(2)}, u32[]{:S(2)}) collective-permute-start(f32[16,16,256]{2,1,0:T(8,128)} %get-tuple-element.95.refs_0_), channel_id=1, source_target_pairs={{0,2},{2,0},{1,3},{3,1},{4,6},{6,4},{5,7},{7,5},{8,10},{10,8},{9,1... | collective-permute-start | bytes 786440 | tf_op jit(solution)/shard_map/ppermute | solution.py:378
  9.1 2.2 %copy-done = f32[1,1,64,128,128]{4,3,2,1,0:T(8,128)S(1)} copy-done((f32[1,1,64,128,128]{4,3,2,1,0:T(8,128)S(1)}, f32[1,1,64,128,128]{4,3,2,1,0:T(8,128)}, u32[]{:S(2)}) %copy-start) | copy-done | bytes 4194328
  11.3 6.3 %shard_map.92 = (bf16[512,2048]{1,0:T(8,128)(2,1)S(1)}, bf16[512,2048]{1,0:T(8,128)(2,1)S(1)}, bf16[512,2048]{1,0:T(8,128)(2,1)S(1)}, bf16[512,2048]{1,0:T(8,128...) custom-call(s32[2]{0:T(128)S(1)} %pad_add_fusion.3.ids, s32[16]{0:T(128)S(1)} %copy-done.5, ...), custom_call_target="tpu_custom_call" | custom-call | bytes 12582912 | tf_op jit(solution)/shard_map/pallas_call | solution.py:352
  26.8 5.5 %collective-permute-done.8.refs_0_ = f32[16,16,256]{2,1,0:T(8,128)S(1)} collective-permute-done((f32[16,16,256]{2,1,0:T(8,128)S(1)}, f32[16,16,256]{2,1,0:T(8,128)S(1)}, u32[]{:S(2)}, u32[]{:S(2)}) %collective-permute-start.8) | collective-permute-done | bytes 262176 | tf_op jit(solution)/shard_map/ppermute | solution.py:417
  34.3 3.6 %collective-permute-done.9.refs_0_ = f32[16,16,256]{2,1,0:T(8,128)S(1)} collective-permute-done((f32[16,16,256]{2,1,0:T(8,128)S(1)}, f32[16,16,256]{2,1,0:T(8,128)S(1)}, u32[]{:S(2)}, u32[]{:S(2)}) %collective-permute-start.9) | collective-permute-done | bytes 262176 | tf_op jit(solution)/shard_map/ppermute | solution.py:417
  38.5 3.9 %collective-permute-start.10 = (f32[8,16,256]{2,1,0:T(8,128)S(1)}, f32[8,16,256]{2,1,0:T(8,128)S(1)}, u32[]{:S(2)}, u32[]{:S(2)}) collective-permute-start(f32[8,16,256]{2,1,0:T(8,128)S(1)} %get-tuple-element.116), channel_id=1, source_target_pairs={{0,12},{4,8},{8,4},{12,0},{1,13},{5,9},{9,5},{13,1},{2,14},{6,10},... | collective-permute-start | bytes 393224 | tf_op jit(solution)/shard_map/ppermute | solution.py:464
  46.5 4.2 %collective-permute-start.16 = (f32[8,16,256]{2,1,0:T(8,128)S(1)}, f32[8,16,256]{2,1,0:T(8,128)S(1)}, u32[]{:S(2)}, u32[]{:S(2)}) collective-permute-start(f32[8,16,256]{2,1,0:T(8,128)S(1)} %get-tuple-element.127), channel_id=1, source_target_pairs={{0,12},{4,8},{8,4},{12,0},{1,13},{5,9},{9,5},{13,1},{2,14},{6,10},... | collective-permute-start | bytes 393224 | tf_op jit(solution)/shard_map/ppermute | solution.py:464
  50.7 6.4 %collective-permute-done.11.refs_4_ = f32[8,16,256]{2,1,0:T(8,128)S(1)} collective-permute-done((f32[8,16,256]{2,1,0:T(8,128)S(1)}, f32[8,16,256]{2,1,0:T(8,128)S(1)}, u32[]{:S(2)}, u32[]{:S(2)}) %collective-permute-start.11) | collective-permute-done | bytes 131104 | tf_op jit(solution)/shard_map/ppermute | solution.py:464
  57.1 4.1 %collective-permute-start.18 = (f32[8,16,256]{2,1,0:T(8,128)S(1)}, f32[8,16,256]{2,1,0:T(8,128)S(1)}, u32[]{:S(2)}, u32[]{:S(2)}) collective-permute-start(f32[8,16,256]{2,1,0:T(8,128)S(1)} %get-tuple-element.112.refs_0_), channel_id=1, source_target_pairs={{0,4},{4,0},{8,12},{12,8},{1,5},{5,1},{9,13},{13,9},{2,6},{6,2},{1... | collective-permute-start | bytes 393224 | tf_op jit(solution)/shard_map/ppermute | solution.py:464
  61.2 2.0 %shard_map.99 = (f32[16,16,512]{2,1,0:T(8,128)S(1)}, f32[16,16,256]{2,1,0:T(8,128)S(1)}) custom-call(s32[16]{0:T(128)S(1)} %get-tuple-element.188.recv_pos, f32[8,16,256]{2,1,0:T(8,128)S(1)} %get-tuple-element.112.refs_0_, f32[16,32,512]{2,1,0:T(8,128)S(1)} %copy-done.2, f32[16,16,256]{2,1,0:T(8,128)S(1)} %get-tuple-element.115.refs_2_, ...), custom_call_target="tpu_custom_call" | custom-call | flops 805306368 | tf_op jit(solution)/shard_map/pallas_call | solution.py:477
  64.9 2.0 %shard_map.101 = (f32[16,16,512]{2,1,0:T(8,128)S(1)}, f32[16,16,256]{2,1,0:T(8,128)S(1)}) custom-call(s32[16]{0:T(128)S(1)} %get-tuple-element.188.recv_pos, s32[4,129]{1,0:T(4,128)S(1)} %pad_add_fusion.refs_0_, f32[16,32,512]{2,1,0:T(8,128)S(1)} %copy-done.2, f32[16,16,256]{2,1,0:T(8,128)S(1)} %get-tuple-element.126.refs_2_, ...), custom_call_target="tpu_custom_call" | custom-call | flops 805306368 | tf_op jit(solution)/shard_map/pallas_call | solution.py:477
  69.1 3.7 %shard_map.100.one = bf16[512,2048]{1,0:T(8,128)(2,1)S(1)} custom-call(s32[2]{0:T(128)S(1)} %pad_add_fusion.3.ids, s32[16]{0:T(128)S(1)} %copy-done.5, s32[4,128]{1,0:T(4,128)S(1)} %slice.70.pats, s32[4]{0:T(128)S(1)} %slice_reduce_fusion.live, f32[64,128,128]{2,1,0:T(8,128)S(1)} %bitcast.51, f32[64,128,128]{2,1,0:T(8,128)} %collective-permute-done.1.theirs, ...), custom_call_target="tpu_custom_call" | custom-call | bytes 6291456 | tf_op jit(solution)/shard_map/pallas_call | solution.py:446
  83.0 2.6 %collective-permute-done.24.refs_0_ = f32[16,16,256]{2,1,0:T(8,128)S(1)} collective-permute-done((f32[16,16,256]{2,1,0:T(8,128)S(1)}, f32[16,16,256]{2,1,0:T(8,128)S(1)}, u32[]{:S(2)}, u32[]{:S(2)}) %collective-permute-start.24) | collective-permute-done | bytes 262176 | tf_op jit(solution)/shard_map/ppermute | solution.py:417
  87.9 2.1 %collective-permute-start.29 = (f32[8,16,256]{2,1,0:T(8,128)S(1)}, f32[8,16,256]{2,1,0:T(8,128)S(1)}, u32[]{:S(2)}, u32[]{:S(2)}) collective-permute-start(f32[8,16,256]{2,1,0:T(8,128)S(1)} %get-tuple-element.148), channel_id=1, source_target_pairs={{0,12},{4,8},{8,4},{12,0},{1,13},{5,9},{9,5},{13,1},{2,14},{6,10},... | collective-permute-start | bytes 393224 | tf_op jit(solution)/shard_map/ppermute | solution.py:464
  91.9 2.1 %shard_map.106 = (f32[16,16,512]{2,1,0:T(8,128)S(1)}, f32[16,16,256]{2,1,0:T(8,128)S(1)}) custom-call(s32[16]{0:T(128)S(1)} %get-tuple-element.188.recv_pos, f32[8,16,256]{2,1,0:T(8,128)S(1)} %get-tuple-element.138.refs_0_, f32[16,16,512]{2,1,0:T(8,128)S(1)} %get-tuple-element.139.refs_1_, f32[16,16,256]{2,1,0:T(8,128)S(1)} %get-tuple-element.140.refs_2_, ...), custom_call_target="tpu_custom_call" | custom-call | flops 805306368 | tf_op jit(solution)/shard_map/pallas_call | solution.py:477
  94.6 7.9 %collective-permute-done.28.refs_2_ = f32[8,16,256]{2,1,0:T(8,128)S(1)} collective-permute-done((f32[8,16,256]{2,1,0:T(8,128)S(1)}, f32[8,16,256]{2,1,0:T(8,128)S(1)}, u32[]{:S(2)}, u32[]{:S(2)}) %collective-permute-start.28) | collective-permute-done | bytes 131104 | tf_op jit(solution)/shard_map/ppermute | solution.py:464
  102.5 2.1 %shard_map.107 = (f32[16,16,512]{2,1,0:T(8,128)S(1)}, f32[16,16,256]{2,1,0:T(8,128)S(1)}) custom-call(s32[16]{0:T(128)S(1)} %get-tuple-element.188.recv_pos, f32[16,16,512]{2,1,0:T(8,128)S(1)} %get-tuple-element.145.refs_0_, f32[16,16,256]{2,1,0:T(8,128)S(1)} %get-tuple-element.146.refs_1_, f32[8,16,256]{2,1,0:T(8,128)S(1)} %collective-permute-done.28.refs_2_, ...), custom_call_target="tpu_custom_call" | custom-call | flops 805306368 | tf_op jit(solution)/shard_map/pallas_call | solution.py:477
  105.7 5.8 %collective-permute-done.34.refs_1_ = f32[16,16,256]{2,1,0:T(8,128)S(1)} collective-permute-done((f32[16,16,256]{2,1,0:T(8,128)S(1)}, f32[16,16,256]{2,1,0:T(8,128)S(1)}, u32[]{:S(2)}, u32[]{:S(2)}) %collective-permute-start.34) | collective-permute-done | bytes 262176 | tf_op jit(solution)/shard_map/ppermute | solution.py:378
  115.6 4.5 %collective-permute-start.38 = (f32[8,16,256]{2,1,0:T(8,128)S(1)}, f32[8,16,256]{2,1,0:T(8,128)S(1)}, u32[]{:S(2)}, u32[]{:S(2)}) collective-permute-start(f32[8,16,256]{2,1,0:T(8,128)S(1)} %get-tuple-element.160), channel_id=1, source_target_pairs={{0,8},{4,12},{8,0},{12,4},{1,9},{5,13},{9,1},{13,5},{2,10},{6,14},... | collective-permute-start | bytes 393224 | tf_op jit(solution)/shard_map/ppermute | solution.py:464
  124.3 4.7 %collective-permute-start.41 = (f32[8,16,256]{2,1,0:T(8,128)S(1)}, f32[8,16,256]{2,1,0:T(8,128)S(1)}, u32[]{:S(2)}, u32[]{:S(2)}) collective-permute-start(f32[8,16,256]{2,1,0:T(8,128)S(1)} %get-tuple-element.165), channel_id=1, source_target_pairs={{0,8},{4,12},{8,0},{12,4},{1,9},{5,13},{9,1},{13,5},{2,10},{6,14},... | collective-permute-start | bytes 393224 | tf_op jit(solution)/shard_map/ppermute | solution.py:464
  131.0 2.3 %shard_map.112.refs_0_ = f32[16,32,512]{2,1,0:T(8,128)} custom-call(s32[16]{0:T(128)S(1)} %get-tuple-element.188.recv_pos, f32[8,16,256]{2,1,0:T(8,128)S(1)} %get-tuple-element.157.refs_0_, f32[16,16,512]{2,1,0:T(8,128)S(1)} %get-tuple-element.158.refs_1_, f32[16,16,256]{2,1,0:T(8,128)S(1)} %get-tuple-element.159.refs_2_, ...), custom_call_target="tpu_custom_call" | custom-call | flops 805306368 | tf_op jit(solution)/shard_map/pallas_call | solution.py:477
  133.4 8.0 %collective-permute-done.41.refs_3_ = f32[8,16,256]{2,1,0:T(8,128)S(1)} collective-permute-done((f32[8,16,256]{2,1,0:T(8,128)S(1)}, f32[8,16,256]{2,1,0:T(8,128)S(1)}, u32[]{:S(2)}, u32[]{:S(2)}) %collective-permute-start.41) | collective-permute-done | bytes 131104 | tf_op jit(solution)/shard_map/ppermute | solution.py:464
  141.3 2.3 %shard_map.113 = f32[16,32,512]{2,1,0:T(8,128)} custom-call(s32[16]{0:T(128)S(1)} %get-tuple-element.188.recv_pos, f32[16,32,512]{2,1,0:T(8,128)} %shard_map.112.refs_0_, f32[16,16,512]{2,1,0:T(8,128)S(1)} %get-tuple-element.163.refs_1_, f32[16,16,256]{2,1,0:T(8,128)S(1)} %get-tuple-element.164.refs_2_, ...), custom_call_target="tpu_custom_call", output_to_operand_aliasing={{}: (1, {})} | custom-call | flops 805306368 | tf_op jit(solution)/shard_map/pallas_call | solution.py:477
  (133 shorter events, 48.3 us)
Async XLA Ops:
  3.6 16.0 %collective-permute-start.2 = (f32[16,16,256]{2,1,0:T(8,128)}, f32[16,16,256]{2,1,0:T(8,128)S(1)}, u32[]{:S(2)}, u32[]{:S(2)}) collective-permute-start(f32[16,16,256]{2,1,0:T(8,128)} %get-tuple-element.95.refs_0_), channel_id=1, source_target_pairs={{0,1},{1,0},{2,3},{3,2},{4,5},{5,4},{6,7},{7,6},{8,9},{9,8},{10,11... | collective-permute-start | bytes 786440 | tf_op jit(solution)/shard_map/ppermute | solution.py:379
  3.7 13.9 %collective-permute-start.4 = (f32[16,16,256]{2,1,0:T(8,128)}, f32[16,16,256]{2,1,0:T(8,128)S(1)}, u32[]{:S(2)}, u32[]{:S(2)}) collective-permute-start(f32[16,16,256]{2,1,0:T(8,128)} %get-tuple-element.95.refs_0_), channel_id=1, source_target_pairs={{0,2},{2,0},{1,3},{3,1},{4,6},{6,4},{5,7},{7,5},{8,10},{10,8},{9,1... | collective-permute-start | bytes 786440 | tf_op jit(solution)/shard_map/ppermute | solution.py:378
  7.6 11.4 %collective-permute-start.5 = (f32[16,16,256]{2,1,0:T(8,128)}, f32[16,16,256]{2,1,0:T(8,128)S(1)}, u32[]{:S(2)}, u32[]{:S(2)}) collective-permute-start(f32[16,16,256]{2,1,0:T(8,128)} %get-tuple-element.96.refs_1_), channel_id=1, source_target_pairs={{0,2},{2,0},{1,3},{3,1},{4,6},{6,4},{5,7},{7,5},{8,10},{10,8},{9,1... | collective-permute-start | bytes 786440 | tf_op jit(solution)/shard_map/ppermute | solution.py:378
  8.8 10.9 %collective-permute-start.3 = (f32[16,16,256]{2,1,0:T(8,128)}, f32[16,16,256]{2,1,0:T(8,128)S(1)}, u32[]{:S(2)}, u32[]{:S(2)}) collective-permute-start(f32[16,16,256]{2,1,0:T(8,128)} %get-tuple-element.96.refs_1_), channel_id=1, source_target_pairs={{0,1},{1,0},{2,3},{3,2},{4,5},{5,4},{6,7},{7,6},{8,9},{9,8},{10,11... | collective-permute-start | bytes 786440 | tf_op jit(solution)/shard_map/ppermute | solution.py:379
  25.4 12.5 %collective-permute-start.9 = (f32[16,16,256]{2,1,0:T(8,128)S(1)}, f32[16,16,256]{2,1,0:T(8,128)S(1)}, u32[]{:S(2)}, u32[]{:S(2)}) collective-permute-start(f32[16,16,256]{2,1,0:T(8,128)S(1)} %bitcast.56), channel_id=1, source_target_pairs={{0,2},{2,0},{1,3},{3,1},{4,6},{6,4},{5,7},{7,5},{8,10},{10,8},{9,1... | collective-permute-start | bytes 786440 | tf_op jit(solution)/shard_map/ppermute | solution.py:417
  32.9 30.4 %collective-permute-start.15 = (f32[65,16,128]{2,1,0:T(8,128)S(1)}, f32[65,16,128]{2,1,0:T(8,128)S(1)}, u32[]{:S(2)}, u32[]{:S(2)}) collective-permute-start(f32[65,16,128]{2,1,0:T(8,128)S(1)} %get-tuple-element.124), channel_id=1, source_target_pairs={{0,3},{1,2},{2,1},{3,0},{4,7},{5,6},{6,5},{7,4},{8,11},{9,10},{10,... | collective-permute-start | bytes 1597448 | tf_op jit(solution)/shard_map/ppermute | solution.py:443
  42.5 14.7 %collective-permute-start.11 = (f32[8,16,256]{2,1,0:T(8,128)S(1)}, f32[8,16,256]{2,1,0:T(8,128)S(1)}, u32[]{:S(2)}, u32[]{:S(2)}) collective-permute-start(f32[8,16,256]{2,1,0:T(8,128)S(1)} %get-tuple-element.117), channel_id=1, source_target_pairs={{0,8},{4,12},{8,0},{12,4},{1,9},{5,13},{9,1},{13,5},{2,10},{6,14},... | collective-permute-start | bytes 393224 | tf_op jit(solution)/shard_map/ppermute | solution.py:464
  42.5 14.7 %collective-permute-start.12 = (f32[8,16,256]{2,1,0:T(8,128)S(1)}, f32[8,16,256]{2,1,0:T(8,128)S(1)}, u32[]{:S(2)}, u32[]{:S(2)}) collective-permute-start(f32[8,16,256]{2,1,0:T(8,128)S(1)} %get-tuple-element.118), channel_id=1, source_target_pairs={{0,4},{4,0},{8,12},{12,8},{1,5},{5,1},{9,13},{13,9},{2,6},{6,2},{1... | collective-permute-start | bytes 393224 | tf_op jit(solution)/shard_map/ppermute | solution.py:464
  43.1 21.8 %collective-permute-start.14 = (f32[65,16,128]{2,1,0:T(8,128)S(1)}, f32[65,16,128]{2,1,0:T(8,128)S(1)}, u32[]{:S(2)}, u32[]{:S(2)}) collective-permute-start(f32[65,16,128]{2,1,0:T(8,128)S(1)} %get-tuple-element.123), channel_id=1, source_target_pairs={{0,2},{1,3},{2,0},{3,1},{4,6},{5,7},{6,4},{7,5},{8,10},{9,11},{10,... | collective-permute-start | bytes 1597448 | tf_op jit(solution)/shard_map/ppermute | solution.py:443
  46.5 18.4 %collective-permute-start.16 = (f32[8,16,256]{2,1,0:T(8,128)S(1)}, f32[8,16,256]{2,1,0:T(8,128)S(1)}, u32[]{:S(2)}, u32[]{:S(2)}) collective-permute-start(f32[8,16,256]{2,1,0:T(8,128)S(1)} %get-tuple-element.127), channel_id=1, source_target_pairs={{0,12},{4,8},{8,4},{12,0},{1,13},{5,9},{9,5},{13,1},{2,14},{6,10},... | collective-permute-start | bytes 393224 | tf_op jit(solution)/shard_map/ppermute | solution.py:464
  63.3 9.5 %collective-permute-start.13 = (f32[16,16,256]{2,1,0:T(8,128)S(1)}, f32[16,16,256]{2,1,0:T(8,128)S(1)}, u32[]{:S(2)}, u32[]{:S(2)}) collective-permute-start(f32[16,16,256]{2,1,0:T(8,128)S(1)} %get-tuple-element.122.refs_1_), channel_id=1, source_target_pairs={{0,2},{2,0},{1,3},{3,1},{4,6},{6,4},{5,7},{7,5},{8,10},{10,8},{9,1... | collective-permute-start | bytes 786440 | tf_op jit(solution)/shard_map/ppermute | solution.py:378
  78.3 13.5 %collective-permute-start.25 = (f32[8,16,256]{2,1,0:T(8,128)S(1)}, f32[8,16,256]{2,1,0:T(8,128)S(1)}, u32[]{:S(2)}, u32[]{:S(2)}) collective-permute-start(f32[8,16,256]{2,1,0:T(8,128)S(1)} %get-tuple-element.141), channel_id=1, source_target_pairs={{0,8},{4,12},{8,0},{12,4},{1,9},{5,13},{9,1},{13,5},{2,10},{6,14},... | collective-permute-start | bytes 393224 | tf_op jit(solution)/shard_map/ppermute | solution.py:464
  80.0 11.9 %collective-permute-start.26 = (f32[8,16,256]{2,1,0:T(8,128)S(1)}, f32[8,16,256]{2,1,0:T(8,128)S(1)}, u32[]{:S(2)}, u32[]{:S(2)}) collective-permute-start(f32[8,16,256]{2,1,0:T(8,128)S(1)} %get-tuple-element.142), channel_id=1, source_target_pairs={{0,12},{4,8},{8,4},{12,0},{1,13},{5,9},{9,5},{13,1},{2,14},{6,10},... | collective-permute-start | bytes 393224 | tf_op jit(solution)/shard_map/ppermute | solution.py:464
  82.0 9.8 %collective-permute-start.27 = (f32[8,16,256]{2,1,0:T(8,128)S(1)}, f32[8,16,256]{2,1,0:T(8,128)S(1)}, u32[]{:S(2)}, u32[]{:S(2)}) collective-permute-start(f32[8,16,256]{2,1,0:T(8,128)S(1)} %get-tuple-element.143), channel_id=1, source_target_pairs={{0,4},{4,0},{8,12},{12,8},{1,5},{5,1},{9,13},{13,9},{2,6},{6,2},{1... | collective-permute-start | bytes 393224 | tf_op jit(solution)/shard_map/ppermute | solution.py:464
  86.2 16.2 %collective-permute-start.28 = (f32[8,16,256]{2,1,0:T(8,128)S(1)}, f32[8,16,256]{2,1,0:T(8,128)S(1)}, u32[]{:S(2)}, u32[]{:S(2)}) collective-permute-start(f32[8,16,256]{2,1,0:T(8,128)S(1)} %get-tuple-element.147), channel_id=1, source_target_pairs={{0,8},{4,12},{8,0},{12,4},{1,9},{5,13},{9,1},{13,5},{2,10},{6,14},... | collective-permute-start | bytes 393224 | tf_op jit(solution)/shard_map/ppermute | solution.py:464
  87.9 14.6 %collective-permute-start.29 = (f32[8,16,256]{2,1,0:T(8,128)S(1)}, f32[8,16,256]{2,1,0:T(8,128)S(1)}, u32[]{:S(2)}, u32[]{:S(2)}) collective-permute-start(f32[8,16,256]{2,1,0:T(8,128)S(1)} %get-tuple-element.148), channel_id=1, source_target_pairs={{0,12},{4,8},{8,4},{12,0},{1,13},{5,9},{9,5},{13,1},{2,14},{6,10},... | collective-permute-start | bytes 393224 | tf_op jit(solution)/shard_map/ppermute | solution.py:464
  91.9 10.6 %collective-permute-start.30 = (f32[8,16,256]{2,1,0:T(8,128)S(1)}, f32[8,16,256]{2,1,0:T(8,128)S(1)}, u32[]{:S(2)}, u32[]{:S(2)}) collective-permute-start(f32[8,16,256]{2,1,0:T(8,128)S(1)} %get-tuple-element.138.refs_0_), channel_id=1, source_target_pairs={{0,4},{4,0},{8,12},{12,8},{1,5},{5,1},{9,13},{13,9},{2,6},{6,2},{1... | collective-permute-start | bytes 393224 | tf_op jit(solution)/shard_map/ppermute | solution.py:464
  93.9 11.8 %collective-permute-start.33 = (f32[16,16,256]{2,1,0:T(8,128)S(1)}, f32[16,16,256]{2,1,0:T(8,128)S(1)}, u32[]{:S(2)}, u32[]{:S(2)}) collective-permute-start(f32[16,16,256]{2,1,0:T(8,128)S(1)} %get-tuple-element.144.refs_0_), channel_id=1, source_target_pairs={{0,2},{2,0},{1,3},{3,1},{4,6},{6,4},{5,7},{7,5},{8,10},{10,8},{9,1... | collective-permute-start | bytes 786440 | tf_op jit(solution)/shard_map/ppermute | solution.py:378
  115.6 14.5 %collective-permute-start.38 = (f32[8,16,256]{2,1,0:T(8,128)S(1)}, f32[8,16,256]{2,1,0:T(8,128)S(1)}, u32[]{:S(2)}, u32[]{:S(2)}) collective-permute-start(f32[8,16,256]{2,1,0:T(8,128)S(1)} %get-tuple-element.160), channel_id=1, source_target_pairs={{0,8},{4,12},{8,0},{12,4},{1,9},{5,13},{9,1},{13,5},{2,10},{6,14},... | collective-permute-start | bytes 393224 | tf_op jit(solution)/shard_map/ppermute | solution.py:464
  120.1 10.0 %collective-permute-start.39 = (f32[8,16,256]{2,1,0:T(8,128)S(1)}, f32[8,16,256]{2,1,0:T(8,128)S(1)}, u32[]{:S(2)}, u32[]{:S(2)}) collective-permute-start(f32[8,16,256]{2,1,0:T(8,128)S(1)} %get-tuple-element.161), channel_id=1, source_target_pairs={{0,12},{4,8},{8,4},{12,0},{1,13},{5,9},{9,5},{13,1},{2,14},{6,10},... | collective-permute-start | bytes 393224 | tf_op jit(solution)/shard_map/ppermute | solution.py:464
  121.4 9.6 %collective-permute-start.40 = (f32[8,16,256]{2,1,0:T(8,128)S(1)}, f32[8,16,256]{2,1,0:T(8,128)S(1)}, u32[]{:S(2)}, u32[]{:S(2)}) collective-permute-start(f32[8,16,256]{2,1,0:T(8,128)S(1)} %get-tuple-element.162), channel_id=1, source_target_pairs={{0,4},{4,0},{8,12},{12,8},{1,5},{5,1},{9,13},{13,9},{2,6},{6,2},{1... | collective-permute-start | bytes 393224 | tf_op jit(solution)/shard_map/ppermute | solution.py:464
  124.3 17.0 %collective-permute-start.41 = (f32[8,16,256]{2,1,0:T(8,128)S(1)}, f32[8,16,256]{2,1,0:T(8,128)S(1)}, u32[]{:S(2)}, u32[]{:S(2)}) collective-permute-start(f32[8,16,256]{2,1,0:T(8,128)S(1)} %get-tuple-element.165), channel_id=1, source_target_pairs={{0,8},{4,12},{8,0},{12,4},{1,9},{5,13},{9,1},{13,5},{2,10},{6,14},... | collective-permute-start | bytes 393224 | tf_op jit(solution)/shard_map/ppermute | solution.py:464
  129.0 12.3 %collective-permute-start.42 = (f32[8,16,256]{2,1,0:T(8,128)S(1)}, f32[8,16,256]{2,1,0:T(8,128)S(1)}, u32[]{:S(2)}, u32[]{:S(2)}) collective-permute-start(f32[8,16,256]{2,1,0:T(8,128)S(1)} %get-tuple-element.166), channel_id=1, source_target_pairs={{0,12},{4,8},{8,4},{12,0},{1,13},{5,9},{9,5},{13,1},{2,14},{6,10},... | collective-permute-start | bytes 393224 | tf_op jit(solution)/shard_map/ppermute | solution.py:464
  130.1 11.2 %collective-permute-start.43 = (f32[8,16,256]{2,1,0:T(8,128)S(1)}, f32[8,16,256]{2,1,0:T(8,128)S(1)}, u32[]{:S(2)}, u32[]{:S(2)}) collective-permute-start(f32[8,16,256]{2,1,0:T(8,128)S(1)} %get-tuple-element.157.refs_0_), channel_id=1, source_target_pairs={{0,4},{4,0},{8,12},{12,8},{1,5},{5,1},{9,13},{13,9},{2,6},{6,2},{1... | collective-permute-start | bytes 393224 | tf_op jit(solution)/shard_map/ppermute | solution.py:464
  (31 other events, 214.3 us)

commit v7 on v6

--- a/solution.py
+++ b/solution.py
@@ -458,7 +458,10 @@
             fetched = far
         next_feats, next_lows = [None] * n, [None] * n
         result = None
-        steps = sorted(range(1, edges), key=lambda k: (layer == 0 or k != edges // 2, -k))
+        if layer == 0:
+            steps = [edges - 1, *range(1, edges - 1)]
+        else:
+            steps = sorted(range(1, edges), key=lambda k: (k != edges // 2, -k))
         for i, r in enumerate(order):
             off, rc = chunks[r]
             back = [lax.ppermute(packs[r][k - 1], "edge", [(i, i ^ k) for i in range(edges)]) for k in steps]

time: 144 us -> 143 us (level)
  transfers between devices with their start and end apart: 44 -> 44, of which waited for: 14 -> 16; matrix products, arithmetic and copies ran while one was open for 1% -> 2% of each run, Pallas kernels for 24% -> 24%
where the time goes in v7:
time: 143 us
  waiting for transfers between devices  48.2 us (34%)
  starting transfers between devices  47.3 us (33%)
  Pallas kernels  42 us (29%)
  local copies, waits for them, and re-layouts  2.58 us (2%)
  other arithmetic  1.79 us (1%)
    ppermute x18, starting transfers between devices, local(): lax.ppermute(packs[r][k - 1], 'edge', [(i, i ^ k) for i in range(edges)])  31.4 us
    ppermute x18, waiting for transfers between devices, local(): lax.ppermute(packs[r][k - 1], 'edge', [(i, i ^ k) for i in range(edges)])  27 us
    pallas_call x6, Pallas kernels, local(): call(functools.partial(rows_kernel, (clusters, rc, cap, steps), last, len...  12.9 us
    ppermute x4, waiting for transfers between devices, local(): lax.ppermute(sent[d - 1], 'trip', turn(d))  12.5 us
    ppermute x6, waiting for transfers between devices, local(): lax.ppermute(low, 'trip', turn(d))  8.16 us
    ppermute x6, starting transfers between devices, local(): lax.ppermute(low, 'trip', turn(d))  7.36 us
    pallas_call x1, Pallas kernels, local(): call(functools.partial(cells_kernel, (trips, subs, share, chunks, cluster...  6.01 us
    pallas_call x3, Pallas kernels, local(): call(functools.partial(far_kernel, n, len(far), cap, whole), [jax.ShapeDt...  5.21 us
  transfers between devices with their start and end apart: 44, of which 16 were waited for; matrix products, arithmetic and copies ran while one was open for 2% of the time, Pallas kernels for 24%

profile of v7, /device:TPU:0, one launch (start us, length us, event | category | flops | bytes accessed | tf_op | source)
XLA Modules:
  0.0 142.9 jit_solution(538161255861774594)
XLA Ops:
  0.5 3.0 %shard_map.91 = (f32[16,16,256]{2,1,0:T(8,128)}, f32[16,16,256]{2,1,0:T(8,128)}) custom-call(f32[16,32,512]{2,1,0:T(8,128)} %refs_1_.3, f32[3,512,256]{2,1,0:T(8,128)} %down.1), custom_call_target="tpu_custom_call" | custom-call | flops 402653184 | tf_op jit(solution)/shard_map/pallas_call | solution.py:308
  3.7 3.0 %collective-permute-start.4 = (f32[16,16,256]{2,1,0:T(8,128)}, f32[16,16,256]{2,1,0:T(8,128)S(1)}, u32[]{:S(2)}, u32[]{:S(2)}) collective-permute-start(f32[16,16,256]{2,1,0:T(8,128)} %get-tuple-element.95.refs_0_), channel_id=1, source_target_pairs={{0,2},{2,0},{1,3},{3,1},{4,6},{6,4},{5,7},{7,5},{8,10},{10,8},{9,1... | collective-permute-start | bytes 786440 | tf_op jit(solution)/shard_map/ppermute | solution.py:378
  9.1 2.2 %copy-done = f32[1,1,64,128,128]{4,3,2,1,0:T(8,128)S(1)} copy-done((f32[1,1,64,128,128]{4,3,2,1,0:T(8,128)S(1)}, f32[1,1,64,128,128]{4,3,2,1,0:T(8,128)}, u32[]{:S(2)}) %copy-start) | copy-done | bytes 4194328
  11.3 6.0 %shard_map.92 = (bf16[512,2048]{1,0:T(8,128)(2,1)S(1)}, bf16[512,2048]{1,0:T(8,128)(2,1)S(1)}, bf16[512,2048]{1,0:T(8,128)(2,1)S(1)}, bf16[512,2048]{1,0:T(8,128...) custom-call(s32[2]{0:T(128)S(1)} %pad_add_fusion.3.ids, s32[16]{0:T(128)S(1)} %copy-done.5, ...), custom_call_target="tpu_custom_call" | custom-call | bytes 12582912 | tf_op jit(solution)/shard_map/pallas_call | solution.py:352
  26.8 5.5 %collective-permute-done.8.refs_0_ = f32[16,16,256]{2,1,0:T(8,128)S(1)} collective-permute-done((f32[16,16,256]{2,1,0:T(8,128)S(1)}, f32[16,16,256]{2,1,0:T(8,128)S(1)}, u32[]{:S(2)}, u32[]{:S(2)}) %collective-permute-start.8) | collective-permute-done | bytes 262176 | tf_op jit(solution)/shard_map/ppermute | solution.py:417
  34.3 3.6 %collective-permute-done.9.refs_0_ = f32[16,16,256]{2,1,0:T(8,128)S(1)} collective-permute-done((f32[16,16,256]{2,1,0:T(8,128)S(1)}, f32[16,16,256]{2,1,0:T(8,128)S(1)}, u32[]{:S(2)}, u32[]{:S(2)}) %collective-permute-start.9) | collective-permute-done | bytes 262176 | tf_op jit(solution)/shard_map/ppermute | solution.py:417
  38.5 3.9 %collective-permute-start.10 = (f32[8,16,256]{2,1,0:T(8,128)S(1)}, f32[8,16,256]{2,1,0:T(8,128)S(1)}, u32[]{:S(2)}, u32[]{:S(2)}) collective-permute-start(f32[8,16,256]{2,1,0:T(8,128)S(1)} %get-tuple-element.116), channel_id=1, source_target_pairs={{0,12},{4,8},{8,4},{12,0},{1,13},{5,9},{9,5},{13,1},{2,14},{6,10},... | collective-permute-start | bytes 393224 | tf_op jit(solution)/shard_map/ppermute | solution.py:467
  46.6 4.2 %collective-permute-start.16 = (f32[8,16,256]{2,1,0:T(8,128)S(1)}, f32[8,16,256]{2,1,0:T(8,128)S(1)}, u32[]{:S(2)}, u32[]{:S(2)}) collective-permute-start(f32[8,16,256]{2,1,0:T(8,128)S(1)} %get-tuple-element.127), channel_id=1, source_target_pairs={{0,12},{4,8},{8,4},{12,0},{1,13},{5,9},{9,5},{13,1},{2,14},{6,10},... | collective-permute-start | bytes 393224 | tf_op jit(solution)/shard_map/ppermute | solution.py:467
  50.8 2.3 %collective-permute-start.17 = (f32[8,16,256]{2,1,0:T(8,128)S(1)}, f32[8,16,256]{2,1,0:T(8,128)S(1)}, u32[]{:S(2)}, u32[]{:S(2)}) collective-permute-start(f32[8,16,256]{2,1,0:T(8,128)S(1)} %get-tuple-element.112.refs_0_), channel_id=1, source_target_pairs={{0,4},{4,0},{8,12},{12,8},{1,5},{5,1},{9,13},{13,9},{2,6},{6,2},{1... | collective-permute-start | bytes 393224 | tf_op jit(solution)/shard_map/ppermute | solution.py:467
  53.1 4.1 %collective-permute-done.12.refs_5_ = f32[8,16,256]{2,1,0:T(8,128)S(1)} collective-permute-done((f32[8,16,256]{2,1,0:T(8,128)S(1)}, f32[8,16,256]{2,1,0:T(8,128)S(1)}, u32[]{:S(2)}, u32[]{:S(2)}) %collective-permute-start.12) | collective-permute-done | bytes 131104 | tf_op jit(solution)/shard_map/ppermute | solution.py:467
  57.2 2.1 %shard_map.99 = (f32[16,16,512]{2,1,0:T(8,128)S(1)}, f32[16,16,256]{2,1,0:T(8,128)S(1)}) custom-call(s32[16]{0:T(128)S(1)} %get-tuple-element.188.recv_pos, f32[8,16,256]{2,1,0:T(8,128)S(1)} %get-tuple-element.112.refs_0_, f32[16,32,512]{2,1,0:T(8,128)S(1)} %copy-done.2, f32[16,16,256]{2,1,0:T(8,128)S(1)} %get-tuple-element.115.refs_2_, ...), custom_call_target="tpu_custom_call" | custom-call | flops 805306368 | tf_op jit(solution)/shard_map/pallas_call | solution.py:480
  60.9 3.5 %collective-permute-done.18.refs_5_ = f32[8,16,256]{2,1,0:T(8,128)S(1)} collective-permute-done((f32[8,16,256]{2,1,0:T(8,128)S(1)}, f32[8,16,256]{2,1,0:T(8,128)S(1)}, u32[]{:S(2)}, u32[]{:S(2)}) %collective-permute-start.18) | collective-permute-done | bytes 131104 | tf_op jit(solution)/shard_map/ppermute | solution.py:467
  68.7 3.5 %shard_map.100.one = bf16[512,2048]{1,0:T(8,128)(2,1)S(1)} custom-call(s32[2]{0:T(128)S(1)} %pad_add_fusion.3.ids, s32[16]{0:T(128)S(1)} %copy-done.5, s32[4,128]{1,0:T(4,128)S(1)} %slice.70.pats, s32[4]{0:T(128)S(1)} %slice_reduce_fusion.live, f32[64,128,128]{2,1,0:T(8,128)S(1)} %bitcast.51, f32[64,128,128]{2,1,0:T(8,128)} %collective-permute-done.1.theirs, ...), custom_call_target="tpu_custom_call" | custom-call | bytes 6291456 | tf_op jit(solution)/shard_map/pallas_call | solution.py:446
  79.3 3.0 %collective-permute-start.26 = (f32[8,16,256]{2,1,0:T(8,128)S(1)}, f32[8,16,256]{2,1,0:T(8,128)S(1)}, u32[]{:S(2)}, u32[]{:S(2)}) collective-permute-start(f32[8,16,256]{2,1,0:T(8,128)S(1)} %get-tuple-element.142), channel_id=1, source_target_pairs={{0,12},{4,8},{8,4},{12,0},{1,13},{5,9},{9,5},{13,1},{2,14},{6,10},... | collective-permute-start | bytes 393224 | tf_op jit(solution)/shard_map/ppermute | solution.py:467
  87.1 3.1 %collective-permute-start.29 = (f32[8,16,256]{2,1,0:T(8,128)S(1)}, f32[8,16,256]{2,1,0:T(8,128)S(1)}, u32[]{:S(2)}, u32[]{:S(2)}) collective-permute-start(f32[8,16,256]{2,1,0:T(8,128)S(1)} %get-tuple-element.148), channel_id=1, source_target_pairs={{0,12},{4,8},{8,4},{12,0},{1,13},{5,9},{9,5},{13,1},{2,14},{6,10},... | collective-permute-start | bytes 393224 | tf_op jit(solution)/shard_map/ppermute | solution.py:467
  91.5 2.0 %shard_map.106 = (f32[16,16,512]{2,1,0:T(8,128)S(1)}, f32[16,16,256]{2,1,0:T(8,128)S(1)}) custom-call(s32[16]{0:T(128)S(1)} %get-tuple-element.188.recv_pos, f32[8,16,256]{2,1,0:T(8,128)S(1)} %get-tuple-element.138.refs_0_, f32[16,16,512]{2,1,0:T(8,128)S(1)} %get-tuple-element.139.refs_1_, f32[16,16,256]{2,1,0:T(8,128)S(1)} %get-tuple-element.140.refs_2_, ...), custom_call_target="tpu_custom_call" | custom-call | flops 805306368 | tf_op jit(solution)/shard_map/pallas_call | solution.py:480
  94.1 8.0 %collective-permute-done.28.refs_2_ = f32[8,16,256]{2,1,0:T(8,128)S(1)} collective-permute-done((f32[8,16,256]{2,1,0:T(8,128)S(1)}, f32[8,16,256]{2,1,0:T(8,128)S(1)}, u32[]{:S(2)}, u32[]{:S(2)}) %collective-permute-start.28) | collective-permute-done | bytes 131104 | tf_op jit(solution)/shard_map/ppermute | solution.py:467
  102.1 2.1 %shard_map.107 = (f32[16,16,512]{2,1,0:T(8,128)S(1)}, f32[16,16,256]{2,1,0:T(8,128)S(1)}) custom-call(s32[16]{0:T(128)S(1)} %get-tuple-element.188.recv_pos, f32[16,16,512]{2,1,0:T(8,128)S(1)} %get-tuple-element.145.refs_0_, f32[16,16,256]{2,1,0:T(8,128)S(1)} %get-tuple-element.146.refs_1_, f32[8,16,256]{2,1,0:T(8,128)S(1)} %collective-permute-done.28.refs_2_, ...), custom_call_target="tpu_custom_call" | custom-call | flops 805306368 | tf_op jit(solution)/shard_map/pallas_call | solution.py:480
  105.2 5.9 %collective-permute-done.34.refs_1_ = f32[16,16,256]{2,1,0:T(8,128)S(1)} collective-permute-done((f32[16,16,256]{2,1,0:T(8,128)S(1)}, f32[16,16,256]{2,1,0:T(8,128)S(1)}, u32[]{:S(2)}, u32[]{:S(2)}) %collective-permute-start.34) | collective-permute-done | bytes 262176 | tf_op jit(solution)/shard_map/ppermute | solution.py:378
  115.2 4.3 %collective-permute-start.38 = (f32[8,16,256]{2,1,0:T(8,128)S(1)}, f32[8,16,256]{2,1,0:T(8,128)S(1)}, u32[]{:S(2)}, u32[]{:S(2)}) collective-permute-start(f32[8,16,256]{2,1,0:T(8,128)S(1)} %get-tuple-element.160), channel_id=1, source_target_pairs={{0,8},{4,12},{8,0},{12,4},{1,9},{5,13},{9,1},{13,5},{2,10},{6,14},... | collective-permute-start | bytes 393224 | tf_op jit(solution)/shard_map/ppermute | solution.py:467
  124.0 4.2 %collective-permute-start.41 = (f32[8,16,256]{2,1,0:T(8,128)S(1)}, f32[8,16,256]{2,1,0:T(8,128)S(1)}, u32[]{:S(2)}, u32[]{:S(2)}) collective-permute-start(f32[8,16,256]{2,1,0:T(8,128)S(1)} %get-tuple-element.165), channel_id=1, source_target_pairs={{0,8},{4,12},{8,0},{12,4},{1,9},{5,13},{9,1},{13,5},{2,10},{6,14},... | collective-permute-start | bytes 393224 | tf_op jit(solution)/shard_map/ppermute | solution.py:467
  130.3 2.3 %shard_map.112.refs_0_ = f32[16,32,512]{2,1,0:T(8,128)} custom-call(s32[16]{0:T(128)S(1)} %get-tuple-element.188.recv_pos, f32[8,16,256]{2,1,0:T(8,128)S(1)} %get-tuple-element.157.refs_0_, f32[16,16,512]{2,1,0:T(8,128)S(1)} %get-tuple-element.158.refs_1_, f32[16,16,256]{2,1,0:T(8,128)S(1)} %get-tuple-element.159.refs_2_, ...), custom_call_target="tpu_custom_call" | custom-call | flops 805306368 | tf_op jit(solution)/shard_map/pallas_call | solution.py:480
  132.7 8.0 %collective-permute-done.41.refs_3_ = f32[8,16,256]{2,1,0:T(8,128)S(1)} collective-permute-done((f32[8,16,256]{2,1,0:T(8,128)S(1)}, f32[8,16,256]{2,1,0:T(8,128)S(1)}, u32[]{:S(2)}, u32[]{:S(2)}) %collective-permute-start.41) | collective-permute-done | bytes 131104 | tf_op jit(solution)/shard_map/ppermute | solution.py:467
  140.6 2.3 %shard_map.113 = f32[16,32,512]{2,1,0:T(8,128)} custom-call(s32[16]{0:T(128)S(1)} %get-tuple-element.188.recv_pos, f32[16,32,512]{2,1,0:T(8,128)} %shard_map.112.refs_0_, f32[16,16,512]{2,1,0:T(8,128)S(1)} %get-tuple-element.163.refs_1_, f32[16,16,256]{2,1,0:T(8,128)S(1)} %get-tuple-element.164.refs_2_, ...), custom_call_target="tpu_custom_call", output_to_operand_aliasing={{}: (1, {})} | custom-call | flops 805306368 | tf_op jit(solution)/shard_map/pallas_call | solution.py:480
  (133 shorter events, 49.6 us)
Async XLA Ops:
  3.6 16.0 %collective-permute-start.2 = (f32[16,16,256]{2,1,0:T(8,128)}, f32[16,16,256]{2,1,0:T(8,128)S(1)}, u32[]{:S(2)}, u32[]{:S(2)}) collective-permute-start(f32[16,16,256]{2,1,0:T(8,128)} %get-tuple-element.95.refs_0_), channel_id=1, source_target_pairs={{0,1},{1,0},{2,3},{3,2},{4,5},{5,4},{6,7},{7,6},{8,9},{9,8},{10,11... | collective-permute-start | bytes 786440 | tf_op jit(solution)/shard_map/ppermute | solution.py:379
  3.7 13.6 %collective-permute-start.4 = (f32[16,16,256]{2,1,0:T(8,128)}, f32[16,16,256]{2,1,0:T(8,128)S(1)}, u32[]{:S(2)}, u32[]{:S(2)}) collective-permute-start(f32[16,16,256]{2,1,0:T(8,128)} %get-tuple-element.95.refs_0_), channel_id=1, source_target_pairs={{0,2},{2,0},{1,3},{3,1},{4,6},{6,4},{5,7},{7,5},{8,10},{10,8},{9,1... | collective-permute-start | bytes 786440 | tf_op jit(solution)/shard_map/ppermute | solution.py:378
  7.6 11.4 %collective-permute-start.5 = (f32[16,16,256]{2,1,0:T(8,128)}, f32[16,16,256]{2,1,0:T(8,128)S(1)}, u32[]{:S(2)}, u32[]{:S(2)}) collective-permute-start(f32[16,16,256]{2,1,0:T(8,128)} %get-tuple-element.96.refs_1_), channel_id=1, source_target_pairs={{0,2},{2,0},{1,3},{3,1},{4,6},{6,4},{5,7},{7,5},{8,10},{10,8},{9,1... | collective-permute-start | bytes 786440 | tf_op jit(solution)/shard_map/ppermute | solution.py:378
  8.8 10.9 %collective-permute-start.3 = (f32[16,16,256]{2,1,0:T(8,128)}, f32[16,16,256]{2,1,0:T(8,128)S(1)}, u32[]{:S(2)}, u32[]{:S(2)}) collective-permute-start(f32[16,16,256]{2,1,0:T(8,128)} %get-tuple-element.96.refs_1_), channel_id=1, source_target_pairs={{0,1},{1,0},{2,3},{3,2},{4,5},{5,4},{6,7},{7,6},{8,9},{9,8},{10,11... | collective-permute-start | bytes 786440 | tf_op jit(solution)/shard_map/ppermute | solution.py:379
  23.1 9.2 %collective-permute-start.8 = (f32[16,16,256]{2,1,0:T(8,128)S(1)}, f32[16,16,256]{2,1,0:T(8,128)S(1)}, u32[]{:S(2)}, u32[]{:S(2)}) collective-permute-start(f32[16,16,256]{2,1,0:T(8,128)S(1)} %bitcast.59), channel_id=1, source_target_pairs={{0,2},{2,0},{1,3},{3,1},{4,6},{6,4},{5,7},{7,5},{8,10},{10,8},{9,1... | collective-permute-start | bytes 786440 | tf_op jit(solution)/shard_map/ppermute | solution.py:417
  25.4 12.5 %collective-permute-start.9 = (f32[16,16,256]{2,1,0:T(8,128)S(1)}, f32[16,16,256]{2,1,0:T(8,128)S(1)}, u32[]{:S(2)}, u32[]{:S(2)}) collective-permute-start(f32[16,16,256]{2,1,0:T(8,128)S(1)} %bitcast.56), channel_id=1, source_target_pairs={{0,2},{2,0},{1,3},{3,1},{4,6},{6,4},{5,7},{7,5},{8,10},{10,8},{9,1... | collective-permute-start | bytes 786440 | tf_op jit(solution)/shard_map/ppermute | solution.py:417
  32.9 26.3 %collective-permute-start.15 = (f32[65,16,128]{2,1,0:T(8,128)S(1)}, f32[65,16,128]{2,1,0:T(8,128)S(1)}, u32[]{:S(2)}, u32[]{:S(2)}) collective-permute-start(f32[65,16,128]{2,1,0:T(8,128)S(1)} %get-tuple-element.124), channel_id=1, source_target_pairs={{0,3},{1,2},{2,1},{3,0},{4,7},{5,6},{6,5},{7,4},{8,11},{9,10},{10,... | collective-permute-start | bytes 1597448 | tf_op jit(solution)/shard_map/ppermute | solution.py:443
  42.5 14.7 %collective-permute-start.12 = (f32[8,16,256]{2,1,0:T(8,128)S(1)}, f32[8,16,256]{2,1,0:T(8,128)S(1)}, u32[]{:S(2)}, u32[]{:S(2)}) collective-permute-start(f32[8,16,256]{2,1,0:T(8,128)S(1)} %get-tuple-element.118), channel_id=1, source_target_pairs={{0,8},{4,12},{8,0},{12,4},{1,9},{5,13},{9,1},{13,5},{2,10},{6,14},... | collective-permute-start | bytes 393224 | tf_op jit(solution)/shard_map/ppermute | solution.py:467
  43.1 17.8 %collective-permute-start.14 = (f32[65,16,128]{2,1,0:T(8,128)S(1)}, f32[65,16,128]{2,1,0:T(8,128)S(1)}, u32[]{:S(2)}, u32[]{:S(2)}) collective-permute-start(f32[65,16,128]{2,1,0:T(8,128)S(1)} %get-tuple-element.123), channel_id=1, source_target_pairs={{0,2},{1,3},{2,0},{3,1},{4,6},{5,7},{6,4},{7,5},{8,10},{9,11},{10,... | collective-permute-start | bytes 1597448 | tf_op jit(solution)/shard_map/ppermute | solution.py:443
  46.6 14.3 %collective-permute-start.16 = (f32[8,16,256]{2,1,0:T(8,128)S(1)}, f32[8,16,256]{2,1,0:T(8,128)S(1)}, u32[]{:S(2)}, u32[]{:S(2)}) collective-permute-start(f32[8,16,256]{2,1,0:T(8,128)S(1)} %get-tuple-element.127), channel_id=1, source_target_pairs={{0,12},{4,8},{8,4},{12,0},{1,13},{5,9},{9,5},{13,1},{2,14},{6,10},... | collective-permute-start | bytes 393224 | tf_op jit(solution)/shard_map/ppermute | solution.py:467
  50.8 10.1 %collective-permute-start.17 = (f32[8,16,256]{2,1,0:T(8,128)S(1)}, f32[8,16,256]{2,1,0:T(8,128)S(1)}, u32[]{:S(2)}, u32[]{:S(2)}) collective-permute-start(f32[8,16,256]{2,1,0:T(8,128)S(1)} %get-tuple-element.112.refs_0_), channel_id=1, source_target_pairs={{0,4},{4,0},{8,12},{12,8},{1,5},{5,1},{9,13},{13,9},{2,6},{6,2},{1... | collective-permute-start | bytes 393224 | tf_op jit(solution)/shard_map/ppermute | solution.py:467
  59.2 13.0 %collective-permute-start.13 = (f32[16,16,256]{2,1,0:T(8,128)S(1)}, f32[16,16,256]{2,1,0:T(8,128)S(1)}, u32[]{:S(2)}, u32[]{:S(2)}) collective-permute-start(f32[16,16,256]{2,1,0:T(8,128)S(1)} %get-tuple-element.122.refs_1_), channel_id=1, source_target_pairs={{0,2},{2,0},{1,3},{3,1},{4,6},{6,4},{5,7},{7,5},{8,10},{10,8},{9,1... | collective-permute-start | bytes 786440 | tf_op jit(solution)/shard_map/ppermute | solution.py:378
  78.0 12.9 %collective-permute-start.25 = (f32[8,16,256]{2,1,0:T(8,128)S(1)}, f32[8,16,256]{2,1,0:T(8,128)S(1)}, u32[]{:S(2)}, u32[]{:S(2)}) collective-permute-start(f32[8,16,256]{2,1,0:T(8,128)S(1)} %get-tuple-element.141), channel_id=1, source_target_pairs={{0,8},{4,12},{8,0},{12,4},{1,9},{5,13},{9,1},{13,5},{2,10},{6,14},... | collective-permute-start | bytes 393224 | tf_op jit(solution)/shard_map/ppermute | solution.py:467
  79.3 11.6 %collective-permute-start.26 = (f32[8,16,256]{2,1,0:T(8,128)S(1)}, f32[8,16,256]{2,1,0:T(8,128)S(1)}, u32[]{:S(2)}, u32[]{:S(2)}) collective-permute-start(f32[8,16,256]{2,1,0:T(8,128)S(1)} %get-tuple-element.142), channel_id=1, source_target_pairs={{0,12},{4,8},{8,4},{12,0},{1,13},{5,9},{9,5},{13,1},{2,14},{6,10},... | collective-permute-start | bytes 393224 | tf_op jit(solution)/shard_map/ppermute | solution.py:467
  85.7 16.4 %collective-permute-start.28 = (f32[8,16,256]{2,1,0:T(8,128)S(1)}, f32[8,16,256]{2,1,0:T(8,128)S(1)}, u32[]{:S(2)}, u32[]{:S(2)}) collective-permute-start(f32[8,16,256]{2,1,0:T(8,128)S(1)} %get-tuple-element.147), channel_id=1, source_target_pairs={{0,8},{4,12},{8,0},{12,4},{1,9},{5,13},{9,1},{13,5},{2,10},{6,14},... | collective-permute-start | bytes 393224 | tf_op jit(solution)/shard_map/ppermute | solution.py:467
  87.1 15.0 %collective-permute-start.29 = (f32[8,16,256]{2,1,0:T(8,128)S(1)}, f32[8,16,256]{2,1,0:T(8,128)S(1)}, u32[]{:S(2)}, u32[]{:S(2)}) collective-permute-start(f32[8,16,256]{2,1,0:T(8,128)S(1)} %get-tuple-element.148), channel_id=1, source_target_pairs={{0,12},{4,8},{8,4},{12,0},{1,13},{5,9},{9,5},{13,1},{2,14},{6,10},... | collective-permute-start | bytes 393224 | tf_op jit(solution)/shard_map/ppermute | solution.py:467
  90.9 11.2 %collective-permute-start.30 = (f32[8,16,256]{2,1,0:T(8,128)S(1)}, f32[8,16,256]{2,1,0:T(8,128)S(1)}, u32[]{:S(2)}, u32[]{:S(2)}) collective-permute-start(f32[8,16,256]{2,1,0:T(8,128)S(1)} %get-tuple-element.138.refs_0_), channel_id=1, source_target_pairs={{0,4},{4,0},{8,12},{12,8},{1,5},{5,1},{9,13},{13,9},{2,6},{6,2},{1... | collective-permute-start | bytes 393224 | tf_op jit(solution)/shard_map/ppermute | solution.py:467
  93.5 11.7 %collective-permute-start.33 = (f32[16,16,256]{2,1,0:T(8,128)S(1)}, f32[16,16,256]{2,1,0:T(8,128)S(1)}, u32[]{:S(2)}, u32[]{:S(2)}) collective-permute-start(f32[16,16,256]{2,1,0:T(8,128)S(1)} %get-tuple-element.144.refs_0_), channel_id=1, source_target_pairs={{0,2},{2,0},{1,3},{3,1},{4,6},{6,4},{5,7},{7,5},{8,10},{10,8},{9,1... | collective-permute-start | bytes 786440 | tf_op jit(solution)/shard_map/ppermute | solution.py:378
  115.2 14.6 %collective-permute-start.38 = (f32[8,16,256]{2,1,0:T(8,128)S(1)}, f32[8,16,256]{2,1,0:T(8,128)S(1)}, u32[]{:S(2)}, u32[]{:S(2)}) collective-permute-start(f32[8,16,256]{2,1,0:T(8,128)S(1)} %get-tuple-element.160), channel_id=1, source_target_pairs={{0,8},{4,12},{8,0},{12,4},{1,9},{5,13},{9,1},{13,5},{2,10},{6,14},... | collective-permute-start | bytes 393224 | tf_op jit(solution)/shard_map/ppermute | solution.py:467
  119.4 10.3 %collective-permute-start.39 = (f32[8,16,256]{2,1,0:T(8,128)S(1)}, f32[8,16,256]{2,1,0:T(8,128)S(1)}, u32[]{:S(2)}, u32[]{:S(2)}) collective-permute-start(f32[8,16,256]{2,1,0:T(8,128)S(1)} %get-tuple-element.161), channel_id=1, source_target_pairs={{0,12},{4,8},{8,4},{12,0},{1,13},{5,9},{9,5},{13,1},{2,14},{6,10},... | collective-permute-start | bytes 393224 | tf_op jit(solution)/shard_map/ppermute | solution.py:467
  120.9 9.4 %collective-permute-start.40 = (f32[8,16,256]{2,1,0:T(8,128)S(1)}, f32[8,16,256]{2,1,0:T(8,128)S(1)}, u32[]{:S(2)}, u32[]{:S(2)}) collective-permute-start(f32[8,16,256]{2,1,0:T(8,128)S(1)} %get-tuple-element.162), channel_id=1, source_target_pairs={{0,4},{4,0},{8,12},{12,8},{1,5},{5,1},{9,13},{13,9},{2,6},{6,2},{1... | collective-permute-start | bytes 393224 | tf_op jit(solution)/shard_map/ppermute | solution.py:467
  124.0 16.6 %collective-permute-start.41 = (f32[8,16,256]{2,1,0:T(8,128)S(1)}, f32[8,16,256]{2,1,0:T(8,128)S(1)}, u32[]{:S(2)}, u32[]{:S(2)}) collective-permute-start(f32[8,16,256]{2,1,0:T(8,128)S(1)} %get-tuple-element.165), channel_id=1, source_target_pairs={{0,8},{4,12},{8,0},{12,4},{1,9},{5,13},{9,1},{13,5},{2,10},{6,14},... | collective-permute-start | bytes 393224 | tf_op jit(solution)/shard_map/ppermute | solution.py:467
  128.2 12.4 %collective-permute-start.42 = (f32[8,16,256]{2,1,0:T(8,128)S(1)}, f32[8,16,256]{2,1,0:T(8,128)S(1)}, u32[]{:S(2)}, u32[]{:S(2)}) collective-permute-start(f32[8,16,256]{2,1,0:T(8,128)S(1)} %get-tuple-element.166), channel_id=1, source_target_pairs={{0,12},{4,8},{8,4},{12,0},{1,13},{5,9},{9,5},{13,1},{2,14},{6,10},... | collective-permute-start | bytes 393224 | tf_op jit(solution)/shard_map/ppermute | solution.py:467
  129.8 10.8 %collective-permute-start.43 = (f32[8,16,256]{2,1,0:T(8,128)S(1)}, f32[8,16,256]{2,1,0:T(8,128)S(1)}, u32[]{:S(2)}, u32[]{:S(2)}) collective-permute-start(f32[8,16,256]{2,1,0:T(8,128)S(1)} %get-tuple-element.157.refs_0_), channel_id=1, source_target_pairs={{0,4},{4,0},{8,12},{12,8},{1,5},{5,1},{9,13},{13,9},{2,6},{6,2},{1... | collective-permute-start | bytes 393224 | tf_op jit(solution)/shard_map/ppermute | solution.py:467
  (31 other events, 214.1 us)

commit v8 on v7

--- a/solution.py
+++ b/solution.py
@@ -461,7 +461,7 @@
         if layer == 0:
             steps = [edges - 1, *range(1, edges - 1)]
         else:
-            steps = sorted(range(1, edges), key=lambda k: (k != edges // 2, -k))
+            steps = sorted(range(1, edges), key=lambda k: (k != edges // 2, k if last else -k))
         for i, r in enumerate(order):
             off, rc = chunks[r]
             back = [lax.ppermute(packs[r][k - 1], "edge", [(i, i ^ k) for i in range(edges)]) for k in steps]

time: 143 us -> 143 us (level)
  no operation moved by 1% of the time
where the time goes in v8:
time: 143 us
  waiting for transfers between devices  47.9 us (33%)
  starting transfers between devices  47.3 us (33%)
  Pallas kernels  42.2 us (30%)
  local copies, waits for them, and re-layouts  2.58 us (2%)
  other arithmetic  1.79 us (1%)
    ppermute x18, starting transfers between devices, local(): lax.ppermute(packs[r][k - 1], 'edge', [(i, i ^ k) for i in range(edges)])  31.4 us
    ppermute x18, waiting for transfers between devices, local(): lax.ppermute(packs[r][k - 1], 'edge', [(i, i ^ k) for i in range(edges)])  27 us
    pallas_call x6, Pallas kernels, local(): call(functools.partial(rows_kernel, (clusters, rc, cap, steps), last, len...  12.8 us
    ppermute x4, waiting for transfers between devices, local(): lax.ppermute(sent[d - 1], 'trip', turn(d))  12.5 us
    ppermute x6, waiting for transfers between devices, local(): lax.ppermute(low, 'trip', turn(d))  7.93 us
    ppermute x6, starting transfers between devices, local(): lax.ppermute(low, 'trip', turn(d))  7.37 us
    pallas_call x1, Pallas kernels, local(): call(functools.partial(cells_kernel, (trips, subs, share, chunks, cluster...  6.15 us
    pallas_call x3, Pallas kernels, local(): call(functools.partial(far_kernel, n, len(far), cap, whole), [jax.ShapeDt...  5.21 us
  transfers between devices with their start and end apart: 44, of which 16 were waited for; matrix products, arithmetic and copies ran while one was open for 2% of the time, Pallas kernels for 24%

profile of v8, /device:TPU:0, one launch (start us, length us, event | category | flops | bytes accessed | tf_op | source)
XLA Modules:
  0.0 142.9 jit_solution(13068870624578110757)
XLA Ops:
  0.5 3.0 %shard_map.91 = (f32[16,16,256]{2,1,0:T(8,128)}, f32[16,16,256]{2,1,0:T(8,128)}) custom-call(f32[16,32,512]{2,1,0:T(8,128)} %refs_1_.3, f32[3,512,256]{2,1,0:T(8,128)} %down.1), custom_call_target="tpu_custom_call" | custom-call | flops 402653184 | tf_op jit(solution)/shard_map/pallas_call | solution.py:308
  3.7 3.0 %collective-permute-start.4 = (f32[16,16,256]{2,1,0:T(8,128)}, f32[16,16,256]{2,1,0:T(8,128)S(1)}, u32[]{:S(2)}, u32[]{:S(2)}) collective-permute-start(f32[16,16,256]{2,1,0:T(8,128)} %get-tuple-element.95.refs_0_), channel_id=1, source_target_pairs={{0,2},{2,0},{1,3},{3,1},{4,6},{6,4},{5,7},{7,5},{8,10},{10,8},{9,1... | collective-permute-start | bytes 786440 | tf_op jit(solution)/shard_map/ppermute | solution.py:378
  9.1 2.2 %copy-done = f32[1,1,64,128,128]{4,3,2,1,0:T(8,128)S(1)} copy-done((f32[1,1,64,128,128]{4,3,2,1,0:T(8,128)S(1)}, f32[1,1,64,128,128]{4,3,2,1,0:T(8,128)}, u32[]{:S(2)}) %copy-start) | copy-done | bytes 4194328
  11.3 6.1 %shard_map.92 = (bf16[512,2048]{1,0:T(8,128)(2,1)S(1)}, bf16[512,2048]{1,0:T(8,128)(2,1)S(1)}, bf16[512,2048]{1,0:T(8,128)(2,1)S(1)}, bf16[512,2048]{1,0:T(8,128...) custom-call(s32[2]{0:T(128)S(1)} %pad_add_fusion.3.ids, s32[16]{0:T(128)S(1)} %copy-done.5, ...), custom_call_target="tpu_custom_call" | custom-call | bytes 12582912 | tf_op jit(solution)/shard_map/pallas_call | solution.py:352
  26.8 5.5 %collective-permute-done.8.refs_0_ = f32[16,16,256]{2,1,0:T(8,128)S(1)} collective-permute-done((f32[16,16,256]{2,1,0:T(8,128)S(1)}, f32[16,16,256]{2,1,0:T(8,128)S(1)}, u32[]{:S(2)}, u32[]{:S(2)}) %collective-permute-start.8) | collective-permute-done | bytes 262176 | tf_op jit(solution)/shard_map/ppermute | solution.py:417
  34.3 3.6 %collective-permute-done.9.refs_0_ = f32[16,16,256]{2,1,0:T(8,128)S(1)} collective-permute-done((f32[16,16,256]{2,1,0:T(8,128)S(1)}, f32[16,16,256]{2,1,0:T(8,128)S(1)}, u32[]{:S(2)}, u32[]{:S(2)}) %collective-permute-start.9) | collective-permute-done | bytes 262176 | tf_op jit(solution)/shard_map/ppermute | solution.py:417
  38.5 3.9 %collective-permute-start.10 = (f32[8,16,256]{2,1,0:T(8,128)S(1)}, f32[8,16,256]{2,1,0:T(8,128)S(1)}, u32[]{:S(2)}, u32[]{:S(2)}) collective-permute-start(f32[8,16,256]{2,1,0:T(8,128)S(1)} %get-tuple-element.116), channel_id=1, source_target_pairs={{0,12},{4,8},{8,4},{12,0},{1,13},{5,9},{9,5},{13,1},{2,14},{6,10},... | collective-permute-start | bytes 393224 | tf_op jit(solution)/shard_map/ppermute | solution.py:467
  46.6 4.2 %collective-permute-start.16 = (f32[8,16,256]{2,1,0:T(8,128)S(1)}, f32[8,16,256]{2,1,0:T(8,128)S(1)}, u32[]{:S(2)}, u32[]{:S(2)}) collective-permute-start(f32[8,16,256]{2,1,0:T(8,128)S(1)} %get-tuple-element.127), channel_id=1, source_target_pairs={{0,12},{4,8},{8,4},{12,0},{1,13},{5,9},{9,5},{13,1},{2,14},{6,10},... | collective-permute-start | bytes 393224 | tf_op jit(solution)/shard_map/ppermute | solution.py:467
  50.8 2.3 %collective-permute-start.17 = (f32[8,16,256]{2,1,0:T(8,128)S(1)}, f32[8,16,256]{2,1,0:T(8,128)S(1)}, u32[]{:S(2)}, u32[]{:S(2)}) collective-permute-start(f32[8,16,256]{2,1,0:T(8,128)S(1)} %get-tuple-element.112.refs_0_), channel_id=1, source_target_pairs={{0,4},{4,0},{8,12},{12,8},{1,5},{5,1},{9,13},{13,9},{2,6},{6,2},{1... | collective-permute-start | bytes 393224 | tf_op jit(solution)/shard_map/ppermute | solution.py:467
  53.1 4.1 %collective-permute-done.12.refs_5_ = f32[8,16,256]{2,1,0:T(8,128)S(1)} collective-permute-done((f32[8,16,256]{2,1,0:T(8,128)S(1)}, f32[8,16,256]{2,1,0:T(8,128)S(1)}, u32[]{:S(2)}, u32[]{:S(2)}) %collective-permute-start.12) | collective-permute-done | bytes 131104 | tf_op jit(solution)/shard_map/ppermute | solution.py:467
  57.2 2.1 %shard_map.99 = (f32[16,16,512]{2,1,0:T(8,128)S(1)}, f32[16,16,256]{2,1,0:T(8,128)S(1)}) custom-call(s32[16]{0:T(128)S(1)} %get-tuple-element.188.recv_pos, f32[8,16,256]{2,1,0:T(8,128)S(1)} %get-tuple-element.112.refs_0_, f32[16,32,512]{2,1,0:T(8,128)S(1)} %copy-done.2, f32[16,16,256]{2,1,0:T(8,128)S(1)} %get-tuple-element.115.refs_2_, ...), custom_call_target="tpu_custom_call" | custom-call | flops 805306368 | tf_op jit(solution)/shard_map/pallas_call | solution.py:480
  60.9 3.5 %collective-permute-done.18.refs_5_ = f32[8,16,256]{2,1,0:T(8,128)S(1)} collective-permute-done((f32[8,16,256]{2,1,0:T(8,128)S(1)}, f32[8,16,256]{2,1,0:T(8,128)S(1)}, u32[]{:S(2)}, u32[]{:S(2)}) %collective-permute-start.18) | collective-permute-done | bytes 131104 | tf_op jit(solution)/shard_map/ppermute | solution.py:467
  68.7 3.6 %shard_map.100.one = bf16[512,2048]{1,0:T(8,128)(2,1)S(1)} custom-call(s32[2]{0:T(128)S(1)} %pad_add_fusion.3.ids, s32[16]{0:T(128)S(1)} %copy-done.5, s32[4,128]{1,0:T(4,128)S(1)} %slice.70.pats, s32[4]{0:T(128)S(1)} %slice_reduce_fusion.live, f32[64,128,128]{2,1,0:T(8,128)S(1)} %bitcast.51, f32[64,128,128]{2,1,0:T(8,128)} %collective-permute-done.1.theirs, ...), custom_call_target="tpu_custom_call" | custom-call | bytes 6291456 | tf_op jit(solution)/shard_map/pallas_call | solution.py:446
  79.3 3.0 %collective-permute-start.26 = (f32[8,16,256]{2,1,0:T(8,128)S(1)}, f32[8,16,256]{2,1,0:T(8,128)S(1)}, u32[]{:S(2)}, u32[]{:S(2)}) collective-permute-start(f32[8,16,256]{2,1,0:T(8,128)S(1)} %get-tuple-element.142), channel_id=1, source_target_pairs={{0,12},{4,8},{8,4},{12,0},{1,13},{5,9},{9,5},{13,1},{2,14},{6,10},... | collective-permute-start | bytes 393224 | tf_op jit(solution)/shard_map/ppermute | solution.py:467
  87.1 3.1 %collective-permute-start.29 = (f32[8,16,256]{2,1,0:T(8,128)S(1)}, f32[8,16,256]{2,1,0:T(8,128)S(1)}, u32[]{:S(2)}, u32[]{:S(2)}) collective-permute-start(f32[8,16,256]{2,1,0:T(8,128)S(1)} %get-tuple-element.148), channel_id=1, source_target_pairs={{0,12},{4,8},{8,4},{12,0},{1,13},{5,9},{9,5},{13,1},{2,14},{6,10},... | collective-permute-start | bytes 393224 | tf_op jit(solution)/shard_map/ppermute | solution.py:467
  91.5 2.0 %shard_map.106 = (f32[16,16,512]{2,1,0:T(8,128)S(1)}, f32[16,16,256]{2,1,0:T(8,128)S(1)}) custom-call(s32[16]{0:T(128)S(1)} %get-tuple-element.188.recv_pos, f32[8,16,256]{2,1,0:T(8,128)S(1)} %get-tuple-element.138.refs_0_, f32[16,16,512]{2,1,0:T(8,128)S(1)} %get-tuple-element.139.refs_1_, f32[16,16,256]{2,1,0:T(8,128)S(1)} %get-tuple-element.140.refs_2_, ...), custom_call_target="tpu_custom_call" | custom-call | flops 805306368 | tf_op jit(solution)/shard_map/pallas_call | solution.py:480
  94.1 8.0 %collective-permute-done.28.refs_2_ = f32[8,16,256]{2,1,0:T(8,128)S(1)} collective-permute-done((f32[8,16,256]{2,1,0:T(8,128)S(1)}, f32[8,16,256]{2,1,0:T(8,128)S(1)}, u32[]{:S(2)}, u32[]{:S(2)}) %collective-permute-start.28) | collective-permute-done | bytes 131104 | tf_op jit(solution)/shard_map/ppermute | solution.py:467
  102.1 2.1 %shard_map.107 = (f32[16,16,512]{2,1,0:T(8,128)S(1)}, f32[16,16,256]{2,1,0:T(8,128)S(1)}) custom-call(s32[16]{0:T(128)S(1)} %get-tuple-element.188.recv_pos, f32[16,16,512]{2,1,0:T(8,128)S(1)} %get-tuple-element.145.refs_0_, f32[16,16,256]{2,1,0:T(8,128)S(1)} %get-tuple-element.146.refs_1_, f32[8,16,256]{2,1,0:T(8,128)S(1)} %collective-permute-done.28.refs_2_, ...), custom_call_target="tpu_custom_call" | custom-call | flops 805306368 | tf_op jit(solution)/shard_map/pallas_call | solution.py:480
  105.2 5.9 %collective-permute-done.34.refs_1_ = f32[16,16,256]{2,1,0:T(8,128)S(1)} collective-permute-done((f32[16,16,256]{2,1,0:T(8,128)S(1)}, f32[16,16,256]{2,1,0:T(8,128)S(1)}, u32[]{:S(2)}, u32[]{:S(2)}) %collective-permute-start.34) | collective-permute-done | bytes 262176 | tf_op jit(solution)/shard_map/ppermute | solution.py:378
  115.1 4.3 %collective-permute-start.38 = (f32[8,16,256]{2,1,0:T(8,128)S(1)}, f32[8,16,256]{2,1,0:T(8,128)S(1)}, u32[]{:S(2)}, u32[]{:S(2)}) collective-permute-start(f32[8,16,256]{2,1,0:T(8,128)S(1)} %get-tuple-element.160), channel_id=1, source_target_pairs={{0,8},{4,12},{8,0},{12,4},{1,9},{5,13},{9,1},{13,5},{2,10},{6,14},... | collective-permute-start | bytes 393224 | tf_op jit(solution)/shard_map/ppermute | solution.py:467
  124.0 4.2 %collective-permute-start.41 = (f32[8,16,256]{2,1,0:T(8,128)S(1)}, f32[8,16,256]{2,1,0:T(8,128)S(1)}, u32[]{:S(2)}, u32[]{:S(2)}) collective-permute-start(f32[8,16,256]{2,1,0:T(8,128)S(1)} %get-tuple-element.165), channel_id=1, source_target_pairs={{0,8},{4,12},{8,0},{12,4},{1,9},{5,13},{9,1},{13,5},{2,10},{6,14},... | collective-permute-start | bytes 393224 | tf_op jit(solution)/shard_map/ppermute | solution.py:467
  130.2 2.3 %shard_map.112.refs_0_ = f32[16,32,512]{2,1,0:T(8,128)} custom-call(s32[16]{0:T(128)S(1)} %get-tuple-element.188.recv_pos, f32[8,16,256]{2,1,0:T(8,128)S(1)} %get-tuple-element.157.refs_0_, f32[16,16,512]{2,1,0:T(8,128)S(1)} %get-tuple-element.158.refs_1_, f32[16,16,256]{2,1,0:T(8,128)S(1)} %get-tuple-element.159.refs_2_, ...), custom_call_target="tpu_custom_call" | custom-call | flops 805306368 | tf_op jit(solution)/shard_map/pallas_call | solution.py:480
  132.6 8.0 %collective-permute-done.41.refs_3_ = f32[8,16,256]{2,1,0:T(8,128)S(1)} collective-permute-done((f32[8,16,256]{2,1,0:T(8,128)S(1)}, f32[8,16,256]{2,1,0:T(8,128)S(1)}, u32[]{:S(2)}, u32[]{:S(2)}) %collective-permute-start.41) | collective-permute-done | bytes 131104 | tf_op jit(solution)/shard_map/ppermute | solution.py:467
  140.6 2.3 %shard_map.113 = f32[16,32,512]{2,1,0:T(8,128)} custom-call(s32[16]{0:T(128)S(1)} %get-tuple-element.188.recv_pos, f32[16,32,512]{2,1,0:T(8,128)} %shard_map.112.refs_0_, f32[16,16,512]{2,1,0:T(8,128)S(1)} %get-tuple-element.163.refs_1_, f32[16,16,256]{2,1,0:T(8,128)S(1)} %get-tuple-element.164.refs_2_, ...), custom_call_target="tpu_custom_call", output_to_operand_aliasing={{}: (1, {})} | custom-call | flops 805306368 | tf_op jit(solution)/shard_map/pallas_call | solution.py:480
  (133 shorter events, 49.3 us)
Async XLA Ops:
  3.6 16.0 %collective-permute-start.2 = (f32[16,16,256]{2,1,0:T(8,128)}, f32[16,16,256]{2,1,0:T(8,128)S(1)}, u32[]{:S(2)}, u32[]{:S(2)}) collective-permute-start(f32[16,16,256]{2,1,0:T(8,128)} %get-tuple-element.95.refs_0_), channel_id=1, source_target_pairs={{0,1},{1,0},{2,3},{3,2},{4,5},{5,4},{6,7},{7,6},{8,9},{9,8},{10,11... | collective-permute-start | bytes 786440 | tf_op jit(solution)/shard_map/ppermute | solution.py:379
  3.7 13.8 %collective-permute-start.4 = (f32[16,16,256]{2,1,0:T(8,128)}, f32[16,16,256]{2,1,0:T(8,128)S(1)}, u32[]{:S(2)}, u32[]{:S(2)}) collective-permute-start(f32[16,16,256]{2,1,0:T(8,128)} %get-tuple-element.95.refs_0_), channel_id=1, source_target_pairs={{0,2},{2,0},{1,3},{3,1},{4,6},{6,4},{5,7},{7,5},{8,10},{10,8},{9,1... | collective-permute-start | bytes 786440 | tf_op jit(solution)/shard_map/ppermute | solution.py:378
  7.6 11.4 %collective-permute-start.5 = (f32[16,16,256]{2,1,0:T(8,128)}, f32[16,16,256]{2,1,0:T(8,128)S(1)}, u32[]{:S(2)}, u32[]{:S(2)}) collective-permute-start(f32[16,16,256]{2,1,0:T(8,128)} %get-tuple-element.96.refs_1_), channel_id=1, source_target_pairs={{0,2},{2,0},{1,3},{3,1},{4,6},{6,4},{5,7},{7,5},{8,10},{10,8},{9,1... | collective-permute-start | bytes 786440 | tf_op jit(solution)/shard_map/ppermute | solution.py:378
  8.8 10.9 %collective-permute-start.3 = (f32[16,16,256]{2,1,0:T(8,128)}, f32[16,16,256]{2,1,0:T(8,128)S(1)}, u32[]{:S(2)}, u32[]{:S(2)}) collective-permute-start(f32[16,16,256]{2,1,0:T(8,128)} %get-tuple-element.96.refs_1_), channel_id=1, source_target_pairs={{0,1},{1,0},{2,3},{3,2},{4,5},{5,4},{6,7},{7,6},{8,9},{9,8},{10,11... | collective-permute-start | bytes 786440 | tf_op jit(solution)/shard_map/ppermute | solution.py:379
  23.1 9.2 %collective-permute-start.8 = (f32[16,16,256]{2,1,0:T(8,128)S(1)}, f32[16,16,256]{2,1,0:T(8,128)S(1)}, u32[]{:S(2)}, u32[]{:S(2)}) collective-permute-start(f32[16,16,256]{2,1,0:T(8,128)S(1)} %bitcast.59), channel_id=1, source_target_pairs={{0,2},{2,0},{1,3},{3,1},{4,6},{6,4},{5,7},{7,5},{8,10},{10,8},{9,1... | collective-permute-start | bytes 786440 | tf_op jit(solution)/shard_map/ppermute | solution.py:417
  25.4 12.5 %collective-permute-start.9 = (f32[16,16,256]{2,1,0:T(8,128)S(1)}, f32[16,16,256]{2,1,0:T(8,128)S(1)}, u32[]{:S(2)}, u32[]{:S(2)}) collective-permute-start(f32[16,16,256]{2,1,0:T(8,128)S(1)} %bitcast.56), channel_id=1, source_target_pairs={{0,2},{2,0},{1,3},{3,1},{4,6},{6,4},{5,7},{7,5},{8,10},{10,8},{9,1... | collective-permute-start | bytes 786440 | tf_op jit(solution)/shard_map/ppermute | solution.py:417
  32.9 26.3 %collective-permute-start.15 = (f32[65,16,128]{2,1,0:T(8,128)S(1)}, f32[65,16,128]{2,1,0:T(8,128)S(1)}, u32[]{:S(2)}, u32[]{:S(2)}) collective-permute-start(f32[65,16,128]{2,1,0:T(8,128)S(1)} %get-tuple-element.124), channel_id=1, source_target_pairs={{0,3},{1,2},{2,1},{3,0},{4,7},{5,6},{6,5},{7,4},{8,11},{9,10},{10,... | collective-permute-start | bytes 1597448 | tf_op jit(solution)/shard_map/ppermute | solution.py:443
  42.5 14.7 %collective-permute-start.12 = (f32[8,16,256]{2,1,0:T(8,128)S(1)}, f32[8,16,256]{2,1,0:T(8,128)S(1)}, u32[]{:S(2)}, u32[]{:S(2)}) collective-permute-start(f32[8,16,256]{2,1,0:T(8,128)S(1)} %get-tuple-element.118), channel_id=1, source_target_pairs={{0,8},{4,12},{8,0},{12,4},{1,9},{5,13},{9,1},{13,5},{2,10},{6,14},... | collective-permute-start | bytes 393224 | tf_op jit(solution)/shard_map/ppermute | solution.py:467
  43.1 17.8 %collective-permute-start.14 = (f32[65,16,128]{2,1,0:T(8,128)S(1)}, f32[65,16,128]{2,1,0:T(8,128)S(1)}, u32[]{:S(2)}, u32[]{:S(2)}) collective-permute-start(f32[65,16,128]{2,1,0:T(8,128)S(1)} %get-tuple-element.123), channel_id=1, source_target_pairs={{0,2},{1,3},{2,0},{3,1},{4,6},{5,7},{6,4},{7,5},{8,10},{9,11},{10,... | collective-permute-start | bytes 1597448 | tf_op jit(solution)/shard_map/ppermute | solution.py:443
  46.6 14.3 %collective-permute-start.16 = (f32[8,16,256]{2,1,0:T(8,128)S(1)}, f32[8,16,256]{2,1,0:T(8,128)S(1)}, u32[]{:S(2)}, u32[]{:S(2)}) collective-permute-start(f32[8,16,256]{2,1,0:T(8,128)S(1)} %get-tuple-element.127), channel_id=1, source_target_pairs={{0,12},{4,8},{8,4},{12,0},{1,13},{5,9},{9,5},{13,1},{2,14},{6,10},... | collective-permute-start | bytes 393224 | tf_op jit(solution)/shard_map/ppermute | solution.py:467
  50.8 10.1 %collective-permute-start.17 = (f32[8,16,256]{2,1,0:T(8,128)S(1)}, f32[8,16,256]{2,1,0:T(8,128)S(1)}, u32[]{:S(2)}, u32[]{:S(2)}) collective-permute-start(f32[8,16,256]{2,1,0:T(8,128)S(1)} %get-tuple-element.112.refs_0_), channel_id=1, source_target_pairs={{0,4},{4,0},{8,12},{12,8},{1,5},{5,1},{9,13},{13,9},{2,6},{6,2},{1... | collective-permute-start | bytes 393224 | tf_op jit(solution)/shard_map/ppermute | solution.py:467
  59.2 13.1 %collective-permute-start.13 = (f32[16,16,256]{2,1,0:T(8,128)S(1)}, f32[16,16,256]{2,1,0:T(8,128)S(1)}, u32[]{:S(2)}, u32[]{:S(2)}) collective-permute-start(f32[16,16,256]{2,1,0:T(8,128)S(1)} %get-tuple-element.122.refs_1_), channel_id=1, source_target_pairs={{0,2},{2,0},{1,3},{3,1},{4,6},{6,4},{5,7},{7,5},{8,10},{10,8},{9,1... | collective-permute-start | bytes 786440 | tf_op jit(solution)/shard_map/ppermute | solution.py:378
  78.0 12.9 %collective-permute-start.25 = (f32[8,16,256]{2,1,0:T(8,128)S(1)}, f32[8,16,256]{2,1,0:T(8,128)S(1)}, u32[]{:S(2)}, u32[]{:S(2)}) collective-permute-start(f32[8,16,256]{2,1,0:T(8,128)S(1)} %get-tuple-element.141), channel_id=1, source_target_pairs={{0,8},{4,12},{8,0},{12,4},{1,9},{5,13},{9,1},{13,5},{2,10},{6,14},... | collective-permute-start | bytes 393224 | tf_op jit(solution)/shard_map/ppermute | solution.py:467
  79.3 11.6 %collective-permute-start.26 = (f32[8,16,256]{2,1,0:T(8,128)S(1)}, f32[8,16,256]{2,1,0:T(8,128)S(1)}, u32[]{:S(2)}, u32[]{:S(2)}) collective-permute-start(f32[8,16,256]{2,1,0:T(8,128)S(1)} %get-tuple-element.142), channel_id=1, source_target_pairs={{0,12},{4,8},{8,4},{12,0},{1,13},{5,9},{9,5},{13,1},{2,14},{6,10},... | collective-permute-start | bytes 393224 | tf_op jit(solution)/shard_map/ppermute | solution.py:467
  85.7 16.4 %collective-permute-start.28 = (f32[8,16,256]{2,1,0:T(8,128)S(1)}, f32[8,16,256]{2,1,0:T(8,128)S(1)}, u32[]{:S(2)}, u32[]{:S(2)}) collective-permute-start(f32[8,16,256]{2,1,0:T(8,128)S(1)} %get-tuple-element.147), channel_id=1, source_target_pairs={{0,8},{4,12},{8,0},{12,4},{1,9},{5,13},{9,1},{13,5},{2,10},{6,14},... | collective-permute-start | bytes 393224 | tf_op jit(solution)/shard_map/ppermute | solution.py:467
  87.1 15.0 %collective-permute-start.29 = (f32[8,16,256]{2,1,0:T(8,128)S(1)}, f32[8,16,256]{2,1,0:T(8,128)S(1)}, u32[]{:S(2)}, u32[]{:S(2)}) collective-permute-start(f32[8,16,256]{2,1,0:T(8,128)S(1)} %get-tuple-element.148), channel_id=1, source_target_pairs={{0,12},{4,8},{8,4},{12,0},{1,13},{5,9},{9,5},{13,1},{2,14},{6,10},... | collective-permute-start | bytes 393224 | tf_op jit(solution)/shard_map/ppermute | solution.py:467
  90.9 11.2 %collective-permute-start.30 = (f32[8,16,256]{2,1,0:T(8,128)S(1)}, f32[8,16,256]{2,1,0:T(8,128)S(1)}, u32[]{:S(2)}, u32[]{:S(2)}) collective-permute-start(f32[8,16,256]{2,1,0:T(8,128)S(1)} %get-tuple-element.138.refs_0_), channel_id=1, source_target_pairs={{0,4},{4,0},{8,12},{12,8},{1,5},{5,1},{9,13},{13,9},{2,6},{6,2},{1... | collective-permute-start | bytes 393224 | tf_op jit(solution)/shard_map/ppermute | solution.py:467
  93.5 11.7 %collective-permute-start.33 = (f32[16,16,256]{2,1,0:T(8,128)S(1)}, f32[16,16,256]{2,1,0:T(8,128)S(1)}, u32[]{:S(2)}, u32[]{:S(2)}) collective-permute-start(f32[16,16,256]{2,1,0:T(8,128)S(1)} %get-tuple-element.144.refs_0_), channel_id=1, source_target_pairs={{0,2},{2,0},{1,3},{3,1},{4,6},{6,4},{5,7},{7,5},{8,10},{10,8},{9,1... | collective-permute-start | bytes 786440 | tf_op jit(solution)/shard_map/ppermute | solution.py:378
  115.1 13.1 %collective-permute-start.38 = (f32[8,16,256]{2,1,0:T(8,128)S(1)}, f32[8,16,256]{2,1,0:T(8,128)S(1)}, u32[]{:S(2)}, u32[]{:S(2)}) collective-permute-start(f32[8,16,256]{2,1,0:T(8,128)S(1)} %get-tuple-element.160), channel_id=1, source_target_pairs={{0,8},{4,12},{8,0},{12,4},{1,9},{5,13},{9,1},{13,5},{2,10},{6,14},... | collective-permute-start | bytes 393224 | tf_op jit(solution)/shard_map/ppermute | solution.py:467
  119.4 10.4 %collective-permute-start.39 = (f32[8,16,256]{2,1,0:T(8,128)S(1)}, f32[8,16,256]{2,1,0:T(8,128)S(1)}, u32[]{:S(2)}, u32[]{:S(2)}) collective-permute-start(f32[8,16,256]{2,1,0:T(8,128)S(1)} %get-tuple-element.161), channel_id=1, source_target_pairs={{0,4},{4,0},{8,12},{12,8},{1,5},{5,1},{9,13},{13,9},{2,6},{6,2},{1... | collective-permute-start | bytes 393224 | tf_op jit(solution)/shard_map/ppermute | solution.py:467
  119.4 10.8 %collective-permute-start.40 = (f32[8,16,256]{2,1,0:T(8,128)S(1)}, f32[8,16,256]{2,1,0:T(8,128)S(1)}, u32[]{:S(2)}, u32[]{:S(2)}) collective-permute-start(f32[8,16,256]{2,1,0:T(8,128)S(1)} %get-tuple-element.162), channel_id=1, source_target_pairs={{0,12},{4,8},{8,4},{12,0},{1,13},{5,9},{9,5},{13,1},{2,14},{6,10},... | collective-permute-start | bytes 393224 | tf_op jit(solution)/shard_map/ppermute | solution.py:467
  124.0 16.6 %collective-permute-start.41 = (f32[8,16,256]{2,1,0:T(8,128)S(1)}, f32[8,16,256]{2,1,0:T(8,128)S(1)}, u32[]{:S(2)}, u32[]{:S(2)}) collective-permute-start(f32[8,16,256]{2,1,0:T(8,128)S(1)} %get-tuple-element.165), channel_id=1, source_target_pairs={{0,8},{4,12},{8,0},{12,4},{1,9},{5,13},{9,1},{13,5},{2,10},{6,14},... | collective-permute-start | bytes 393224 | tf_op jit(solution)/shard_map/ppermute | solution.py:467
  128.2 12.3 %collective-permute-start.42 = (f32[8,16,256]{2,1,0:T(8,128)S(1)}, f32[8,16,256]{2,1,0:T(8,128)S(1)}, u32[]{:S(2)}, u32[]{:S(2)}) collective-permute-start(f32[8,16,256]{2,1,0:T(8,128)S(1)} %get-tuple-element.157.refs_0_), channel_id=1, source_target_pairs={{0,4},{4,0},{8,12},{12,8},{1,5},{5,1},{9,13},{13,9},{2,6},{6,2},{1... | collective-permute-start | bytes 393224 | tf_op jit(solution)/shard_map/ppermute | solution.py:467
  128.3 12.3 %collective-permute-start.43 = (f32[8,16,256]{2,1,0:T(8,128)S(1)}, f32[8,16,256]{2,1,0:T(8,128)S(1)}, u32[]{:S(2)}, u32[]{:S(2)}) collective-permute-start(f32[8,16,256]{2,1,0:T(8,128)S(1)} %get-tuple-element.166), channel_id=1, source_target_pairs={{0,12},{4,8},{8,4},{12,0},{1,13},{5,9},{9,5},{13,1},{2,14},{6,10},... | collective-permute-start | bytes 393224 | tf_op jit(solution)/shard_map/ppermute | solution.py:467
  (31 other events, 214.1 us)
